TPU v7x, 1024 devices: a whole 4x4x32 slice. The times are simulated.
1024 devices in a mesh: expert: 32 (over z_lo, x), fsdp: 32 (over z_hi, y, core).
Axes of the slice: x: 4, y: 4, z: 32 (z_hi: 4, z_lo: 8; z = z_hi * 8 + z_lo), core: 2. Of those that a mesh axis runs over, the one named last changes fastest.
Arguments:
- tokens: bfloat16 [4096, 4096], P('fsdp', 'expert'), may hold values from -6 to 6
- out_grad: bfloat16 [4096, 4096], P('fsdp', 'expert'), may hold values from -6 to 6
- route_probs: float32 [4096, 8], P('fsdp'), may hold values from 0.1 to 1
- expert_ids: int32 [4096, 8], P('fsdp'), may hold values from 0 to 127, as said below
- gate_weight: bfloat16 [4096, 6144], P('fsdp', 'expert'), may hold values from -0.09375 to 0.09375
- up_weight: bfloat16 [4096, 6144], P('fsdp', 'expert'), may hold values from -0.09375 to 0.09375
- down_weight: bfloat16 [6144, 4096], P('expert', 'fsdp'), may hold values from -0.15625 to 0.15625
Outputs:
- x_grad: bfloat16 [4096, 4096], P('fsdp', 'expert')
- gate_grad: bfloat16 [4096, 6144], P('fsdp', 'expert')
- up_grad: bfloat16 [4096, 6144], P('fsdp', 'expert')
- down_grad: bfloat16 [6144, 4096], P('expert', 'fsdp')
Inputs may be any that keep to these rules, and one draw needn't show every extreme that they name: `expert_ids`: each row names 8 different experts. In each aligned block of 128 rows every expert below 4 is named by 1 to 64 rows, and in every block one of them by exactly 64 rows.
All inputs are finite; a program needn't handle non-finite values.
Results may differ from a plain program's by a relative error of at most 0.023.
Values may be sent and summed in bfloat16 or wider, within the bound.
No kernel may reach another device: no remote copies, remote signals or barrier semaphores. Data moves between devices by JAX's collectives and lax.ppermute only.
A program may use at most 32 MiB of HBM per device.

v0:
```python
import jax
import jax.numpy as jnp
from jax import lax
from jax.sharding import PartitionSpec as P

CAP = 64


def contract(left, right, left_dim, right_dim):
    return lax.dot_general(
        left, right, (((left_dim,), (right_dim,)), ((), ())), preferred_element_type=jnp.float32
    )


def select_pick(prob_group, ids_group, expert):
    hit = ids_group == expert
    weight = jnp.sum(jnp.where(hit, prob_group, jnp.zeros_like(prob_group)), axis=1)
    chosen = jnp.any(hit, axis=1)
    place = jnp.cumsum(chosen.astype(jnp.int32)) - 1
    slots = jnp.arange(CAP, dtype=jnp.int32)
    picker = chosen[None, :] & (place[None, :] == slots[:, None])
    row_weight = jnp.dot(picker.astype(jnp.float32), weight, precision=lax.Precision.HIGHEST)
    return (picker.astype(jnp.bfloat16), row_weight)


def shards(tokens, out_grad, route_probs, expert_ids, gate_weight, up_weight, down_weight):
    slices = min(8, lax.axis_size("expert"))
    expert = lax.axis_index("expert") // slices
    tok_group, grad_group = (
        lax.all_gather(tokens, "expert", axis=1, tiled=True),
        lax.all_gather(out_grad, "expert", axis=1, tiled=True),
    )
    gate_w, up_w, down_w = (
        lax.all_gather(gate_weight, "fsdp", axis=0, tiled=True),
        lax.all_gather(up_weight, "fsdp", axis=0, tiled=True),
        lax.all_gather(down_weight, "fsdp", axis=1, tiled=True),
    )
    pick_half, row_weight = select_pick(route_probs, expert_ids, expert)
    rows = jnp.dot(pick_half, tok_group, preferred_element_type=jnp.float32).astype(jnp.bfloat16)
    gate_value = jnp.dot(rows, gate_w, preferred_element_type=jnp.float32)
    up_value = jnp.dot(rows, up_w, preferred_element_type=jnp.float32)
    sigma = jax.nn.sigmoid(gate_value)
    active = gate_value * sigma
    hidden = (active * up_value).astype(jnp.bfloat16)
    cot_rows = jnp.dot(pick_half, grad_group, preferred_element_type=jnp.float32).astype(
        jnp.bfloat16
    )
    carried = (row_weight[:, None] * cot_rows.astype(jnp.float32)).astype(jnp.bfloat16)
    width = hidden.shape[1]
    hidden_grad = contract(carried, down_w, 1, 1)
    down_term = contract(carried, hidden, 0, 0)
    up_rows_grad = (hidden_grad * active).astype(jnp.bfloat16)
    gate_rows_grad = (hidden_grad * up_value * sigma * (1.0 + gate_value * (1.0 - sigma))).astype(
        jnp.bfloat16
    )
    row_grad = (contract(gate_rows_grad, gate_w, 1, 1) + contract(up_rows_grad, up_w, 1, 1)).astype(
        jnp.bfloat16
    )
    token_term = contract(pick_half, row_grad, 0, 0)
    x_grad = lax.psum_scatter(
        token_term.astype(jnp.bfloat16), "expert", scatter_dimension=1, tiled=True
    )
    gate_term = contract(rows, gate_rows_grad, 0, 0)
    up_term = contract(rows, up_rows_grad, 0, 0)
    stacked = jnp.concatenate([gate_term, up_term, down_term], axis=1)
    summed = lax.psum_scatter(
        stacked.astype(jnp.bfloat16), "fsdp", scatter_dimension=0, tiled=True
    ).astype(jnp.float32)
    gate_grad = summed[:, :width].astype(jnp.bfloat16)
    up_grad = summed[:, width : 2 * width].astype(jnp.bfloat16)
    down_grad = summed[:, 2 * width :].T.astype(jnp.bfloat16)
    return (x_grad, gate_grad, up_grad, down_grad)


def solution(mesh):
    placed = (
        P("fsdp", "expert"),
        P("fsdp", "expert"),
        P("fsdp", None),
        P("fsdp", None),
        P("fsdp", "expert"),
        P("fsdp", "expert"),
        P("expert", "fsdp"),
    )
    return jax.shard_map(
        shards,
        mesh=mesh,
        in_specs=placed,
        out_specs=(
            P("fsdp", "expert"),
            P("fsdp", "expert"),
            P("fsdp", "expert"),
            P("expert", "fsdp"),
        ),
        check_vma=False,
    )
```

profile of v0, /device:TPU:24, one launch (start us, length us, event | category | flops | bytes accessed | tf_op | source)
XLA Modules:
  0.0 1249.9 jit_solution(3958241710268968673)
XLA Ops:
  7.9 0.7 all-gather.6.cloned.1.call-update
  10.6 0.7 select_reduce_fusion
  11.9 193.9 %all-gather.10.cloned.1.call-done = bf16[128,4096]{1,0:T(8,128)(2,1)} async-done(((bf16[128,128]{1,0:T(8,128)(2,1)}), bf16[128,4096]{1,0:T(8,128)(2,1)}) %all-gather.10.cloned.1.call-update) | async-done | bytes 1048592 | tf_op jit(solution)/shard_map/all_gather | solution.py:30
  205.8 1.5 convolution_convert_fusion.4
  207.3 181.3 %all-gather.6.cloned.1.call-done = bf16[128,4096]{1,0:T(8,128)(2,1)} async-done(((bf16[128,128]{1,0:T(8,128)(2,1)}), bf16[128,4096]{1,0:T(8,128)(2,1)}) %all-gather.6.cloned.1.call-update) | async-done | bytes 1048592 | tf_op jit(solution)/shard_map/all_gather | solution.py:31
  388.7 1.5 fusion.3
  390.2 122.8 %all-gather.14.cloned.1.call-done = bf16[4096,192]{0,1:T(8,128)(2,1)} async-done(((bf16[128,192]{0,1:T(8,128)(2,1)}), bf16[4096,192]{0,1:T(8,128)(2,1)}) %all-gather.14.cloned.1.call-update) | async-done | bytes 1572880 | tf_op jit(solution)/shard_map/all_gather | solution.py:34
  513.0 2.0 fusion.23
  515.0 117.3 %all-gather.12.cloned.1.call-done = bf16[4096,192]{0,1:T(8,128)(2,1)} async-done(((bf16[128,192]{0,1:T(8,128)(2,1)}), bf16[4096,192]{0,1:T(8,128)(2,1)}) %all-gather.12.cloned.1.call-update) | async-done | bytes 1572880 | tf_op jit(solution)/shard_map/all_gather | solution.py:35
  632.3 2.0 fusion.22
  634.4 117.3 %all-gather.8.cloned.1.call-done = bf16[192,4096]{1,0:T(8,128)(2,1)} async-done(((bf16[192,128]{1,0:T(8,128)(2,1)}), bf16[192,4096]{1,0:T(8,128)(2,1)}) %all-gather.8.cloned.1.call-update) | async-done | bytes 1572880 | tf_op jit(solution)/shard_map/all_gather | solution.py:36
  751.7 2.2 multiply_convert_fusion.1
  753.9 1.4 fusion.24
  755.3 2.9 convolution_convert_fusion.3
  758.2 2.3 copy.14
  762.4 2.6 pad_maximum_fusion
  765.0 7.6 copy.16
  772.6 226.7 %reduce-scatter.7.cloned.1.call-done = bf16[128,128]{1,0:T(8,128)(2,1)} async-done(((bf16[4096,128]{1,0:T(8,128)(2,1)}), bf16[128,128]{1,0:T(8,128)(2,1)}) %reduce-scatter.7.cloned.1.call-update) | async-done | bytes 32784
  999.4 1.5 copy.15
  1000.8 239.0 %reduce-scatter.9.cloned.1.call-done = bf16[128,576]{1,0:T(8,128)(2,1)} async-done(((bf16[4096,576]{1,0:T(8,128)(2,1)}), bf16[128,576]{1,0:T(8,128)(2,1)}) %reduce-scatter.9.cloned.1.call-update) | async-done | bytes 147472
  1239.8 1.0 fusion.21
  1240.8 0.7 copy.20
  1241.6 0.7 copy.19
  1242.3 0.7 copy.18
  (26 shorter events, 5.2 us)
Async XLA Ops:
  7.2 198.7 %all-gather.10.cloned.1.call-start = ((), (), s32[]{:S(2)}) async-start(), calls=%async_computation.4 | async-start | bytes 1081344 | tf_op jit(solution)/shard_map/all_gather | solution.py:30
  7.9 380.8 %all-gather.6.cloned.1.call-start = ((), (), s32[]{:S(2)}) async-start(), calls=%async_computation.2 | async-start | bytes 1081344 | tf_op jit(solution)/shard_map/all_gather | solution.py:31
  8.6 504.3 %all-gather.14.cloned.1.call-start = ((), (), s32[]{:S(2)}) async-start(), calls=%async_computation.6 | async-start | bytes 1622016 | tf_op jit(solution)/shard_map/all_gather | solution.py:34
  9.4 623.0 %all-gather.12.cloned.1.call-start = ((), (), s32[]{:S(2)}) async-start(), calls=%async_computation.5 | async-start | bytes 1622016 | tf_op jit(solution)/shard_map/all_gather | solution.py:35
  10.0 741.7 %all-gather.8.cloned.1.call-start = ((), (), s32[]{:S(2)}) async-start(), calls=%async_computation.3 | async-start | bytes 1622016 | tf_op jit(solution)/shard_map/all_gather | solution.py:36
  10.5 988.8 %reduce-scatter.7.cloned.1.call-start = ((), (), s32[]{:S(2)}) async-start(), calls=%async_computation.7 | async-start | bytes 1081344
  751.7 2.2 copy-start.1
  753.8 1.5 copy-start
  760.5 479.3 %reduce-scatter.9.cloned.1.call-start = ((), (), s32[]{:S(2)}) async-start(), calls=%async_computation.8 | async-start | bytes 5406720
Sparse Core Ops, SparseCore 0:
  10.6 195.1 all-gather.9
  208.4 180.2 all-gather.5
  392.9 120.0 all-gather.13
  517.1 115.2 all-gather.11
  636.4 115.2 all-gather.7
  760.7 238.6 reduce-scatter.6
  1006.1 233.6 reduce-scatter.8
where the time goes:
time: 1250 us
  waiting for transfers between devices  1200 us (96%)
  matrix products  15.5 us (1%)
  local copies, waits for them, and re-layouts  14.8 us (1%)
  between operations  14.2 us (1%)
    unnamed x9, waiting for transfers between devices  469 us
    all_gather x1, waiting for transfers between devices, shards(): lax.all_gather(tokens, 'expert', axis=1, tiled=True)  194 us
    all_gather x1, waiting for transfers between devices, shards(): lax.all_gather(out_grad, 'expert', axis=1, tiled=True)  181 us
    all_gather x1, waiting for transfers between devices, shards(): lax.all_gather(gate_weight, 'fsdp', axis=0, tiled=True)  123 us
    all_gather x1, waiting for transfers between devices, shards(): lax.all_gather(up_weight, 'fsdp', axis=0, tiled=True)  117 us
    all_gather x1, waiting for transfers between devices, shards(): lax.all_gather(down_weight, 'fsdp', axis=1, tiled=True)  117 us
  transfers between devices with their start and end apart: 7, of which 7 were waited for; matrix products, arithmetic and copies ran while one was open for 2% of the time, Pallas kernels for 0%

commit v1 on v0

v1 whole, which is shorter than its diff:
```python
import jax
import jax.numpy as jnp
from jax import lax
from jax.sharding import Mesh, PartitionSpec as P

CAP = 64
WINDOW = 4
SHAPE = (4, 2, 4, 4, 4, 2)
AXES = ("zp", "l", "x", "zh", "y", "c")
EXPERT = ("zp", "l", "x")
FSDP = ("zh", "y", "c")
PIECE = ("l", "x")
GROUP = ("y", "c")


def contract(left, right, left_dim, right_dim):
    return lax.dot_general(
        left, right, (((left_dim,), (right_dim,)), ((), ())), preferred_element_type=jnp.float32
    )


def gather(block, axis, size):
    copies = jnp.broadcast_to(block[None], (size,) + block.shape)
    return lax.all_to_all(copies, axis, 0, 0)


def exchange(blocks, axis):
    return lax.all_to_all(blocks, axis, 0, 0)


def swap(block):
    pairs = [(piece * 8 + group, group * 8 + piece) for piece in range(8) for group in range(8)]
    return lax.ppermute(block, PIECE + GROUP, pairs)


def select(probs, ids):
    window = jnp.arange(WINDOW, dtype=jnp.int32)
    hit = ids[None] == window[:, None, None]
    weight = jnp.sum(jnp.where(hit, probs[None], 0.0), axis=2)
    chosen = jnp.any(hit, axis=2)
    count = ids.shape[0]
    before = jnp.arange(count)[:, None] <= jnp.arange(count)[None, :]
    place = jnp.dot(
        chosen.astype(jnp.bfloat16), before.astype(jnp.bfloat16), preferred_element_type=jnp.float32
    ).astype(jnp.int32)
    slots = jnp.arange(1, CAP + 1, dtype=jnp.int32)
    picker = chosen[:, None, :] & (place[:, None, :] == slots[None, :, None])
    row_weight = jnp.sum(jnp.where(picker, weight[:, None, :], 0.0), axis=2)
    return picker.reshape(WINDOW * CAP, count).astype(jnp.bfloat16), row_weight.reshape(-1)


def shards(tokens, out_grad, route_probs, expert_ids, gate_weight, up_weight, down_weight):
    hid, feat = down_weight.shape
    own = jnp.concatenate([gate_weight.T, up_weight.T, down_weight], axis=0)
    weights = gather(own, "zh", 4).transpose(1, 0, 2).reshape(3 * hid, 4 * feat)
    gate_up, down = weights[: 2 * hid], weights[2 * hid :]

    picker, row_weight = select(route_probs, expert_ids)
    picked = jnp.dot(picker, tokens, preferred_element_type=jnp.float32).astype(jnp.bfloat16)
    cot_rows = jnp.dot(picker, out_grad, preferred_element_type=jnp.float32)
    carried = (row_weight[:, None] * cot_rows).astype(jnp.bfloat16)
    both = jnp.stack([picked, carried]).reshape(2, WINDOW, CAP, feat).transpose(1, 2, 0, 3)
    both = exchange(both.reshape(WINDOW, CAP, 2 * feat), "zp")
    both = both.reshape(4, CAP, 2, feat).transpose(1, 2, 0, 3).reshape(CAP, 8 * feat)
    both = gather(swap(both), PIECE, 8).reshape(8 * CAP, 8 * feat)
    rows, carried = both[:, : 4 * feat], both[:, 4 * feat :]

    parts = jnp.concatenate(
        [contract(rows, gate_up, 1, 1), contract(carried, down, 1, 1)], axis=1
    ).astype(jnp.bfloat16)
    values = jnp.sum(
        exchange(parts.reshape(8, CAP, 3 * hid), GROUP).astype(jnp.float32), axis=0
    )
    gate_value, up_value, hidden_grad = (
        values[:, :hid],
        values[:, hid : 2 * hid],
        values[:, 2 * hid :],
    )
    sigma = jax.nn.sigmoid(gate_value)
    active = gate_value * sigma
    hidden = (active * up_value).astype(jnp.bfloat16)
    up_rows_grad = (hidden_grad * active).astype(jnp.bfloat16)
    gate_rows_grad = (hidden_grad * up_value * sigma * (1.0 + gate_value * (1.0 - sigma))).astype(
        jnp.bfloat16
    )
    acts = jnp.concatenate([gate_rows_grad, up_rows_grad, hidden], axis=1)
    acts = gather(acts, GROUP, 8).reshape(8 * CAP, 3 * hid)
    row_grads, hidden = acts[:, : 2 * hid], acts[:, 2 * hid :]

    terms = jnp.concatenate(
        [contract(row_grads, rows, 0, 0), contract(hidden, carried, 0, 0)], axis=0
    ).astype(jnp.bfloat16)
    summed = exchange(terms.reshape(3 * hid, 4, feat).transpose(1, 0, 2), "zh")
    summed = jnp.sum(summed.astype(jnp.float32), axis=0).astype(jnp.bfloat16)
    gate_grad, up_grad = summed[:hid].T, summed[hid : 2 * hid].T
    down_grad = summed[2 * hid :]

    row_grad = contract(row_grads, gate_up, 1, 0).astype(jnp.bfloat16).reshape(8, CAP, 4 * feat)
    row_grad = exchange(row_grad, PIECE).astype(jnp.float32)
    row_grad = swap(jnp.sum(row_grad, axis=0).astype(jnp.bfloat16))
    row_grad = exchange(row_grad.reshape(CAP, 4, feat).transpose(1, 0, 2), "zp")
    x_grad = contract(picker, row_grad.reshape(WINDOW * CAP, feat), 0, 0).astype(jnp.bfloat16)
    return (x_grad, gate_grad, up_grad, down_grad)


def solution(mesh):
    fine = Mesh(mesh.devices.reshape(SHAPE), AXES)
    placed = (
        P(FSDP, EXPERT),
        P(FSDP, EXPERT),
        P(FSDP, None),
        P(FSDP, None),
        P(FSDP, EXPERT),
        P(FSDP, EXPERT),
        P(EXPERT, FSDP),
    )
    return jax.shard_map(
        shards,
        mesh=fine,
        in_specs=placed,
        out_specs=(P(FSDP, EXPERT), P(FSDP, EXPERT), P(FSDP, EXPERT), P(EXPERT, FSDP)),
        check_vma=False,
    )
```

time: 1250 us -> 274 us (0.22)
  waiting for transfers between devices: 1200 us -> 161 us
  starting transfers between devices: 0.27 us -> 68.5 us
  blocking collectives: 0 us -> 28.4 us
  between operations: 14.2 us -> 0.89 us
    all_gather x5 -> x0, waiting for transfers between devices: 733 us -> none  [the longest x1 194 us: shards(): lax.all_gather(tokens, 'expert', axis=1, tiled=True)]
    unnamed x9 -> x0, waiting for transfers between devices: 469 us -> none
    ppermute x0 -> x2, waiting for transfers between devices: none -> 95.3 us  [swap(): return lax.ppermute(block, PIECE + GROUP, pairs)]
    all_to_all x0 -> x6, waiting for transfers between devices: none -> 65.3 us  [the longest x4 42.3 us: exchange(): return lax.all_to_all(blocks, axis, 0, 0)]
    all_to_all x0 -> x6, starting transfers between devices: none -> 60 us  [the longest x4 34.7 us: exchange(): return lax.all_to_all(blocks, axis, 0, 0)]
    all_to_all x0 -> x2, blocking collectives: none -> 28.4 us  [the longest x1 14.2 us: exchange(): return lax.all_to_all(blocks, axis, 0, 0)]
    unnamed x10 -> x8, local copies, waits for them, and re-layouts: 13.6 us -> 0.02 us
  transfers between devices with their start and end apart: 7 -> 8, of which waited for: 7 -> 8; matrix products, arithmetic and copies ran while one was open for 2% -> 2% of each run, Pallas kernels for 0% -> 0%
where the time goes in v1:
time: 274 us; the launch traced here: 272 us
  waiting for transfers between devices  161 us (59%)
  starting transfers between devices  68.5 us (25%)
  blocking collectives  28.4 us (10%)
  local copies, waits for them, and re-layouts  5.74 us (2%)
  matrix products  4.78 us (2%)
  other arithmetic  3.44 us (1%)
    ppermute x2, waiting for transfers between devices, swap(): return lax.ppermute(block, PIECE + GROUP, pairs)  95.3 us
    all_to_all x4, waiting for transfers between devices, exchange(): return lax.all_to_all(blocks, axis, 0, 0)  42.3 us
    all_to_all x4, starting transfers between devices, exchange(): return lax.all_to_all(blocks, axis, 0, 0)  34.7 us
    all_to_all x2, starting transfers between devices, gather(): return lax.all_to_all(copies, axis, 0, 0)  25.3 us
    all_to_all x2, waiting for transfers between devices, gather(): return lax.all_to_all(copies, axis, 0, 0)  23 us
    all_to_all x1, blocking collectives, exchange(): return lax.all_to_all(blocks, axis, 0, 0)  14.2 us
    all_to_all x1, blocking collectives, gather(): return lax.all_to_all(copies, axis, 0, 0)  14.2 us
    ppermute x2, starting transfers between devices, swap(): return lax.ppermute(block, PIECE + GROUP, pairs)  8.45 us
  transfers between devices with their start and end apart: 8, of which 8 were waited for; matrix products, arithmetic and copies ran while one was open for 2% of the time, Pallas kernels for 0%

profile of v1, /device:TPU:24, one launch (start us, length us, event | category | flops | bytes accessed | tf_op | source)
XLA Modules:
  0.0 272.4 jit_solution(9733478290985378592)
XLA Ops:
  3.0 0.9 fusion.2
  5.1 11.2 %all-to-all-start = ((bf16[4,64,256]{2,1,0:T(8,128)(2,1)}), bf16[4,64,256]{2,1,0:T(8,128)(2,1)S(1)}, u32[]{:S(2)}, u32[]{:S(2)}) async-start(bf16[4,64,256]{2,1,0:T(8,128)(2,1)} %reshape.65), calls=%async_computation | async-start | bytes 262144 | tf_op jit(solution)/shard_map/all_to_all | solution.py:28
  16.3 12.1 %all-to-all-done = bf16[4,64,256]{2,1,0:T(8,128)(2,1)S(1)} async-done(((bf16[4,64,256]{2,1,0:T(8,128)(2,1)}), bf16[4,64,256]{2,1,0:T(8,128)(2,1)S(1)}, u32[]{:S(2)}, u32[]{:S(2)}) %all-to-all-start) | async-done | bytes 131104 | tf_op jit(solution)/shard_map/all_to_all | solution.py:28
  28.4 0.9 broadcast_in_dim.35
  29.3 21.0 %all-to-all-start.2 = ((bf16[4,576,128]{2,1,0:T(8,128)(2,1)}), bf16[4,576,128]{2,1,0:T(8,128)(2,1)S(1)}, u32[]{:S(2)}, u32[]{:S(2)}) async-start(bf16[4,576,128]{2,1,0:T(8,128)(2,1)} %broadcast_in_dim.35), calls=%async_computation.2 | async-start | bytes 1179648 | tf_op jit(solution)/shard_map/all_to_all | solution.py:24
  50.7 3.8 %collective-permute-start = (bf16[64,1024]{1,0:T(8,128)(2,1)S(1)}, bf16[64,1024]{1,0:T(8,128)(2,1)S(1)}, u32[]{:S(2)}, u32[]{:S(2)}) collective-permute-start(bf16[64,1024]{1,0:T(8,128)(2,1)S(1)} %reshape.67), channel_id=1, source_target_pairs={{0,0},{1,32},{2,64},{3,96},{4,128},{5,160},{6,192},{7,224},{32,1},... | collective-permute-start | bytes 393224 | tf_op jit(solution)/shard_map/ppermute | solution.py:33
  54.4 48.2 %collective-permute-done = bf16[64,1024]{1,0:T(8,128)(2,1)S(1)} collective-permute-done((bf16[64,1024]{1,0:T(8,128)(2,1)S(1)}, bf16[64,1024]{1,0:T(8,128)(2,1)S(1)}, u32[]{:S(2)}, u32[]{:S(2)}) %collective-permute-start) | collective-permute-done | bytes 131104 | tf_op jit(solution)/shard_map/ppermute | solution.py:33
  102.7 13.3 %all-to-all-done.2 = bf16[4,576,128]{2,1,0:T(8,128)(2,1)S(1)} async-done(((bf16[4,576,128]{2,1,0:T(8,128)(2,1)}), bf16[4,576,128]{2,1,0:T(8,128)(2,1)S(1)}, u32[]{:S(2)}, u32[]{:S(2)}) %all-to-all-start.2) | async-done | bytes 589856 | tf_op jit(solution)/shard_map/all_to_all | solution.py:24
  115.9 1.1 broadcast_in_dim.34
  117.0 4.3 %all-to-all-start.1 = ((bf16[8,64,1024]{2,1,0:T(8,128)(2,1)}), bf16[8,64,1024]{2,1,0:T(8,128)(2,1)S(1)}, u32[]{:S(2)}, u32[]{:S(2)}) async-start(bf16[8,64,1024]{2,1,0:T(8,128)(2,1)} %broadcast_in_dim.34), calls=%async_computation.1 | async-start | bytes 2097152 | tf_op jit(solution)/shard_map/all_to_all | solution.py:24
  122.2 9.7 %all-to-all-done.1 = bf16[8,64,1024]{2,1,0:T(8,128)(2,1)S(1)} async-done(((bf16[8,64,1024]{2,1,0:T(8,128)(2,1)}), bf16[8,64,1024]{2,1,0:T(8,128)(2,1)S(1)}, u32[]{:S(2)}, u32[]{:S(2)}) %all-to-all-start.1) | async-done | bytes 1048608 | tf_op jit(solution)/shard_map/all_to_all | solution.py:24
  132.9 14.2 %all_to_all.40 = bf16[8,64,576]{2,1,0:T(8,128)(2,1)S(1)} all-to-all(bf16[8,64,576]{2,1,0:T(8,128)(2,1)S(1)} %pad_maximum_fusion), channel_id=1, replica_groups=mesh['zp'=4,'l'=2,'x'=4,'zh'=4,'y'=4,'c'=2] {'y','c'}, dimensions={0} | all-to-all | bytes 1179648 | tf_op jit(solution)/shard_map/all_to_all | solution.py:28
  147.4 14.2 %all_to_all.41 = bf16[8,64,576]{2,1,0:T(8,128)(2,1)S(1)} all-to-all(bf16[8,64,576]{2,1,0:T(8,128)(2,1)S(1)} %broadcast_in_dim.36), channel_id=1, replica_groups=mesh['zp'=4,'l'=2,'x'=4,'zh'=4,'y'=4,'c'=2] {'y','c'}, dimensions={0} | all-to-all | bytes 1179648 | tf_op jit(solution)/shard_map/all_to_all | solution.py:24
  161.6 1.2 convolution_convert_fusion
  162.9 3.6 %all-to-all-start.5 = ((bf16[8,64,512]{2,1,0:T(8,128)(2,1)}), bf16[8,64,512]{2,1,0:T(8,128)(2,1)S(1)}, u32[]{:S(2)}, u32[]{:S(2)}) async-start(bf16[8,64,512]{2,1,0:T(8,128)(2,1)} %bitcast.13), calls=%async_computation.5 | async-start | bytes 1048576 | tf_op jit(solution)/shard_map/all_to_all | solution.py:28
  167.3 0.9 maximum_bitcast_fusion
  168.2 7.8 %all-to-all-done.5 = bf16[8,64,512]{2,1,0:T(8,128)(2,1)S(1)} async-done(((bf16[8,64,512]{2,1,0:T(8,128)(2,1)}), bf16[8,64,512]{2,1,0:T(8,128)(2,1)S(1)}, u32[]{:S(2)}, u32[]{:S(2)}) %all-to-all-start.5) | async-done | bytes 524320 | tf_op jit(solution)/shard_map/all_to_all | solution.py:28
  176.0 13.2 %all-to-all-start.7 = ((bf16[4,576,128]{2,1,0:T(8,128)(2,1)}), bf16[4,576,128]{2,1,0:T(8,128)(2,1)S(1)}, u32[]{:S(2)}, u32[]{:S(2)}) async-start(bf16[4,576,128]{2,1,0:T(8,128)(2,1)} %maximum_bitcast_fusion), calls=%async_computation.7 | async-start | bytes 1179648 | tf_op jit(solution)/shard_map/all_to_all | solution.py:28
  189.3 4.7 %collective-permute-start.1 = (bf16[64,512]{1,0:T(8,128)(2,1)S(1)}, bf16[64,512]{1,0:T(8,128)(2,1)S(1)}, u32[]{:S(2)}, u32[]{:S(2)}) collective-permute-start(bf16[64,512]{1,0:T(8,128)(2,1)S(1)} %reduce_sum.54), channel_id=1, source_target_pairs={{0,0},{1,32},{2,64},{3,96},{4,128},{5,160},{6,192},{7,224},{32,1},... | collective-permute-start | bytes 196616 | tf_op jit(solution)/shard_map/ppermute | solution.py:33
  194.0 47.1 %collective-permute-done.1 = bf16[64,512]{1,0:T(8,128)(2,1)S(1)} collective-permute-done((bf16[64,512]{1,0:T(8,128)(2,1)S(1)}, bf16[64,512]{1,0:T(8,128)(2,1)S(1)}, u32[]{:S(2)}, u32[]{:S(2)}) %collective-permute-start.1) | collective-permute-done | bytes 65568 | tf_op jit(solution)/shard_map/ppermute | solution.py:33
  241.7 13.4 %all-to-all-done.7 = bf16[4,576,128]{2,1,0:T(8,128)(2,1)S(1)} async-done(((bf16[4,576,128]{2,1,0:T(8,128)(2,1)}), bf16[4,576,128]{2,1,0:T(8,128)(2,1)S(1)}, u32[]{:S(2)}, u32[]{:S(2)}) %all-to-all-start.7) | async-done | bytes 589856 | tf_op jit(solution)/shard_map/all_to_all | solution.py:28
  255.2 6.7 %all-to-all-start.6 = ((bf16[4,64,128]{2,1,0:T(8,128)(2,1)}), bf16[4,64,128]{2,1,0:T(8,128)(2,1)S(1)}, u32[]{:S(2)}, u32[]{:S(2)}) async-start(bf16[4,64,128]{2,1,0:T(8,128)(2,1)} %bitcast_bitcast_fusion), calls=%async_computation.6 | async-start | bytes 131072 | tf_op jit(solution)/shard_map/all_to_all | solution.py:28
  262.6 8.9 %all-to-all-done.6 = bf16[4,64,128]{2,1,0:T(8,128)(2,1)S(1)} async-done(((bf16[4,64,128]{2,1,0:T(8,128)(2,1)}), bf16[4,64,128]{2,1,0:T(8,128)(2,1)S(1)}, u32[]{:S(2)}, u32[]{:S(2)}) %all-to-all-start.6) | async-done | bytes 65568 | tf_op jit(solution)/shard_map/all_to_all | solution.py:28
  271.5 0.9 fusion.3
  (48 shorter events, 8.0 us)
Async XLA Ops:
  0.6 2.1 copy-start
  0.6 15.6 %copy-start.1 = (bf16[192,128]{1,0:T(8,128)(2,1)S(1)}, bf16[192,128]{1,0:T(8,128)(2,1)}, u32[]{:S(2)}) copy-start(bf16[192,128]{1,0:T(8,128)(2,1)} %param.13) | copy-start | bytes 147460
  0.7 15.6 %copy-start.2 = (bf16[128,192]{0,1:T(8,128)(2,1)S(1)}, bf16[128,192]{0,1:T(8,128)(2,1)}, u32[]{:S(2)}) copy-start(bf16[128,192]{0,1:T(8,128)(2,1)} %param.12) | copy-start | bytes 147460
  0.7 15.6 %copy-start.3 = (bf16[128,192]{0,1:T(8,128)(2,1)S(1)}, bf16[128,192]{0,1:T(8,128)(2,1)}, u32[]{:S(2)}) copy-start(bf16[128,192]{0,1:T(8,128)(2,1)} %param.11) | copy-start | bytes 147460
  5.1 23.3 %all-to-all-start = ((bf16[4,64,256]{2,1,0:T(8,128)(2,1)}), bf16[4,64,256]{2,1,0:T(8,128)(2,1)S(1)}, u32[]{:S(2)}, u32[]{:S(2)}) async-start(bf16[4,64,256]{2,1,0:T(8,128)(2,1)} %reshape.65), calls=%async_computation | async-start | bytes 262144 | tf_op jit(solution)/shard_map/all_to_all | solution.py:28
  29.3 86.6 %all-to-all-start.2 = ((bf16[4,576,128]{2,1,0:T(8,128)(2,1)}), bf16[4,576,128]{2,1,0:T(8,128)(2,1)S(1)}, u32[]{:S(2)}, u32[]{:S(2)}) async-start(bf16[4,576,128]{2,1,0:T(8,128)(2,1)} %broadcast_in_dim.35), calls=%async_computation.2 | async-start | bytes 1179648 | tf_op jit(solution)/shard_map/all_to_all | solution.py:24
  50.7 52.0 %collective-permute-start = (bf16[64,1024]{1,0:T(8,128)(2,1)S(1)}, bf16[64,1024]{1,0:T(8,128)(2,1)S(1)}, u32[]{:S(2)}, u32[]{:S(2)}) collective-permute-start(bf16[64,1024]{1,0:T(8,128)(2,1)S(1)} %reshape.67), channel_id=1, source_target_pairs={{0,0},{1,32},{2,64},{3,96},{4,128},{5,160},{6,192},{7,224},{32,1},... | collective-permute-start | bytes 393224 | tf_op jit(solution)/shard_map/ppermute | solution.py:33
  117.0 14.9 %all-to-all-start.1 = ((bf16[8,64,1024]{2,1,0:T(8,128)(2,1)}), bf16[8,64,1024]{2,1,0:T(8,128)(2,1)S(1)}, u32[]{:S(2)}, u32[]{:S(2)}) async-start(bf16[8,64,1024]{2,1,0:T(8,128)(2,1)} %broadcast_in_dim.34), calls=%async_computation.1 | async-start | bytes 2097152 | tf_op jit(solution)/shard_map/all_to_all | solution.py:24
  162.9 13.2 %all-to-all-start.5 = ((bf16[8,64,512]{2,1,0:T(8,128)(2,1)}), bf16[8,64,512]{2,1,0:T(8,128)(2,1)S(1)}, u32[]{:S(2)}, u32[]{:S(2)}) async-start(bf16[8,64,512]{2,1,0:T(8,128)(2,1)} %bitcast.13), calls=%async_computation.5 | async-start | bytes 1048576 | tf_op jit(solution)/shard_map/all_to_all | solution.py:28
  176.0 79.1 %all-to-all-start.7 = ((bf16[4,576,128]{2,1,0:T(8,128)(2,1)}), bf16[4,576,128]{2,1,0:T(8,128)(2,1)S(1)}, u32[]{:S(2)}, u32[]{:S(2)}) async-start(bf16[4,576,128]{2,1,0:T(8,128)(2,1)} %maximum_bitcast_fusion), calls=%async_computation.7 | async-start | bytes 1179648 | tf_op jit(solution)/shard_map/all_to_all | solution.py:28
  189.3 51.8 %collective-permute-start.1 = (bf16[64,512]{1,0:T(8,128)(2,1)S(1)}, bf16[64,512]{1,0:T(8,128)(2,1)S(1)}, u32[]{:S(2)}, u32[]{:S(2)}) collective-permute-start(bf16[64,512]{1,0:T(8,128)(2,1)S(1)} %reduce_sum.54), channel_id=1, source_target_pairs={{0,0},{1,32},{2,64},{3,96},{4,128},{5,160},{6,192},{7,224},{32,1},... | collective-permute-start | bytes 196616 | tf_op jit(solution)/shard_map/ppermute | solution.py:33
  255.2 16.3 %all-to-all-start.6 = ((bf16[4,64,128]{2,1,0:T(8,128)(2,1)}), bf16[4,64,128]{2,1,0:T(8,128)(2,1)S(1)}, u32[]{:S(2)}, u32[]{:S(2)}) async-start(bf16[4,64,128]{2,1,0:T(8,128)(2,1)} %bitcast_bitcast_fusion), calls=%async_computation.6 | async-start | bytes 131072 | tf_op jit(solution)/shard_map/all_to_all | solution.py:28

commit v2 on v1

--- a/solution.py
+++ b/solution.py
@@ -51,16 +51,18 @@
 
 def shards(tokens, out_grad, route_probs, expert_ids, gate_weight, up_weight, down_weight):
     hid, feat = down_weight.shape
-    own = jnp.concatenate([gate_weight.T, up_weight.T, down_weight], axis=0)
-    weights = gather(own, "zh", 4).transpose(1, 0, 2).reshape(3 * hid, 4 * feat)
-    gate_up, down = weights[: 2 * hid], weights[2 * hid :]
-
     picker, row_weight = select(route_probs, expert_ids)
     picked = jnp.dot(picker, tokens, preferred_element_type=jnp.float32).astype(jnp.bfloat16)
     cot_rows = jnp.dot(picker, out_grad, preferred_element_type=jnp.float32)
     carried = (row_weight[:, None] * cot_rows).astype(jnp.bfloat16)
     both = jnp.stack([picked, carried]).reshape(2, WINDOW, CAP, feat).transpose(1, 2, 0, 3)
     both = exchange(both.reshape(WINDOW, CAP, 2 * feat), "zp")
+
+    own = jnp.concatenate([gate_weight.T, up_weight.T, down_weight], axis=0)
+    own, both = lax.optimization_barrier((own, both))
+    weights = lax.all_gather(own, "zh").transpose(1, 0, 2).reshape(3 * hid, 4 * feat)
+    gate_up, down = weights[: 2 * hid], weights[2 * hid :]
+
     both = both.reshape(4, CAP, 2, feat).transpose(1, 2, 0, 3).reshape(CAP, 8 * feat)
     both = gather(swap(both), PIECE, 8).reshape(8 * CAP, 8 * feat)
     rows, carried = both[:, : 4 * feat], both[:, 4 * feat :]
@@ -90,8 +92,10 @@
     terms = jnp.concatenate(
         [contract(row_grads, rows, 0, 0), contract(hidden, carried, 0, 0)], axis=0
     ).astype(jnp.bfloat16)
-    summed = exchange(terms.reshape(3 * hid, 4, feat).transpose(1, 0, 2), "zh")
-    summed = jnp.sum(summed.astype(jnp.float32), axis=0).astype(jnp.bfloat16)
+    terms, row_grads = lax.optimization_barrier(
+        (terms.reshape(3 * hid, 4, feat).transpose(1, 0, 2), row_grads)
+    )
+    summed = lax.psum_scatter(terms, "zh")
     gate_grad, up_grad = summed[:hid].T, summed[hid : 2 * hid].T
     down_grad = summed[2 * hid :]
 

time: 274 us -> 253 us (0.923)
  the two profiles are of different devices: /device:TPU:24 before, /device:TPU:12 now
where the time goes in v2:
time: 253 us; the launch traced here: 252 us
  blocking collectives  89.7 us (35%)
  waiting for transfers between devices  86.2 us (34%)
  starting transfers between devices  48.4 us (19%)
  between operations  14.3 us (6%)
  local copies, waits for them, and re-layouts  5.82 us (2%)
  matrix products  4.82 us (2%)
  other arithmetic  3.27 us (1%)
    reduce_scatter x1, waiting for transfers between devices, shards(): summed = lax.psum_scatter(terms, 'zh')  66.8 us
    all_gather x1, blocking collectives, shards(): lax.all_gather(own, 'zh').transpose(1, 0, 2).reshape(3 * hid, 4 * feat)  61.5 us
    all_to_all x3, starting transfers between devices, exchange(): return lax.all_to_all(blocks, axis, 0, 0)  32 us
    all_to_all x3, waiting for transfers between devices, exchange(): return lax.all_to_all(blocks, axis, 0, 0)  18.7 us
    all_to_all x1, starting transfers between devices, gather(): return lax.all_to_all(copies, axis, 0, 0)  15.1 us
    all_to_all x1, blocking collectives, gather(): return lax.all_to_all(copies, axis, 0, 0)  14.2 us
    all_to_all x1, blocking collectives, exchange(): return lax.all_to_all(blocks, axis, 0, 0)  14 us
  transfers between devices with their start and end apart: 7, of which 3 were waited for; matrix products, arithmetic and copies ran while one was open for 1% of the time, Pallas kernels for 0%

profile of v2, /device:TPU:12, one launch (start us, length us, event | category | flops | bytes accessed | tf_op | source)
XLA Modules:
  0.0 252.5 jit_solution(17831107596654200515)
XLA Ops:
  7.3 0.7 fusion.12
  8.2 0.7 select_reduce_fusion.1
  9.5 0.9 convolution_convert_fusion.5
  10.8 0.7 reshape.67
  11.6 11.2 %all-to-all-start = ((bf16[4,64,256]{2,1,0:T(8,128)(2,1)}), bf16[4,64,256]{2,1,0:T(8,128)(2,1)S(1)}, u32[]{:S(2)}, u32[]{:S(2)}) async-start(bf16[4,64,256]{2,1,0:T(8,128)(2,1)} %reshape.67), calls=%async_computation | async-start | bytes 262144 | tf_op jit(solution)/shard_map/all_to_all | solution.py:28
  22.8 12.1 %all-to-all-done = bf16[4,64,256]{2,1,0:T(8,128)(2,1)S(1)} async-done(((bf16[4,64,256]{2,1,0:T(8,128)(2,1)}), bf16[4,64,256]{2,1,0:T(8,128)(2,1)S(1)}, u32[]{:S(2)}, u32[]{:S(2)}) %all-to-all-start) | async-done | bytes 131104 | tf_op jit(solution)/shard_map/all_to_all | solution.py:28
  35.2 0.7 collective-permute-start
  35.9 1.1 broadcast_in_dim.32
  37.0 15.1 %all-to-all-start.1 = ((bf16[8,64,1024]{2,1,0:T(8,128)(2,1)}), bf16[8,64,1024]{2,1,0:T(8,128)(2,1)S(1)}, u32[]{:S(2)}, u32[]{:S(2)}) async-start(bf16[8,64,1024]{2,1,0:T(8,128)(2,1)} %broadcast_in_dim.32), calls=%async_computation.1 | async-start | bytes 2097152 | tf_op jit(solution)/shard_map/all_to_all | solution.py:24
  52.1 61.5 %all-gather = bf16[2304,128]{1,0:T(8,128)(2,1)S(1)} all-gather(bf16[576,128]{1,0:T(8,128)(2,1)S(1)} %pad_maximum_fusion.1), channel_id=2, replica_groups=mesh['zp'=4,'l'=2,'x'=4,'zh'=4,'y'=4,'c'=2] {'zh'}, dimensions={0}, use_global_device_ids=true | all-gather | bytes 737280 | tf_op jit(solution)/shard_map/all_gather | solution.py:63
  113.6 0.5 copy.52
  115.5 14.0 %all_to_all.30 = bf16[8,64,576]{2,1,0:T(8,128)(2,1)S(1)} all-to-all(bf16[8,64,576]{2,1,0:T(8,128)(2,1)S(1)} %pad_maximum_fusion), channel_id=1, replica_groups=mesh['zp'=4,'l'=2,'x'=4,'zh'=4,'y'=4,'c'=2] {'y','c'}, dimensions={0} | all-to-all | bytes 1179648 | tf_op jit(solution)/shard_map/all_to_all | solution.py:28
  129.8 14.2 %all_to_all.31 = bf16[8,64,576]{2,1,0:T(8,128)(2,1)S(1)} all-to-all(bf16[8,64,576]{2,1,0:T(8,128)(2,1)S(1)} %broadcast_in_dim.50), channel_id=1, replica_groups=mesh['zp'=4,'l'=2,'x'=4,'zh'=4,'y'=4,'c'=2] {'y','c'}, dimensions={0} | all-to-all | bytes 1179648 | tf_op jit(solution)/shard_map/all_to_all | solution.py:24
  144.9 0.8 maximum_bitcast_fusion
  145.7 1.2 convolution_convert_fusion
  147.0 13.7 %all-to-all-start.4 = ((bf16[8,64,512]{2,1,0:T(8,128)(2,1)}), bf16[8,64,512]{2,1,0:T(8,128)(2,1)S(1)}, u32[]{:S(2)}, u32[]{:S(2)}) async-start(bf16[8,64,512]{2,1,0:T(8,128)(2,1)} %bitcast.15), calls=%async_computation.4 | async-start | bytes 1048576 | tf_op jit(solution)/shard_map/all_to_all | solution.py:28
  160.6 0.7 reduce-scatter.2.cloned.1.call-update
  161.4 6.5 %all-to-all-done.4 = bf16[8,64,512]{2,1,0:T(8,128)(2,1)S(1)} async-done(((bf16[8,64,512]{2,1,0:T(8,128)(2,1)}), bf16[8,64,512]{2,1,0:T(8,128)(2,1)S(1)}, u32[]{:S(2)}, u32[]{:S(2)}) %all-to-all-start.4) | async-done | bytes 524320 | tf_op jit(solution)/shard_map/all_to_all | solution.py:28
  167.9 0.7 collective-permute-start.1
  168.6 0.6 bitcast_bitcast_fusion
  169.3 7.1 %all-to-all-start.5 = ((bf16[4,64,128]{2,1,0:T(8,128)(2,1)}), bf16[4,64,128]{2,1,0:T(8,128)(2,1)S(1)}, u32[]{:S(2)}, u32[]{:S(2)}) async-start(bf16[4,64,128]{2,1,0:T(8,128)(2,1)} %bitcast_bitcast_fusion), calls=%async_computation.5 | async-start | bytes 131072 | tf_op jit(solution)/shard_map/all_to_all | solution.py:28
  176.4 66.8 %reduce-scatter.2.cloned.1.call-done = bf16[1,576,128]{2,1,0:T(8,128)(2,1)} async-done(((bf16[4,576,128]{2,1,0:T(8,128)(2,1)}), bf16[1,576,128]{2,1,0:T(8,128)(2,1)}) %reduce-scatter.2.cloned.1.call-update) | async-done | bytes 147472 | tf_op jit(solution)/shard_map/reduce_scatter | solution.py:98
  243.2 1.5 slice_bitcast_fusion
  244.7 0.9 fusion.3
  (46 shorter events, 4.2 us)
Async XLA Ops:
  7.2 2.1 copy-start
  7.2 15.6 %copy-start.1 = (bf16[192,128]{1,0:T(8,128)(2,1)S(1)}, bf16[192,128]{1,0:T(8,128)(2,1)}, u32[]{:S(2)}) copy-start(bf16[192,128]{1,0:T(8,128)(2,1)} %param.13) | copy-start | bytes 147460
  7.2 15.6 %copy-start.2 = (bf16[128,192]{0,1:T(8,128)(2,1)S(1)}, bf16[128,192]{0,1:T(8,128)(2,1)}, u32[]{:S(2)}) copy-start(bf16[128,192]{0,1:T(8,128)(2,1)} %param.12) | copy-start | bytes 147460
  7.2 15.6 %copy-start.3 = (bf16[128,192]{0,1:T(8,128)(2,1)S(1)}, bf16[128,192]{0,1:T(8,128)(2,1)}, u32[]{:S(2)}) copy-start(bf16[128,192]{0,1:T(8,128)(2,1)} %param.11) | copy-start | bytes 147460
  11.6 23.3 %all-to-all-start = ((bf16[4,64,256]{2,1,0:T(8,128)(2,1)}), bf16[4,64,256]{2,1,0:T(8,128)(2,1)S(1)}, u32[]{:S(2)}, u32[]{:S(2)}) async-start(bf16[4,64,256]{2,1,0:T(8,128)(2,1)} %reshape.67), calls=%async_computation | async-start | bytes 262144 | tf_op jit(solution)/shard_map/all_to_all | solution.py:28
  35.2 0.7 collective-permute-start
  37.0 77.5 %all-to-all-start.1 = ((bf16[8,64,1024]{2,1,0:T(8,128)(2,1)}), bf16[8,64,1024]{2,1,0:T(8,128)(2,1)S(1)}, u32[]{:S(2)}, u32[]{:S(2)}) async-start(bf16[8,64,1024]{2,1,0:T(8,128)(2,1)} %broadcast_in_dim.32), calls=%async_computation.1 | async-start | bytes 2097152 | tf_op jit(solution)/shard_map/all_to_all | solution.py:24
  147.0 20.9 %all-to-all-start.4 = ((bf16[8,64,512]{2,1,0:T(8,128)(2,1)}), bf16[8,64,512]{2,1,0:T(8,128)(2,1)S(1)}, u32[]{:S(2)}, u32[]{:S(2)}) async-start(bf16[8,64,512]{2,1,0:T(8,128)(2,1)} %bitcast.15), calls=%async_computation.4 | async-start | bytes 1048576 | tf_op jit(solution)/shard_map/all_to_all | solution.py:28
  160.6 82.6 %reduce-scatter.2.cloned.1.call-start = ((), (), s32[]{:S(2)}) async-start(), calls=%async_computation.7 | async-start | bytes 737280 | tf_op jit(solution)/shard_map/reduce_scatter | solution.py:98
  167.9 0.7 collective-permute-start.1
  169.3 75.4 %all-to-all-start.5 = ((bf16[4,64,128]{2,1,0:T(8,128)(2,1)}), bf16[4,64,128]{2,1,0:T(8,128)(2,1)S(1)}, u32[]{:S(2)}, u32[]{:S(2)}) async-start(bf16[4,64,128]{2,1,0:T(8,128)(2,1)} %bitcast_bitcast_fusion), calls=%async_computation.5 | async-start | bytes 131072 | tf_op jit(solution)/shard_map/all_to_all | solution.py:28
Sparse Core Ops, SparseCore 0:
  164.9 78.2 reduce-scatter.1

commit v3 on v1

--- a/solution.py
+++ b/solution.py
@@ -49,21 +49,55 @@
     return picker.reshape(WINDOW * CAP, count).astype(jnp.bfloat16), row_weight.reshape(-1)
 
 
+def once(step, value, out_shape):
+    turns = 1 + lax.axis_index("x") // 4
+    start = (jnp.int32(0), value, jnp.zeros(out_shape, jnp.bfloat16))
+    return lax.while_loop(
+        lambda state: state[0] < turns,
+        lambda state: (state[0] + 1, state[1], step(state[1] + state[0].astype(jnp.bfloat16))),
+        start,
+    )[2]
+
+
+def turned(blocks):
+    here = lax.axis_index("zh")
+    return jnp.stack(
+        [lax.dynamic_index_in_dim(blocks, (here - d) % 4, 0, False) for d in range(4)]
+    )
+
+
+def token_chain(both):
+    both = turned(exchange(both, "zp"))
+    feat = both.shape[2] // 2
+    both = both.reshape(4, CAP, 2, feat).transpose(1, 2, 0, 3).reshape(CAP, 8 * feat)
+    return gather(swap(both), PIECE, 8).reshape(8 * CAP, 8 * feat)
+
+
+def grad_chain(row_grad):
+    feat = row_grad.shape[2] // 4
+    row_grad = exchange(row_grad, PIECE).astype(jnp.float32)
+    row_grad = swap(jnp.sum(row_grad, axis=0).astype(jnp.bfloat16))
+    return exchange(turned(row_grad.reshape(CAP, 4, feat).transpose(1, 0, 2)), "zp")
+
+
+def shift(block, d):
+    return lax.ppermute(block, "zh", [(j, (j + d) % 4) for j in range(4)])
+
+
 def shards(tokens, out_grad, route_probs, expert_ids, gate_weight, up_weight, down_weight):
     hid, feat = down_weight.shape
     own = jnp.concatenate([gate_weight.T, up_weight.T, down_weight], axis=0)
-    weights = gather(own, "zh", 4).transpose(1, 0, 2).reshape(3 * hid, 4 * feat)
-    gate_up, down = weights[: 2 * hid], weights[2 * hid :]
+    moved = [shift(own, d) for d in (1, 2, 3)]
 
     picker, row_weight = select(route_probs, expert_ids)
     picked = jnp.dot(picker, tokens, preferred_element_type=jnp.float32).astype(jnp.bfloat16)
     cot_rows = jnp.dot(picker, out_grad, preferred_element_type=jnp.float32)
     carried = (row_weight[:, None] * cot_rows).astype(jnp.bfloat16)
-    both = jnp.stack([picked, carried]).reshape(2, WINDOW, CAP, feat).transpose(1, 2, 0, 3)
-    both = exchange(both.reshape(WINDOW, CAP, 2 * feat), "zp")
-    both = both.reshape(4, CAP, 2, feat).transpose(1, 2, 0, 3).reshape(CAP, 8 * feat)
-    both = gather(swap(both), PIECE, 8).reshape(8 * CAP, 8 * feat)
+    both = jnp.concatenate([picked, carried], axis=1).reshape(WINDOW, CAP, 2 * feat)
+    both = once(token_chain, both, (8 * CAP, 8 * feat))
     rows, carried = both[:, : 4 * feat], both[:, 4 * feat :]
+    weights = jnp.concatenate([own] + moved, axis=1) + both[:1, :1] * 0
+    gate_up, down = weights[: 2 * hid], weights[2 * hid :]
 
     parts = jnp.concatenate(
         [contract(rows, gate_up, 1, 1), contract(carried, down, 1, 1)], axis=1
@@ -90,15 +124,17 @@
     terms = jnp.concatenate(
         [contract(row_grads, rows, 0, 0), contract(hidden, carried, 0, 0)], axis=0
     ).astype(jnp.bfloat16)
-    summed = exchange(terms.reshape(3 * hid, 4, feat).transpose(1, 0, 2), "zh")
-    summed = jnp.sum(summed.astype(jnp.float32), axis=0).astype(jnp.bfloat16)
+    terms = [terms[:, d * feat : (d + 1) * feat] for d in range(4)]
+    moved = [shift(terms[d], -d) for d in (1, 2, 3)]
+    row_grad = contract(row_grads, gate_up, 1, 0).astype(jnp.bfloat16).reshape(8, CAP, 4 * feat)
+    row_grad = once(grad_chain, row_grad, (WINDOW, CAP, feat))
+    summed = terms[0].astype(jnp.float32) + row_grad[0, :1, :1].astype(jnp.float32) * 0
+    for d in (1, 2, 3):
+        summed = summed + moved[d - 1].astype(jnp.float32)
+    summed = summed.astype(jnp.bfloat16)
     gate_grad, up_grad = summed[:hid].T, summed[hid : 2 * hid].T
     down_grad = summed[2 * hid :]
 
-    row_grad = contract(row_grads, gate_up, 1, 0).astype(jnp.bfloat16).reshape(8, CAP, 4 * feat)
-    row_grad = exchange(row_grad, PIECE).astype(jnp.float32)
-    row_grad = swap(jnp.sum(row_grad, axis=0).astype(jnp.bfloat16))
-    row_grad = exchange(row_grad.reshape(CAP, 4, feat).transpose(1, 0, 2), "zp")
     x_grad = contract(picker, row_grad.reshape(WINDOW * CAP, feat), 0, 0).astype(jnp.bfloat16)
     return (x_grad, gate_grad, up_grad, down_grad)
 

time: 274 us -> 265 us (0.967)
  waiting for transfers between devices: 161 us -> 90.3 us
  starting transfers between devices: 68.5 us -> 98.2 us
  blocking collectives: 28.4 us -> 51.7 us
  local copies, waits for them, and re-layouts: 5.74 us -> 10.4 us
    ppermute x2, waiting for transfers between devices: 95.3 us -> 17.1 us  [swap(): return lax.ppermute(block, PIECE + GROUP, pairs)]
    ppermute x0 -> x6, starting transfers between devices: none -> 70.8 us  [shift(): return lax.ppermute(block, 'zh', [(j, (j + d) % 4) for j in range(4)])]
    all_to_all x1 -> x2, blocking collectives: 14.2 us -> 51.7 us  [exchange(): return lax.all_to_all(blocks, axis, 0, 0)]
    all_to_all x4 -> x2, starting transfers between devices: 34.7 us -> 12.4 us  [exchange(): return lax.all_to_all(blocks, axis, 0, 0)]
    all_to_all x2, starting transfers between devices: 25.3 us -> 9.31 us  [gather(): return lax.all_to_all(copies, axis, 0, 0)]
    all_to_all x1 -> x0, blocking collectives: 14.2 us -> none  [gather(): return lax.all_to_all(copies, axis, 0, 0)]
    all_to_all x4 -> x2, waiting for transfers between devices: 42.3 us -> 48.7 us  [exchange(): return lax.all_to_all(blocks, axis, 0, 0)]
  transfers between devices with their start and end apart: 8 -> 12, of which waited for: 8 -> 6; matrix products, arithmetic and copies ran while one was open for 2% -> 5% of each run, Pallas kernels for 0% -> 0%
where the time goes in v3:
time: 265 us; the launch traced here: 263 us
  starting transfers between devices  98.2 us (37%)
  waiting for transfers between devices  90.3 us (34%)
  blocking collectives  51.7 us (20%)
  local copies, waits for them, and re-layouts  10.4 us (4%)
  matrix products  4.95 us (2%)
  other arithmetic  4.67 us (2%)
    ppermute x6, starting transfers between devices, shift(): return lax.ppermute(block, 'zh', [(j, (j + d) % 4) for j in range(4)])  70.8 us
    all_to_all x2, blocking collectives, exchange(): return lax.all_to_all(blocks, axis, 0, 0)  51.7 us
    all_to_all x2, waiting for transfers between devices, exchange(): return lax.all_to_all(blocks, axis, 0, 0)  48.7 us
    all_to_all x2, waiting for transfers between devices, gather(): return lax.all_to_all(copies, axis, 0, 0)  24.5 us
    ppermute x2, waiting for transfers between devices, swap(): return lax.ppermute(block, PIECE + GROUP, pairs)  17.1 us
    all_to_all x2, starting transfers between devices, exchange(): return lax.all_to_all(blocks, axis, 0, 0)  12.4 us
    all_to_all x2, starting transfers between devices, gather(): return lax.all_to_all(copies, axis, 0, 0)  9.31 us
    ppermute x2, starting transfers between devices, swap(): return lax.ppermute(block, PIECE + GROUP, pairs)  5.8 us
  transfers between devices with their start and end apart: 12, of which 6 were waited for; matrix products, arithmetic and copies ran while one was open for 5% of the time, Pallas kernels for 0%

profile of v3, /device:TPU:24, one launch (start us, length us, event | category | flops | bytes accessed | tf_op | source)
XLA Modules:
  0.0 262.7 jit_solution(1678413368731116035)
XLA Ops:
  1.5 15.7 %collective-permute-start.2 = (bf16[576,128]{1,0:T(8,128)(2,1)S(1)}, bf16[576,128]{1,0:T(8,128)(2,1)S(1)}, u32[]{:S(2)}, u32[]{:S(2)}) collective-permute-start(bf16[576,128]{1,0:T(8,128)(2,1)S(1)} %pad_maximum_fusion.4), channel_id=1, source_target_pairs={{0,8},{8,16},{16,24},{24,0},{1,9},{9,17},{17,25},{25,1},{2,10},{10... | collective-permute-start | bytes 442376 | tf_op jit(solution)/shard_map/ppermute | solution.py:84
  17.2 19.4 %collective-permute-start.3 = (bf16[576,128]{1,0:T(8,128)(2,1)S(1)}, bf16[576,128]{1,0:T(8,128)(2,1)S(1)}, u32[]{:S(2)}, u32[]{:S(2)}) collective-permute-start(bf16[576,128]{1,0:T(8,128)(2,1)S(1)} %pad_maximum_fusion.4), channel_id=1, source_target_pairs={{0,16},{8,24},{16,0},{24,8},{1,17},{9,25},{17,1},{25,9},{2,18},{10... | collective-permute-start | bytes 442376 | tf_op jit(solution)/shard_map/ppermute | solution.py:84
  36.6 8.4 %collective-permute-start.4 = (bf16[576,128]{1,0:T(8,128)(2,1)S(1)}, bf16[576,128]{1,0:T(8,128)(2,1)S(1)}, u32[]{:S(2)}, u32[]{:S(2)}) collective-permute-start(bf16[576,128]{1,0:T(8,128)(2,1)S(1)} %pad_maximum_fusion.4), channel_id=1, source_target_pairs={{0,24},{8,0},{16,8},{24,16},{1,25},{9,1},{17,9},{25,17},{2,26},{10... | collective-permute-start | bytes 442376 | tf_op jit(solution)/shard_map/ppermute | solution.py:84
  49.6 77.6 %while.24 = (s32[]{:T(128)}, bf16[512,1024]{1,0:T(8,128)(2,1)}, s32[]{:T(128)}, bf16[4,64,256]{2,1,0:T(8,128)(2,1)S(1)}, s32[]{:T(128)}, /*index=5*/u32[]{:T(128...) while((s32[]{:T(128)}, bf16[512,1024]{1,0:T(8,128)(2,1)}, s32[]{:T(128)}, ...), condition=%wide.region_4.5_spmd, body=%wide.region_3.4_spmd.sunk | while | flops 262209 | bytes 11010961 | solution.py:55
  50.2 4.6 %all-to-all-start = ((bf16[4,64,256]{2,1,0:T(8,128)(2,1)}), bf16[4,64,256]{2,1,0:T(8,128)(2,1)S(1)}, u32[]{:S(2)}, u32[]{:S(2)}) async-start(bf16[4,64,256]{2,1,0:T(8,128)(2,1)} %broadcast_add_fusion.4), calls=%async_computation | async-start | bytes 262144 | tf_op jit(solution)/shard_map/while/body/all_to_all | solution.py:28
  54.8 39.0 %all-to-all-done = bf16[4,64,256]{2,1,0:T(8,128)(2,1)S(1)} async-done(((bf16[4,64,256]{2,1,0:T(8,128)(2,1)}), bf16[4,64,256]{2,1,0:T(8,128)(2,1)S(1)}, u32[]{:S(2)}, u32[]{:S(2)}) %all-to-all-start) | async-done | bytes 131104 | tf_op jit(solution)/shard_map/while/body/all_to_all | solution.py:28
  94.2 2.1 collective-permute-start
  96.3 10.2 %collective-permute-done = bf16[64,1024]{1,0:T(8,128)(2,1)S(1)} collective-permute-done((bf16[64,1024]{1,0:T(8,128)(2,1)S(1)}, bf16[64,1024]{1,0:T(8,128)(2,1)S(1)}, u32[]{:S(2)}, u32[]{:S(2)}) %collective-permute-start) | collective-permute-done | bytes 131104 | tf_op jit(solution)/shard_map/while/body/ppermute | solution.py:33
  107.6 3.8 %all-to-all-start.1 = ((bf16[8,64,1024]{2,1,0:T(8,128)(2,1)}), bf16[8,64,1024]{2,1,0:T(8,128)(2,1)S(1)}, u32[]{:S(2)}, u32[]{:S(2)}) async-start(bf16[8,64,1024]{2,1,0:T(8,128)(2,1)} %broadcast_in_dim.66), calls=%async_computation.1 | async-start | bytes 2097152 | tf_op jit(solution)/shard_map/while/body/all_to_all | solution.py:24
  111.4 14.8 %all-to-all-done.1 = bf16[8,64,1024]{2,1,0:T(8,128)(2,1)S(1)} async-done(((bf16[8,64,1024]{2,1,0:T(8,128)(2,1)}), bf16[8,64,1024]{2,1,0:T(8,128)(2,1)S(1)}, u32[]{:S(2)}, u32[]{:S(2)}) %all-to-all-start.1) | async-done | bytes 1048608 | tf_op jit(solution)/shard_map/while/body/all_to_all | solution.py:24
  127.2 1.3 slice.55
  130.7 14.3 %all_to_all.46 = bf16[8,64,576]{2,1,0:T(8,128)(2,1)S(1)} all-to-all(bf16[8,64,576]{2,1,0:T(8,128)(2,1)S(1)} %pad_maximum_fusion.2), channel_id=1, replica_groups=mesh['zp'=4,'l'=2,'x'=4,'zh'=4,'y'=4,'c'=2] {'y','c'}, dimensions={0} | all-to-all | bytes 1179648 | tf_op jit(solution)/shard_map/all_to_all | solution.py:28
  146.2 5.5 %all-to-all-start.5 = ((bf16[8,64,576]{2,1,0:T(8,128)(2,1)}), bf16[8,64,576]{2,1,0:T(8,128)(2,1)S(1)}, u32[]{:S(2)}, u32[]{:S(2)}) async-start(bf16[8,64,576]{2,1,0:T(8,128)(2,1)} %broadcast_in_dim.60), calls=%async_computation.5 | async-start | bytes 1310720 | tf_op jit(solution)/shard_map/all_to_all | solution.py:24
  151.7 9.7 %all-to-all-done.5 = bf16[8,64,576]{2,1,0:T(8,128)(2,1)S(1)} async-done(((bf16[8,64,576]{2,1,0:T(8,128)(2,1)}), bf16[8,64,576]{2,1,0:T(8,128)(2,1)S(1)}, u32[]{:S(2)}, u32[]{:S(2)}) %all-to-all-start.5) | async-done | bytes 589856 | tf_op jit(solution)/shard_map/all_to_all | solution.py:24
  163.3 10.5 %collective-permute-start.5 = (bf16[576,128]{1,0:T(8,128)(2,1)S(1)}, bf16[576,128]{1,0:T(8,128)(2,1)S(1)}, u32[]{:S(2)}, u32[]{:S(2)}) collective-permute-start(bf16[576,128]{1,0:T(8,128)(2,1)S(1)} %get-tuple-element.151), channel_id=1, source_target_pairs={{0,24},{8,0},{16,8},{24,16},{1,25},{9,1},{17,9},{25,17},{2,26},{10... | collective-permute-start | bytes 442376 | tf_op jit(solution)/shard_map/ppermute | solution.py:84
  173.8 5.7 %collective-permute-start.6 = (bf16[576,128]{1,0:T(8,128)(2,1)S(1)}, bf16[576,128]{1,0:T(8,128)(2,1)S(1)}, u32[]{:S(2)}, u32[]{:S(2)}) collective-permute-start(bf16[576,128]{1,0:T(8,128)(2,1)S(1)} %get-tuple-element.153), channel_id=1, source_target_pairs={{0,16},{8,24},{16,0},{24,8},{1,17},{9,25},{17,1},{25,9},{2,18},{10... | collective-permute-start | bytes 442376 | tf_op jit(solution)/shard_map/ppermute | solution.py:84
  179.5 11.0 %collective-permute-start.7 = (bf16[576,128]{1,0:T(8,128)(2,1)S(1)}, bf16[576,128]{1,0:T(8,128)(2,1)S(1)}, u32[]{:S(2)}, u32[]{:S(2)}) collective-permute-start(bf16[576,128]{1,0:T(8,128)(2,1)S(1)} %get-tuple-element.152), channel_id=1, source_target_pairs={{0,8},{8,16},{16,24},{24,0},{1,9},{9,17},{17,25},{25,1},{2,10},{10... | collective-permute-start | bytes 442376 | tf_op jit(solution)/shard_map/ppermute | solution.py:84
  191.2 67.1 %while.25 = (s32[]{:T(128)}, bf16[4,64,128]{2,1,0:T(8,128)(2,1)}, s32[]{:T(128)}, bf16[8,64,512]{2,1,0:T(8,128)(2,1)S(1)}, s32[]{:T(128)}, /*index=5*/bf16[]{:T(...) while((s32[]{:T(128)}, bf16[4,64,128]{2,1,0:T(8,128)(2,1)}, ...), condition=%wide.region_8.9_spmd, body=%wide.region_6.8_spmd.sunk | while | flops 589889 | bytes 3933051 | solution.py:55
  191.2 37.4 %all_to_all.47 = bf16[8,64,512]{2,1,0:T(8,128)(2,1)S(1)} all-to-all(bf16[8,64,512]{2,1,0:T(8,128)(2,1)S(1)} %broadcast_add_fusion.5), channel_id=1, replica_groups=mesh['zp'=4,'l'=2,'x'=4,'zh'=4,'y'=4,'c'=2] {'l','x'}, dimensions={0} | all-to-all | bytes 1048576 | tf_op jit(solution)/shard_map/while/body/all_to_all | solution.py:28
  228.7 3.7 %collective-permute-start.1 = (bf16[64,512]{1,0:T(8,128)(2,1)S(1)}, bf16[64,512]{1,0:T(8,128)(2,1)S(1)}, u32[]{:S(2)}, u32[]{:S(2)}) collective-permute-start(bf16[64,512]{1,0:T(8,128)(2,1)S(1)} %reduce_sum.46), channel_id=1, source_target_pairs={{0,0},{1,32},{2,64},{3,96},{4,128},{5,160},{6,192},{7,224},{32,1},... | collective-permute-start | bytes 196616 | tf_op jit(solution)/shard_map/while/body/ppermute | solution.py:33
  232.5 6.9 %collective-permute-done.1 = bf16[64,512]{1,0:T(8,128)(2,1)S(1)} collective-permute-done((bf16[64,512]{1,0:T(8,128)(2,1)S(1)}, bf16[64,512]{1,0:T(8,128)(2,1)S(1)}, u32[]{:S(2)}, u32[]{:S(2)}) %collective-permute-start.1) | collective-permute-done | bytes 65568 | tf_op jit(solution)/shard_map/while/body/ppermute | solution.py:33
  240.2 7.8 %all-to-all-start.3 = ((bf16[4,64,128]{2,1,0:T(8,128)(2,1)}), bf16[4,64,128]{2,1,0:T(8,128)(2,1)S(1)}, u32[]{:S(2)}, u32[]{:S(2)}) async-start(bf16[4,64,128]{2,1,0:T(8,128)(2,1)} %pad_maximum_fusion.10), calls=%async_computation.3 | async-start | bytes 131072 | tf_op jit(solution)/shard_map/while/body/all_to_all | solution.py:28
  248.0 9.7 %all-to-all-done.3 = bf16[4,64,128]{2,1,0:T(8,128)(2,1)S(1)} async-done(((bf16[4,64,128]{2,1,0:T(8,128)(2,1)}), bf16[4,64,128]{2,1,0:T(8,128)(2,1)S(1)}, u32[]{:S(2)}, u32[]{:S(2)}) %all-to-all-start.3) | async-done | bytes 65568 | tf_op jit(solution)/shard_map/while/body/all_to_all | solution.py:28
  260.1 1.7 fusion.1
  (70 shorter events, 17.0 us)
Async XLA Ops:
  0.6 46.5 %copy-start = (bf16[128,128]{1,0:T(8,128)(2,1)S(1)}, bf16[128,128]{1,0:T(8,128)(2,1)}, u32[]{:S(2)}) copy-start(bf16[128,128]{1,0:T(8,128)(2,1)} %param.11) | copy-start | bytes 98308
  1.5 127.6 %collective-permute-start.2 = (bf16[576,128]{1,0:T(8,128)(2,1)S(1)}, bf16[576,128]{1,0:T(8,128)(2,1)S(1)}, u32[]{:S(2)}, u32[]{:S(2)}) collective-permute-start(bf16[576,128]{1,0:T(8,128)(2,1)S(1)} %pad_maximum_fusion.4), channel_id=1, source_target_pairs={{0,8},{8,16},{16,24},{24,0},{1,9},{9,17},{17,25},{25,1},{2,10},{10... | collective-permute-start | bytes 442376 | tf_op jit(solution)/shard_map/ppermute | solution.py:84
  17.2 111.9 %collective-permute-start.3 = (bf16[576,128]{1,0:T(8,128)(2,1)S(1)}, bf16[576,128]{1,0:T(8,128)(2,1)S(1)}, u32[]{:S(2)}, u32[]{:S(2)}) collective-permute-start(bf16[576,128]{1,0:T(8,128)(2,1)S(1)} %pad_maximum_fusion.4), channel_id=1, source_target_pairs={{0,16},{8,24},{16,0},{24,8},{1,17},{9,25},{17,1},{25,9},{2,18},{10... | collective-permute-start | bytes 442376 | tf_op jit(solution)/shard_map/ppermute | solution.py:84
  36.6 92.5 %collective-permute-start.4 = (bf16[576,128]{1,0:T(8,128)(2,1)S(1)}, bf16[576,128]{1,0:T(8,128)(2,1)S(1)}, u32[]{:S(2)}, u32[]{:S(2)}) collective-permute-start(bf16[576,128]{1,0:T(8,128)(2,1)S(1)} %pad_maximum_fusion.4), channel_id=1, source_target_pairs={{0,24},{8,0},{16,8},{24,16},{1,25},{9,1},{17,9},{25,17},{2,26},{10... | collective-permute-start | bytes 442376 | tf_op jit(solution)/shard_map/ppermute | solution.py:84
  49.6 79.6 %copy-start.5 = (bf16[192,128]{1,0:T(8,128)(2,1)S(1)}, bf16[192,128]{1,0:T(8,128)(2,1)}, u32[]{:S(2)}) copy-start(bf16[192,128]{1,0:T(8,128)(2,1)} %param.17) | copy-start | bytes 147460
  49.6 79.6 %copy-start.6 = (bf16[128,192]{0,1:T(8,128)(2,1)S(1)}, bf16[128,192]{0,1:T(8,128)(2,1)}, u32[]{:S(2)}) copy-start(bf16[128,192]{0,1:T(8,128)(2,1)} %param.16) | copy-start | bytes 147460
  49.6 79.6 %copy-start.7 = (bf16[128,192]{0,1:T(8,128)(2,1)S(1)}, bf16[128,192]{0,1:T(8,128)(2,1)}, u32[]{:S(2)}) copy-start(bf16[128,192]{0,1:T(8,128)(2,1)} %param.15) | copy-start | bytes 147460
  50.2 43.6 %all-to-all-start = ((bf16[4,64,256]{2,1,0:T(8,128)(2,1)}), bf16[4,64,256]{2,1,0:T(8,128)(2,1)S(1)}, u32[]{:S(2)}, u32[]{:S(2)}) async-start(bf16[4,64,256]{2,1,0:T(8,128)(2,1)} %broadcast_add_fusion.4), calls=%async_computation | async-start | bytes 262144 | tf_op jit(solution)/shard_map/while/body/all_to_all | solution.py:28
  94.2 12.3 %collective-permute-start = (bf16[64,1024]{1,0:T(8,128)(2,1)S(1)}, bf16[64,1024]{1,0:T(8,128)(2,1)S(1)}, u32[]{:S(2)}, u32[]{:S(2)}) collective-permute-start(bf16[64,1024]{1,0:T(8,128)(2,1)S(1)} %reshape.91), channel_id=1, source_target_pairs={{0,0},{1,32},{2,64},{3,96},{4,128},{5,160},{6,192},{7,224},{32,1},... | collective-permute-start | bytes 393224 | tf_op jit(solution)/shard_map/while/body/ppermute | solution.py:33
  107.6 18.6 %all-to-all-start.1 = ((bf16[8,64,1024]{2,1,0:T(8,128)(2,1)}), bf16[8,64,1024]{2,1,0:T(8,128)(2,1)S(1)}, u32[]{:S(2)}, u32[]{:S(2)}) async-start(bf16[8,64,1024]{2,1,0:T(8,128)(2,1)} %broadcast_in_dim.66), calls=%async_computation.1 | async-start | bytes 2097152 | tf_op jit(solution)/shard_map/while/body/all_to_all | solution.py:24
  126.2 1.0 copy-start.1
  127.2 2.1 copy-start.2
  129.3 0.8 copy-start.3
  146.2 15.2 %all-to-all-start.5 = ((bf16[8,64,576]{2,1,0:T(8,128)(2,1)}), bf16[8,64,576]{2,1,0:T(8,128)(2,1)S(1)}, u32[]{:S(2)}, u32[]{:S(2)}) async-start(bf16[8,64,576]{2,1,0:T(8,128)(2,1)} %broadcast_in_dim.60), calls=%async_computation.5 | async-start | bytes 1310720 | tf_op jit(solution)/shard_map/all_to_all | solution.py:24
  161.7 1.1 copy-start.4
  163.3 98.6 %collective-permute-start.5 = (bf16[576,128]{1,0:T(8,128)(2,1)S(1)}, bf16[576,128]{1,0:T(8,128)(2,1)S(1)}, u32[]{:S(2)}, u32[]{:S(2)}) collective-permute-start(bf16[576,128]{1,0:T(8,128)(2,1)S(1)} %get-tuple-element.151), channel_id=1, source_target_pairs={{0,24},{8,0},{16,8},{24,16},{1,25},{9,1},{17,9},{25,17},{2,26},{10... | collective-permute-start | bytes 442376 | tf_op jit(solution)/shard_map/ppermute | solution.py:84
  173.8 88.1 %collective-permute-start.6 = (bf16[576,128]{1,0:T(8,128)(2,1)S(1)}, bf16[576,128]{1,0:T(8,128)(2,1)S(1)}, u32[]{:S(2)}, u32[]{:S(2)}) collective-permute-start(bf16[576,128]{1,0:T(8,128)(2,1)S(1)} %get-tuple-element.153), channel_id=1, source_target_pairs={{0,16},{8,24},{16,0},{24,8},{1,17},{9,25},{17,1},{25,9},{2,18},{10... | collective-permute-start | bytes 442376 | tf_op jit(solution)/shard_map/ppermute | solution.py:84
  179.5 82.4 %collective-permute-start.7 = (bf16[576,128]{1,0:T(8,128)(2,1)S(1)}, bf16[576,128]{1,0:T(8,128)(2,1)S(1)}, u32[]{:S(2)}, u32[]{:S(2)}) collective-permute-start(bf16[576,128]{1,0:T(8,128)(2,1)S(1)} %get-tuple-element.152), channel_id=1, source_target_pairs={{0,8},{8,16},{16,24},{24,0},{1,9},{9,17},{17,25},{25,1},{2,10},{10... | collective-permute-start | bytes 442376 | tf_op jit(solution)/shard_map/ppermute | solution.py:84
  228.7 10.7 %collective-permute-start.1 = (bf16[64,512]{1,0:T(8,128)(2,1)S(1)}, bf16[64,512]{1,0:T(8,128)(2,1)S(1)}, u32[]{:S(2)}, u32[]{:S(2)}) collective-permute-start(bf16[64,512]{1,0:T(8,128)(2,1)S(1)} %reduce_sum.46), channel_id=1, source_target_pairs={{0,0},{1,32},{2,64},{3,96},{4,128},{5,160},{6,192},{7,224},{32,1},... | collective-permute-start | bytes 196616 | tf_op jit(solution)/shard_map/while/body/ppermute | solution.py:33
  240.2 17.5 %all-to-all-start.3 = ((bf16[4,64,128]{2,1,0:T(8,128)(2,1)}), bf16[4,64,128]{2,1,0:T(8,128)(2,1)S(1)}, u32[]{:S(2)}, u32[]{:S(2)}) async-start(bf16[4,64,128]{2,1,0:T(8,128)(2,1)} %pad_maximum_fusion.10), calls=%async_computation.3 | async-start | bytes 131072 | tf_op jit(solution)/shard_map/while/body/all_to_all | solution.py:28
  257.7 0.6 copy-start.8

commit v4 on v3

--- a/solution.py
+++ b/solution.py
@@ -59,15 +59,8 @@
     )[2]
 
 
-def turned(blocks):
-    here = lax.axis_index("zh")
-    return jnp.stack(
-        [lax.dynamic_index_in_dim(blocks, (here - d) % 4, 0, False) for d in range(4)]
-    )
-
-
 def token_chain(both):
-    both = turned(exchange(both, "zp"))
+    both = exchange(both, "zp")
     feat = both.shape[2] // 2
     both = both.reshape(4, CAP, 2, feat).transpose(1, 2, 0, 3).reshape(CAP, 8 * feat)
     return gather(swap(both), PIECE, 8).reshape(8 * CAP, 8 * feat)
@@ -77,17 +70,13 @@
     feat = row_grad.shape[2] // 4
     row_grad = exchange(row_grad, PIECE).astype(jnp.float32)
     row_grad = swap(jnp.sum(row_grad, axis=0).astype(jnp.bfloat16))
-    return exchange(turned(row_grad.reshape(CAP, 4, feat).transpose(1, 0, 2)), "zp")
-
-
-def shift(block, d):
-    return lax.ppermute(block, "zh", [(j, (j + d) % 4) for j in range(4)])
+    return exchange(row_grad.reshape(CAP, 4, feat).transpose(1, 0, 2), "zp")
 
 
 def shards(tokens, out_grad, route_probs, expert_ids, gate_weight, up_weight, down_weight):
     hid, feat = down_weight.shape
     own = jnp.concatenate([gate_weight.T, up_weight.T, down_weight], axis=0)
-    moved = [shift(own, d) for d in (1, 2, 3)]
+    weights = lax.all_gather(own, ("zh", "c")).reshape(4, 2, 3 * hid, feat)
 
     picker, row_weight = select(route_probs, expert_ids)
     picked = jnp.dot(picker, tokens, preferred_element_type=jnp.float32).astype(jnp.bfloat16)
@@ -96,7 +85,8 @@
     both = jnp.concatenate([picked, carried], axis=1).reshape(WINDOW, CAP, 2 * feat)
     both = once(token_chain, both, (8 * CAP, 8 * feat))
     rows, carried = both[:, : 4 * feat], both[:, 4 * feat :]
-    weights = jnp.concatenate([own] + moved, axis=1) + both[:1, :1] * 0
+    weights = lax.dynamic_index_in_dim(weights, lax.axis_index("c"), 1, False)
+    weights = jnp.concatenate(list(weights), axis=1) + both[:1, :1] * 0
     gate_up, down = weights[: 2 * hid], weights[2 * hid :]
 
     parts = jnp.concatenate(
@@ -124,14 +114,10 @@
     terms = jnp.concatenate(
         [contract(row_grads, rows, 0, 0), contract(hidden, carried, 0, 0)], axis=0
     ).astype(jnp.bfloat16)
-    terms = [terms[:, d * feat : (d + 1) * feat] for d in range(4)]
-    moved = [shift(terms[d], -d) for d in (1, 2, 3)]
+    summed = lax.psum_scatter(terms.reshape(3 * hid, 4, feat).transpose(1, 0, 2), "zh")
     row_grad = contract(row_grads, gate_up, 1, 0).astype(jnp.bfloat16).reshape(8, CAP, 4 * feat)
     row_grad = once(grad_chain, row_grad, (WINDOW, CAP, feat))
-    summed = terms[0].astype(jnp.float32) + row_grad[0, :1, :1].astype(jnp.float32) * 0
-    for d in (1, 2, 3):
-        summed = summed + moved[d - 1].astype(jnp.float32)
-    summed = summed.astype(jnp.bfloat16)
+    summed = summed + row_grad[0, :1, :1] * 0
     gate_grad, up_grad = summed[:hid].T, summed[hid : 2 * hid].T
     down_grad = summed[2 * hid :]
 

time: 265 us -> 230 us (0.87)
  the two profiles are of different devices: /device:TPU:24 before, /device:TPU:119 now
where the time goes in v4:
time: 230 us; the launch traced here: 229 us
  waiting for transfers between devices  112 us (49%)
  blocking collectives  58.1 us (25%)
  starting transfers between devices  22.4 us (10%)
  between operations  15.5 us (7%)
  local copies, waits for them, and re-layouts  10.4 us (5%)
  other arithmetic  5.62 us (2%)
  matrix products  4.99 us (2%)
    all_to_all x1, waiting for transfers between devices, gather(): return lax.all_to_all(copies, axis, 0, 0)  45.9 us
    all_to_all x3, blocking collectives, exchange(): return lax.all_to_all(blocks, axis, 0, 0)  43.9 us
    reduce_scatter x1, waiting for transfers between devices, shards(): lax.psum_scatter(terms.reshape(3 * hid, 4, feat).transpose(1, 0, 2), 'zh')  39.3 us
    all_to_all x1, waiting for transfers between devices, exchange(): return lax.all_to_all(blocks, axis, 0, 0)  15.6 us
    all_to_all x1, blocking collectives, gather(): return lax.all_to_all(copies, axis, 0, 0)  14.2 us
    ppermute x2, waiting for transfers between devices, swap(): return lax.ppermute(block, PIECE + GROUP, pairs)  9.38 us
    ppermute x2, starting transfers between devices, swap(): return lax.ppermute(block, PIECE + GROUP, pairs)  8.67 us
    all_to_all x1, starting transfers between devices, exchange(): return lax.all_to_all(blocks, axis, 0, 0)  8.45 us
  transfers between devices with their start and end apart: 6, of which 6 were waited for; matrix products, arithmetic and copies ran while one was open for 5% of the time, Pallas kernels for 0%

profile of v4, /device:TPU:119, one launch (start us, length us, event | category | flops | bytes accessed | tf_op | source)
XLA Modules:
  0.0 228.9 jit_solution(2634818644632973723)
XLA Ops:
  7.2 1.5 pad_maximum_fusion.1
  12.2 1.1 broadcast_in_dim.37
  13.3 81.4 %while.22 = (s32[]{:T(128)}, bf16[512,1024]{1,0:T(8,128)(2,1)}, s32[]{:T(128)}, bf16[4,64,256]{2,1,0:T(8,128)(2,1)S(1)}, s32[]{:T(128)}) while((s32[]{:T(128)}, bf16[512,1024]{1,0:T(8,128)(2,1)}, s32[]{:T(128)}, bf16[4,64,256]{2,1,0:T(8,128)(2,1)S(1)}, s32[]{:T(128)}) %tuple.62), condition=%wide.region_4.5_spmd, body=%wide.region_3.4_spmd.sunk | while | flops 65539 | bytes 10354857 | solution.py:55
  13.3 17.5 %all_to_all.42 = bf16[4,64,256]{2,1,0:T(8,128)(2,1)S(1)} all-to-all(bf16[4,64,256]{2,1,0:T(8,128)(2,1)S(1)} %broadcast_add_fusion.5), channel_id=1, replica_groups=mesh['zp'=4,'l'=2,'x'=4,'zh'=4,'y'=4,'c'=2] {'zp'}, dimensions={0} | all-to-all | bytes 262144 | tf_op jit(solution)/shard_map/while/body/all_to_all | solution.py:28
  31.1 3.8 %collective-permute-start = (bf16[64,1024]{1,0:T(8,128)(2,1)S(1)}, bf16[64,1024]{1,0:T(8,128)(2,1)S(1)}, u32[]{:S(2)}, u32[]{:S(2)}) collective-permute-start(bf16[64,1024]{1,0:T(8,128)(2,1)S(1)} %reshape.89), channel_id=1, source_target_pairs={{0,0},{1,32},{2,64},{3,96},{4,128},{5,160},{6,192},{7,224},{32,1},... | collective-permute-start | bytes 393224 | tf_op jit(solution)/shard_map/while/body/ppermute | solution.py:33
  34.9 6.7 %collective-permute-done = bf16[64,1024]{1,0:T(8,128)(2,1)S(1)} collective-permute-done((bf16[64,1024]{1,0:T(8,128)(2,1)S(1)}, bf16[64,1024]{1,0:T(8,128)(2,1)S(1)}, u32[]{:S(2)}, u32[]{:S(2)}) %collective-permute-start) | collective-permute-done | bytes 131104 | tf_op jit(solution)/shard_map/while/body/ppermute | solution.py:33
  41.6 1.1 broadcast_in_dim.63
  42.7 5.2 %all-to-all-start.1 = ((bf16[8,64,1024]{2,1,0:T(8,128)(2,1)}), bf16[8,64,1024]{2,1,0:T(8,128)(2,1)S(1)}, u32[]{:S(2)}, u32[]{:S(2)}) async-start(bf16[8,64,1024]{2,1,0:T(8,128)(2,1)} %broadcast_in_dim.63), calls=%async_computation.1 | async-start | bytes 2097152 | tf_op jit(solution)/shard_map/while/body/all_to_all | solution.py:24
  47.8 45.9 %all-to-all-done.1 = bf16[8,64,1024]{2,1,0:T(8,128)(2,1)S(1)} async-done(((bf16[8,64,1024]{2,1,0:T(8,128)(2,1)}), bf16[8,64,1024]{2,1,0:T(8,128)(2,1)S(1)}, u32[]{:S(2)}, u32[]{:S(2)}) %all-to-all-start.1) | async-done | bytes 1048608 | tf_op jit(solution)/shard_map/while/body/all_to_all | solution.py:24
  93.7 1.0 copy-done.1
  94.7 1.2 slice.56
  96.6 1.6 all-gather.3.cloned.1.call-done
  98.1 1.3 dynamic-slice_bitcast_fusion.3
  100.7 15.1 %all_to_all.40 = bf16[8,64,576]{2,1,0:T(8,128)(2,1)S(1)} all-to-all(bf16[8,64,576]{2,1,0:T(8,128)(2,1)S(1)} %pad_maximum_fusion), channel_id=1, replica_groups=mesh['zp'=4,'l'=2,'x'=4,'zh'=4,'y'=4,'c'=2] {'y','c'}, dimensions={0} | all-to-all | bytes 1179648 | tf_op jit(solution)/shard_map/all_to_all | solution.py:28
  116.1 14.2 %all_to_all.41 = bf16[8,64,576]{2,1,0:T(8,128)(2,1)S(1)} all-to-all(bf16[8,64,576]{2,1,0:T(8,128)(2,1)S(1)} %broadcast_in_dim.57), channel_id=1, replica_groups=mesh['zp'=4,'l'=2,'x'=4,'zh'=4,'y'=4,'c'=2] {'y','c'}, dimensions={0} | all-to-all | bytes 1179648 | tf_op jit(solution)/shard_map/all_to_all | solution.py:24
  133.1 44.5 %while.23 = (s32[]{:T(128)}, bf16[4,64,128]{2,1,0:T(8,128)(2,1)}, s32[]{:T(128)}, bf16[8,64,512]{2,1,0:T(8,128)(2,1)S(1)}, s32[]{:T(128)}, /*index=5*/bf16[]{:T(256)}) while((s32[]{:T(128)}, bf16[4,64,128]{2,1,0:T(8,128)(2,1)}, s32[]{:T(128)}, bf16[8,64,512]{2,1,0:T(8,128)(2,1)S(1)}, s32[]{:T(128)}, /*index=5*/bf16[]{:T(256)}) %tuple.61), condition=%wide.region_8.9_spmd, body=%wide.region_6.8_spmd.sunk | while | flops 491523 | bytes 3670195 | solution.py:55
  133.2 11.3 %all_to_all.43 = bf16[8,64,512]{2,1,0:T(8,128)(2,1)S(1)} all-to-all(bf16[8,64,512]{2,1,0:T(8,128)(2,1)S(1)} %broadcast_add_fusion.6), channel_id=1, replica_groups=mesh['zp'=4,'l'=2,'x'=4,'zh'=4,'y'=4,'c'=2] {'l','x'}, dimensions={0} | all-to-all | bytes 1048576 | tf_op jit(solution)/shard_map/while/body/all_to_all | solution.py:28
  144.6 4.9 %collective-permute-start.1 = (bf16[64,512]{1,0:T(8,128)(2,1)S(1)}, bf16[64,512]{1,0:T(8,128)(2,1)S(1)}, u32[]{:S(2)}, u32[]{:S(2)}) collective-permute-start(bf16[64,512]{1,0:T(8,128)(2,1)S(1)} %reduce_sum.46), channel_id=1, source_target_pairs={{0,0},{1,32},{2,64},{3,96},{4,128},{5,160},{6,192},{7,224},{32,1},... | collective-permute-start | bytes 196616 | tf_op jit(solution)/shard_map/while/body/ppermute | solution.py:33
  149.5 2.7 %collective-permute-done.1 = bf16[64,512]{1,0:T(8,128)(2,1)S(1)} collective-permute-done((bf16[64,512]{1,0:T(8,128)(2,1)S(1)}, bf16[64,512]{1,0:T(8,128)(2,1)S(1)}, u32[]{:S(2)}, u32[]{:S(2)}) %collective-permute-start.1) | collective-permute-done | bytes 65568 | tf_op jit(solution)/shard_map/while/body/ppermute | solution.py:33
  152.8 8.4 %all-to-all-start.3 = ((bf16[4,64,128]{2,1,0:T(8,128)(2,1)}), bf16[4,64,128]{2,1,0:T(8,128)(2,1)S(1)}, u32[]{:S(2)}, u32[]{:S(2)}) async-start(bf16[4,64,128]{2,1,0:T(8,128)(2,1)} %copy.58), calls=%async_computation.3 | async-start | bytes 131072 | tf_op jit(solution)/shard_map/while/body/all_to_all | solution.py:28
  161.3 15.6 %all-to-all-done.3 = bf16[4,64,128]{2,1,0:T(8,128)(2,1)S(1)} async-done(((bf16[4,64,128]{2,1,0:T(8,128)(2,1)}), bf16[4,64,128]{2,1,0:T(8,128)(2,1)S(1)}, u32[]{:S(2)}, u32[]{:S(2)}) %all-to-all-start.3) | async-done | bytes 65568 | tf_op jit(solution)/shard_map/while/body/all_to_all | solution.py:28
  177.6 1.2 slice.65
  179.4 1.7 fusion.3
  181.2 39.3 %reduce-scatter.2.cloned.1.call-done = bf16[1,576,128]{2,1,0:T(8,128)(2,1)} async-done(((bf16[4,576,128]{2,1,0:T(8,128)(2,1)}), bf16[1,576,128]{2,1,0:T(8,128)(2,1)}) %reduce-scatter.2.cloned.1.call-update) | async-done | bytes 147472 | tf_op jit(solution)/shard_map/reduce_scatter | solution.py:117
  (50 shorter events, 11.0 us)
Async XLA Ops:
  7.2 3.7 %copy-start = (bf16[128,128]{1,0:T(8,128)(2,1)S(1)}, bf16[128,128]{1,0:T(8,128)(2,1)}, u32[]{:S(2)}) copy-start(bf16[128,128]{1,0:T(8,128)(2,1)} %param.11) | copy-start | bytes 98308
  7.2 91.0 %all-gather.3.cloned.1.call-start = ((), (), s32[]{:S(2)}) async-start(), calls=%async_computation.8 | async-start | bytes 1327104 | tf_op jit(solution)/shard_map/all_gather | solution.py:79
  8.8 211.7 %reduce-scatter.2.cloned.1.call-start = ((), (), s32[]{:S(2)}) async-start(), calls=%async_computation.7 | async-start | bytes 737280 | tf_op jit(solution)/shard_map/reduce_scatter | solution.py:117
  31.1 10.4 %collective-permute-start = (bf16[64,1024]{1,0:T(8,128)(2,1)S(1)}, bf16[64,1024]{1,0:T(8,128)(2,1)S(1)}, u32[]{:S(2)}, u32[]{:S(2)}) collective-permute-start(bf16[64,1024]{1,0:T(8,128)(2,1)S(1)} %reshape.89), channel_id=1, source_target_pairs={{0,0},{1,32},{2,64},{3,96},{4,128},{5,160},{6,192},{7,224},{32,1},... | collective-permute-start | bytes 393224 | tf_op jit(solution)/shard_map/while/body/ppermute | solution.py:33
  42.7 51.0 %all-to-all-start.1 = ((bf16[8,64,1024]{2,1,0:T(8,128)(2,1)}), bf16[8,64,1024]{2,1,0:T(8,128)(2,1)S(1)}, u32[]{:S(2)}, u32[]{:S(2)}) async-start(bf16[8,64,1024]{2,1,0:T(8,128)(2,1)} %broadcast_in_dim.63), calls=%async_computation.1 | async-start | bytes 2097152 | tf_op jit(solution)/shard_map/while/body/all_to_all | solution.py:24
  93.7 1.0 copy-start.1
  98.1 1.5 copy-start.2
  144.6 7.6 %collective-permute-start.1 = (bf16[64,512]{1,0:T(8,128)(2,1)S(1)}, bf16[64,512]{1,0:T(8,128)(2,1)S(1)}, u32[]{:S(2)}, u32[]{:S(2)}) collective-permute-start(bf16[64,512]{1,0:T(8,128)(2,1)S(1)} %reduce_sum.46), channel_id=1, source_target_pairs={{0,0},{1,32},{2,64},{3,96},{4,128},{5,160},{6,192},{7,224},{32,1},... | collective-permute-start | bytes 196616 | tf_op jit(solution)/shard_map/while/body/ppermute | solution.py:33
  152.8 24.1 %all-to-all-start.3 = ((bf16[4,64,128]{2,1,0:T(8,128)(2,1)}), bf16[4,64,128]{2,1,0:T(8,128)(2,1)S(1)}, u32[]{:S(2)}, u32[]{:S(2)}) async-start(bf16[4,64,128]{2,1,0:T(8,128)(2,1)} %copy.58), calls=%async_computation.3 | async-start | bytes 131072 | tf_op jit(solution)/shard_map/while/body/all_to_all | solution.py:28
  176.9 0.6 copy-start.3
Sparse Core Ops, SparseCore 0:
  10.7 87.3 all-gather.2
  132.6 87.8 reduce-scatter.1

commit v5 on v4

--- a/solution.py
+++ b/solution.py
@@ -5,12 +5,12 @@
 
 CAP = 64
 WINDOW = 4
-SHAPE = (4, 2, 4, 4, 4, 2)
-AXES = ("zp", "l", "x", "zh", "y", "c")
+SHAPE = (4, 2, 4, 4, 2, 2, 2)
+AXES = ("zp", "l", "x", "zh", "y_high", "y_low", "c")
 EXPERT = ("zp", "l", "x")
-FSDP = ("zh", "y", "c")
-PIECE = ("l", "x")
-GROUP = ("y", "c")
+FSDP = ("zh", "y_high", "y_low", "c")
+PIECE = ("x", "l")
+GROUP = ("y_low", "c", "y_high")
 
 
 def contract(left, right, left_dim, right_dim):
@@ -28,9 +28,11 @@
     return lax.all_to_all(blocks, axis, 0, 0)
 
 
-def swap(block):
-    pairs = [(piece * 8 + group, group * 8 + piece) for piece in range(8) for group in range(8)]
-    return lax.ppermute(block, PIECE + GROUP, pairs)
+def swap(block, flip=0):
+    pairs = [
+        (piece * 8 + group, (group ^ flip) * 8 + piece) for piece in range(8) for group in range(8)
+    ]
+    return lax.ppermute(block, ("l", "x", "y_high", "y_low", "c"), pairs)
 
 
 def select(probs, ids):
@@ -63,7 +65,10 @@
     both = exchange(both, "zp")
     feat = both.shape[2] // 2
     both = both.reshape(4, CAP, 2, feat).transpose(1, 2, 0, 3).reshape(CAP, 8 * feat)
-    return gather(swap(both), PIECE, 8).reshape(8 * CAP, 8 * feat)
+    same, other = swap(both), swap(both, 4)
+    low = lax.axis_index("l") == 0
+    both = jnp.stack([jnp.where(low, same, other), jnp.where(low, other, same)])
+    return gather(both, "x", 4).reshape(8 * CAP, 8 * feat)
 
 
 def grad_chain(row_grad):

time: 230 us -> 234 us (1.017)
  the two profiles are of different devices: /device:TPU:119 before, /device:TPU:155 now
where the time goes in v5:
time: 234 us
  waiting for transfers between devices  105 us (45%)
  blocking collectives  53.6 us (23%)
  starting transfers between devices  38.4 us (16%)
  between operations  15.5 us (7%)
  local copies, waits for them, and re-layouts  10.4 us (4%)
  other arithmetic  5.67 us (2%)
  matrix products  4.99 us (2%)
    reduce_scatter x1, waiting for transfers between devices, shards(): lax.psum_scatter(terms.reshape(3 * hid, 4, feat).transpose(1, 0, 2), 'zh')  53.5 us
    all_to_all x3, blocking collectives, exchange(): return lax.all_to_all(blocks, axis, 0, 0)  39.6 us
    all_gather x1, waiting for transfers between devices, shards(): weights = lax.all_gather(own, ('zh', 'c')).reshape(4, 2, 3 * hid, feat)  25.4 us
    all_to_all x1, starting transfers between devices, exchange(): return lax.all_to_all(blocks, axis, 0, 0)  15.3 us
    ppermute x3, starting transfers between devices, swap(): return lax.ppermute(block, ('l', 'x', 'y_high', 'y_low', 'c'), pairs)  15.3 us
    all_to_all x1, blocking collectives, gather(): return lax.all_to_all(copies, axis, 0, 0)  14 us
    all_to_all x1, waiting for transfers between devices, gather(): return lax.all_to_all(copies, axis, 0, 0)  12.7 us
    ppermute x3, waiting for transfers between devices, swap(): return lax.ppermute(block, ('l', 'x', 'y_high', 'y_low', 'c'), pairs)  9.25 us
  transfers between devices with their start and end apart: 7, of which 7 were waited for; matrix products, arithmetic and copies ran while one was open for 5% of the time, Pallas kernels for 0%

profile of v5, /device:TPU:155, one launch (start us, length us, event | category | flops | bytes accessed | tf_op | source)
XLA Modules:
  0.0 233.6 jit_solution(7861600794245045720)
XLA Ops:
  7.2 1.5 pad_maximum_fusion.2
  13.3 51.0 %while.22 = (s32[]{:T(128)}, bf16[512,1024]{1,0:T(8,128)(2,1)}, s32[]{:T(128)}, bf16[4,64,256]{2,1,0:T(8,128)(2,1)S(1)}, s32[]{:T(128)}, /*index=5*/u32[]{:T(128)}, u32[]{:T(128)}, s32[]{:T(128)}) while((s32[]{:T(128)}, bf16[512,1024]{1,0:T(8,128)(2,1)}, s32[]{:T(128)}, bf16[4,64,256]{2,1,0:T(8,128)(2,1)S(1)}, s32[]{:T(128)}, ...), condition=%wide.region_4.5_spmd, body=%wide.region_3.4_spmd.sunk | while | flops 327687 | bytes 12058899 | solution.py:57
  13.3 13.2 %all_to_all.42 = bf16[4,64,256]{2,1,0:T(8,128)(2,1)S(1)} all-to-all(bf16[4,64,256]{2,1,0:T(8,128)(2,1)S(1)} %broadcast_add_fusion.5), channel_id=1, replica_groups=mesh['zp'=4,'l'=2,'x'=4,'zh'=4,'y_high'=2,'y_low'=2,'c'=2] {'zp'}, dimensions={0} | all-to-all | bytes 262144 | tf_op jit(solution)/shard_map/while/body/all_to_all | solution.py:28
  26.8 5.8 %collective-permute-start = (bf16[64,1024]{1,0:T(8,128)(2,1)S(1)}, bf16[64,1024]{1,0:T(8,128)(2,1)S(1)}, u32[]{:S(2)}, u32[]{:S(2)}) collective-permute-start(bf16[64,1024]{1,0:T(8,128)(2,1)S(1)} %reshape.89), channel_id=1, source_target_pairs={{0,0},{1,32},{2,64},{3,96},{4,128},{5,160},{6,192},{7,224},{32,1},... | collective-permute-start | bytes 393224 | tf_op jit(solution)/shard_map/while/body/ppermute | solution.py:35
  32.7 1.9 collective-permute-start.1
  34.6 3.8 %collective-permute-done = bf16[64,1024]{1,0:T(8,128)(2,1)S(1)} collective-permute-done((bf16[64,1024]{1,0:T(8,128)(2,1)S(1)}, bf16[64,1024]{1,0:T(8,128)(2,1)S(1)}, u32[]{:S(2)}, u32[]{:S(2)}) %collective-permute-start) | collective-permute-done | bytes 131104 | tf_op jit(solution)/shard_map/while/body/ppermute | solution.py:35
  38.4 3.3 %collective-permute-done.1 = bf16[64,1024]{1,0:T(8,128)(2,1)S(1)} collective-permute-done((bf16[64,1024]{1,0:T(8,128)(2,1)S(1)}, bf16[64,1024]{1,0:T(8,128)(2,1)S(1)}, u32[]{:S(2)}, u32[]{:S(2)}) %collective-permute-start.1) | collective-permute-done | bytes 131104 | tf_op jit(solution)/shard_map/while/body/ppermute | solution.py:35
  41.8 1.1 broadcast_in_dim.63
  42.9 7.7 %all-to-all-start.1 = ((bf16[4,2,64,1024]{3,2,1,0:T(8,128)(2,1)}), bf16[4,2,64,1024]{3,2,1,0:T(8,128)(2,1)S(1)}, u32[]{:S(2)}, u32[]{:S(2)}) async-start(bf16[4,2,64,1024]{3,2,1,0:T(8,128)(2,1)} %broadcast_in_dim.63), calls=%async_computation.1 | async-start | bytes 2097152 | tf_op jit(solution)/shard_map/while/body/all_to_all | solution.py:24
  50.6 12.7 %all-to-all-done.1 = bf16[4,2,64,1024]{3,2,1,0:T(8,128)(2,1)S(1)} async-done(((bf16[4,2,64,1024]{3,2,1,0:T(8,128)(2,1)}), bf16[4,2,64,1024]{3,2,1,0:T(8,128)(2,1)S(1)}, u32[]{:S(2)}, u32[]{:S(2)}) %all-to-all-start.1) | async-done | bytes 1048608 | tf_op jit(solution)/shard_map/while/body/all_to_all | solution.py:24
  64.3 1.2 slice.56
  66.1 25.4 %all-gather.3.cloned.1.call-done = bf16[4608,128]{1,0:T(8,128)(2,1)} async-done(((bf16[576,128]{1,0:T(8,128)(2,1)}), bf16[4608,128]{1,0:T(8,128)(2,1)}) %all-gather.3.cloned.1.call-update) | async-done | bytes 1179664 | tf_op jit(solution)/shard_map/all_gather | solution.py:84
  91.6 1.3 dynamic-slice_bitcast_fusion.3
  94.1 14.7 %all_to_all.40 = bf16[8,64,576]{2,1,0:T(8,128)(2,1)S(1)} all-to-all(bf16[8,64,576]{2,1,0:T(8,128)(2,1)S(1)} %pad_maximum_fusion.1), channel_id=1, replica_groups=mesh['zp'=4,'l'=2,'x'=4,'zh'=4,'y_high'=2,'y_low'=2,'c'=2] {'y_low','c',..., dimensions={0} | all-to-all | bytes 1179648 | tf_op jit(solution)/shard_map/all_to_all | solution.py:28
  109.1 14.0 %all_to_all.41 = bf16[8,64,576]{2,1,0:T(8,128)(2,1)S(1)} all-to-all(bf16[8,64,576]{2,1,0:T(8,128)(2,1)S(1)} %broadcast_in_dim.57), channel_id=1, replica_groups=mesh['zp'=4,'l'=2,'x'=4,'zh'=4,'y_high'=2,'y_low'=2,'c'=2] {'y_low','c',..., dimensions={0} | all-to-all | bytes 1179648 | tf_op jit(solution)/shard_map/all_to_all | solution.py:24
  125.9 42.2 %while.23 = (s32[]{:T(128)}, bf16[4,64,128]{2,1,0:T(8,128)(2,1)}, s32[]{:T(128)}, bf16[8,64,512]{2,1,0:T(8,128)(2,1)S(1)}, s32[]{:T(128)}, /*index=5*/bf16[]{:T(256)}) while((s32[]{:T(128)}, bf16[4,64,128]{2,1,0:T(8,128)(2,1)}, s32[]{:T(128)}, bf16[8,64,512]{2,1,0:T(8,128)(2,1)S(1)}, s32[]{:T(128)}, /*index=5*/bf16[]{:T(256)}) %tuple.64), condition=%wide.region_8.9_spmd, body=%wide.region_6.8_spmd.sunk | while | flops 491523 | bytes 3670195 | solution.py:57
  125.9 11.8 %all_to_all.43 = bf16[8,64,512]{2,1,0:T(8,128)(2,1)S(1)} all-to-all(bf16[8,64,512]{2,1,0:T(8,128)(2,1)S(1)} %broadcast_add_fusion.6), channel_id=1, replica_groups=mesh['zp'=4,'l'=2,'x'=4,'zh'=4,'y_high'=2,'y_low'=2,'c'=2] {'x','l'}, dimensions={0} | all-to-all | bytes 1048576 | tf_op jit(solution)/shard_map/while/body/all_to_all | solution.py:28
  137.8 7.5 %collective-permute-start.2 = (bf16[64,512]{1,0:T(8,128)(2,1)S(1)}, bf16[64,512]{1,0:T(8,128)(2,1)S(1)}, u32[]{:S(2)}, u32[]{:S(2)}) collective-permute-start(bf16[64,512]{1,0:T(8,128)(2,1)S(1)} %reduce_sum.46), channel_id=1, source_target_pairs={{0,0},{1,32},{2,64},{3,96},{4,128},{5,160},{6,192},{7,224},{32,1},... | collective-permute-start | bytes 196616 | tf_op jit(solution)/shard_map/while/body/ppermute | solution.py:35
  145.3 2.2 collective-permute-done.2
  148.1 15.3 %all-to-all-start.3 = ((bf16[4,64,128]{2,1,0:T(8,128)(2,1)}), bf16[4,64,128]{2,1,0:T(8,128)(2,1)S(1)}, u32[]{:S(2)}, u32[]{:S(2)}) async-start(bf16[4,64,128]{2,1,0:T(8,128)(2,1)} %copy.58), calls=%async_computation.3 | async-start | bytes 131072 | tf_op jit(solution)/shard_map/while/body/all_to_all | solution.py:28
  163.4 4.0 %all-to-all-done.3 = bf16[4,64,128]{2,1,0:T(8,128)(2,1)S(1)} async-done(((bf16[4,64,128]{2,1,0:T(8,128)(2,1)}), bf16[4,64,128]{2,1,0:T(8,128)(2,1)S(1)}, u32[]{:S(2)}, u32[]{:S(2)}) %all-to-all-start.3) | async-done | bytes 65568 | tf_op jit(solution)/shard_map/while/body/all_to_all | solution.py:28
  168.1 1.2 slice.65
  169.9 1.7 fusion.3
  171.7 53.5 %reduce-scatter.2.cloned.1.call-done = bf16[1,576,128]{2,1,0:T(8,128)(2,1)} async-done(((bf16[4,576,128]{2,1,0:T(8,128)(2,1)}), bf16[1,576,128]{2,1,0:T(8,128)(2,1)}) %reduce-scatter.2.cloned.1.call-update) | async-done | bytes 147472 | tf_op jit(solution)/shard_map/reduce_scatter | solution.py:122
  (54 shorter events, 13.2 us)
Async XLA Ops:
  7.2 3.7 %copy-start = (bf16[128,128]{1,0:T(8,128)(2,1)S(1)}, bf16[128,128]{1,0:T(8,128)(2,1)}, u32[]{:S(2)}) copy-start(bf16[128,128]{1,0:T(8,128)(2,1)} %param.11) | copy-start | bytes 98308
  7.2 84.4 %all-gather.3.cloned.1.call-start = ((), (), s32[]{:S(2)}) async-start(), calls=%async_computation.8 | async-start | bytes 1327104 | tf_op jit(solution)/shard_map/all_gather | solution.py:84
  8.8 216.4 %reduce-scatter.2.cloned.1.call-start = ((), (), s32[]{:S(2)}) async-start(), calls=%async_computation.7 | async-start | bytes 737280 | tf_op jit(solution)/shard_map/reduce_scatter | solution.py:122
  26.8 11.6 %collective-permute-start = (bf16[64,1024]{1,0:T(8,128)(2,1)S(1)}, bf16[64,1024]{1,0:T(8,128)(2,1)S(1)}, u32[]{:S(2)}, u32[]{:S(2)}) collective-permute-start(bf16[64,1024]{1,0:T(8,128)(2,1)S(1)} %reshape.89), channel_id=1, source_target_pairs={{0,0},{1,32},{2,64},{3,96},{4,128},{5,160},{6,192},{7,224},{32,1},... | collective-permute-start | bytes 393224 | tf_op jit(solution)/shard_map/while/body/ppermute | solution.py:35
  32.7 9.0 %collective-permute-start.1 = (bf16[64,1024]{1,0:T(8,128)(2,1)S(1)}, bf16[64,1024]{1,0:T(8,128)(2,1)S(1)}, u32[]{:S(2)}, u32[]{:S(2)}) collective-permute-start(bf16[64,1024]{1,0:T(8,128)(2,1)S(1)} %reshape.89), channel_id=1, source_target_pairs={{0,128},{1,160},{2,192},{3,224},{4,0},{5,32},{6,64},{7,96},{32,129... | collective-permute-start | bytes 393224 | tf_op jit(solution)/shard_map/while/body/ppermute | solution.py:35
  42.9 20.4 %all-to-all-start.1 = ((bf16[4,2,64,1024]{3,2,1,0:T(8,128)(2,1)}), bf16[4,2,64,1024]{3,2,1,0:T(8,128)(2,1)S(1)}, u32[]{:S(2)}, u32[]{:S(2)}) async-start(bf16[4,2,64,1024]{3,2,1,0:T(8,128)(2,1)} %broadcast_in_dim.63), calls=%async_computation.1 | async-start | bytes 2097152 | tf_op jit(solution)/shard_map/while/body/all_to_all | solution.py:24
  63.3 1.0 copy-start.1
  91.6 1.5 copy-start.2
  137.8 9.7 %collective-permute-start.2 = (bf16[64,512]{1,0:T(8,128)(2,1)S(1)}, bf16[64,512]{1,0:T(8,128)(2,1)S(1)}, u32[]{:S(2)}, u32[]{:S(2)}) collective-permute-start(bf16[64,512]{1,0:T(8,128)(2,1)S(1)} %reduce_sum.46), channel_id=1, source_target_pairs={{0,0},{1,32},{2,64},{3,96},{4,128},{5,160},{6,192},{7,224},{32,1},... | collective-permute-start | bytes 196616 | tf_op jit(solution)/shard_map/while/body/ppermute | solution.py:35
  148.1 19.3 %all-to-all-start.3 = ((bf16[4,64,128]{2,1,0:T(8,128)(2,1)}), bf16[4,64,128]{2,1,0:T(8,128)(2,1)S(1)}, u32[]{:S(2)}, u32[]{:S(2)}) async-start(bf16[4,64,128]{2,1,0:T(8,128)(2,1)} %copy.58), calls=%async_computation.3 | async-start | bytes 131072 | tf_op jit(solution)/shard_map/while/body/all_to_all | solution.py:28
  167.5 0.6 copy-start.3
Sparse Core Ops, SparseCore 0:
  10.7 80.7 all-gather.2
  125.4 99.7 reduce-scatter.1

commit v6 on v5

--- a/solution.py
+++ b/solution.py
@@ -28,9 +28,11 @@
     return lax.all_to_all(blocks, axis, 0, 0)
 
 
-def swap(block, flip=0):
+def swap(block, piece_flip=0, group_flip=0):
     pairs = [
-        (piece * 8 + group, (group ^ flip) * 8 + piece) for piece in range(8) for group in range(8)
+        (piece * 8 + group, (group ^ piece_flip) * 8 + (piece ^ group_flip))
+        for piece in range(8)
+        for group in range(8)
     ]
     return lax.ppermute(block, ("l", "x", "y_high", "y_low", "c"), pairs)
 
@@ -61,38 +63,46 @@
     )[2]
 
 
+def ordered(same, other):
+    low = lax.axis_index("l") == 0
+    return jnp.where(low, same, other), jnp.where(low, other, same)
+
+
 def token_chain(both):
     both = exchange(both, "zp")
     feat = both.shape[2] // 2
     both = both.reshape(4, CAP, 2, feat).transpose(1, 2, 0, 3).reshape(CAP, 8 * feat)
-    same, other = swap(both), swap(both, 4)
-    low = lax.axis_index("l") == 0
-    both = jnp.stack([jnp.where(low, same, other), jnp.where(low, other, same)])
+    both = jnp.stack(ordered(swap(both), swap(both, piece_flip=4)))
     return gather(both, "x", 4).reshape(8 * CAP, 8 * feat)
 
 
 def grad_chain(row_grad):
-    feat = row_grad.shape[2] // 4
-    row_grad = exchange(row_grad, PIECE).astype(jnp.float32)
-    row_grad = swap(jnp.sum(row_grad, axis=0).astype(jnp.bfloat16))
+    feat = row_grad.shape[3] // 4
+    row_grad = jnp.sum(exchange(row_grad, "x").astype(jnp.float32), axis=0).astype(jnp.bfloat16)
+    same, other = ordered(row_grad[0], row_grad[1])
+    same, other = swap(same), swap(other, group_flip=4)
+    row_grad = (same.astype(jnp.float32) + other.astype(jnp.float32)).astype(jnp.bfloat16)
     return exchange(row_grad.reshape(CAP, 4, feat).transpose(1, 0, 2), "zp")
+
+
+def shift(block, d):
+    return lax.ppermute(block, "zh", [(j, (j + d) % 4) for j in range(4)])
 
 
 def shards(tokens, out_grad, route_probs, expert_ids, gate_weight, up_weight, down_weight):
     hid, feat = down_weight.shape
     own = jnp.concatenate([gate_weight.T, up_weight.T, down_weight], axis=0)
-    weights = lax.all_gather(own, ("zh", "c")).reshape(4, 2, 3 * hid, feat)
+    weights = lax.all_gather(own, "zh")
+    weights = jnp.concatenate(list(weights), axis=1)
+    gate_up, down = weights[: 2 * hid], weights[2 * hid :]
 
     picker, row_weight = select(route_probs, expert_ids)
     picked = jnp.dot(picker, tokens, preferred_element_type=jnp.float32).astype(jnp.bfloat16)
     cot_rows = jnp.dot(picker, out_grad, preferred_element_type=jnp.float32)
     carried = (row_weight[:, None] * cot_rows).astype(jnp.bfloat16)
     both = jnp.concatenate([picked, carried], axis=1).reshape(WINDOW, CAP, 2 * feat)
-    both = once(token_chain, both, (8 * CAP, 8 * feat))
+    both = token_chain(both)
     rows, carried = both[:, : 4 * feat], both[:, 4 * feat :]
-    weights = lax.dynamic_index_in_dim(weights, lax.axis_index("c"), 1, False)
-    weights = jnp.concatenate(list(weights), axis=1) + both[:1, :1] * 0
-    gate_up, down = weights[: 2 * hid], weights[2 * hid :]
 
     parts = jnp.concatenate(
         [contract(rows, gate_up, 1, 1), contract(carried, down, 1, 1)], axis=1
@@ -119,10 +129,17 @@
     terms = jnp.concatenate(
         [contract(row_grads, rows, 0, 0), contract(hidden, carried, 0, 0)], axis=0
     ).astype(jnp.bfloat16)
-    summed = lax.psum_scatter(terms.reshape(3 * hid, 4, feat).transpose(1, 0, 2), "zh")
-    row_grad = contract(row_grads, gate_up, 1, 0).astype(jnp.bfloat16).reshape(8, CAP, 4 * feat)
+    terms = terms.reshape(3 * hid, 4, feat).transpose(1, 0, 2)
+    here = lax.axis_index("zh")
+    parts = [lax.dynamic_index_in_dim(terms, (here + d) % 4, 0, False) for d in range(4)]
+    moved = [shift(parts[d], d) for d in (1, 2, 3)]
+    row_grad = contract(row_grads, gate_up, 1, 0).astype(jnp.bfloat16)
+    row_grad = row_grad.reshape(4, 2, CAP, 4 * feat)
     row_grad = once(grad_chain, row_grad, (WINDOW, CAP, feat))
-    summed = summed + row_grad[0, :1, :1] * 0
+    summed = parts[0].astype(jnp.float32) + row_grad[0, :1, :1].astype(jnp.float32) * 0
+    for part in moved:
+        summed = summed + part.astype(jnp.float32)
+    summed = summed.astype(jnp.bfloat16)
     gate_grad, up_grad = summed[:hid].T, summed[hid : 2 * hid].T
     down_grad = summed[2 * hid :]
 

time: 234 us -> 241 us (1.030)
  the two profiles are of different devices: /device:TPU:155 before, /device:TPU:24 now
where the time goes in v6:
time: 241 us; the launch traced here: 240 us
  blocking collectives  101 us (42%)
  starting transfers between devices  77.2 us (32%)
  waiting for transfers between devices  45.9 us (19%)
  local copies, waits for them, and re-layouts  6.66 us (3%)
  matrix products  4.96 us (2%)
  other arithmetic  3.26 us (1%)
    all_gather x1, blocking collectives, shards(): weights = lax.all_gather(own, 'zh')  56.9 us
    all_to_all x2, blocking collectives, exchange(): return lax.all_to_all(blocks, axis, 0, 0)  43.7 us
    ppermute x3, starting transfers between devices, shift(): return lax.ppermute(block, 'zh', [(j, (j + d) % 4) for j in range(4)])  26.6 us
    all_to_all x2, starting transfers between devices, exchange(): return lax.all_to_all(blocks, axis, 0, 0)  23.8 us
    ppermute x4, waiting for transfers between devices, swap(): return lax.ppermute(block, ('l', 'x', 'y_high', 'y_low', 'c'), pairs)  18.7 us
    all_to_all x2, waiting for transfers between devices, exchange(): return lax.all_to_all(blocks, axis, 0, 0)  18.2 us
    ppermute x4, starting transfers between devices, swap(): return lax.ppermute(block, ('l', 'x', 'y_high', 'y_low', 'c'), pairs)  17.9 us
    all_to_all x2, waiting for transfers between devices, gather(): return lax.all_to_all(copies, axis, 0, 0)  9.1 us
  transfers between devices with their start and end apart: 11, of which 7 were waited for; matrix products, arithmetic and copies ran while one was open for 2% of the time, Pallas kernels for 0%

profile of v6, /device:TPU:24, one launch (start us, length us, event | category | flops | bytes accessed | tf_op | source)
XLA Modules:
  0.0 240.2 jit_solution(12786379132277524277)
XLA Ops:
  4.0 23.1 %all_to_all.38 = bf16[4,64,256]{2,1,0:T(8,128)(2,1)S(1)} all-to-all(bf16[4,64,256]{2,1,0:T(8,128)(2,1)S(1)} %bitcast.77), channel_id=1, replica_groups=mesh['zp'=4,'l'=2,'x'=4,'zh'=4,'y_high'=2,'y_low'=2,'c'=2] {'zp'}, dimensions={0} | all-to-all | bytes 262144 | tf_op jit(solution)/shard_map/all_to_all | solution.py:28
  27.5 3.9 %collective-permute-start.2 = (bf16[64,1024]{1,0:T(8,128)(2,1)S(1)}, bf16[64,1024]{1,0:T(8,128)(2,1)S(1)}, u32[]{:S(2)}, u32[]{:S(2)}) collective-permute-start(bf16[64,1024]{1,0:T(8,128)(2,1)S(1)} %reshape.80), channel_id=1, source_target_pairs={{0,0},{1,32},{2,64},{3,96},{4,128},{5,160},{6,192},{7,224},{32,1},... | collective-permute-start | bytes 393224 | tf_op jit(solution)/shard_map/ppermute | solution.py:37
  31.4 4.1 %collective-permute-start.3 = (bf16[64,1024]{1,0:T(8,128)(2,1)S(1)}, bf16[64,1024]{1,0:T(8,128)(2,1)S(1)}, u32[]{:S(2)}, u32[]{:S(2)}) collective-permute-start(bf16[64,1024]{1,0:T(8,128)(2,1)S(1)} %reshape.80), channel_id=1, source_target_pairs={{0,128},{1,160},{2,192},{3,224},{4,0},{5,32},{6,64},{7,96},{32,129... | collective-permute-start | bytes 393224 | tf_op jit(solution)/shard_map/ppermute | solution.py:37
  35.5 4.2 %collective-permute-done.2 = bf16[64,1024]{1,0:T(8,128)(2,1)S(1)} collective-permute-done((bf16[64,1024]{1,0:T(8,128)(2,1)S(1)}, bf16[64,1024]{1,0:T(8,128)(2,1)S(1)}, u32[]{:S(2)}, u32[]{:S(2)}) %collective-permute-start.2) | collective-permute-done | bytes 131104 | tf_op jit(solution)/shard_map/ppermute | solution.py:37
  39.7 3.4 %collective-permute-done.3 = bf16[64,1024]{1,0:T(8,128)(2,1)S(1)} collective-permute-done((bf16[64,1024]{1,0:T(8,128)(2,1)S(1)}, bf16[64,1024]{1,0:T(8,128)(2,1)S(1)}, u32[]{:S(2)}, u32[]{:S(2)}) %collective-permute-start.3) | collective-permute-done | bytes 131104 | tf_op jit(solution)/shard_map/ppermute | solution.py:37
  44.3 3.6 %all-to-all-start.3 = ((bf16[4,2,64,1024]{3,2,1,0:T(8,128)(2,1)}), bf16[4,2,64,1024]{3,2,1,0:T(8,128)(2,1)S(1)}, u32[]{:S(2)}, u32[]{:S(2)}) async-start(bf16[4,2,64,1024]{3,2,1,0:T(8,128)(2,1)} %broadcast_in_dim.53), calls=%async_computation.3 | async-start | bytes 2097152 | tf_op jit(solution)/shard_map/all_to_all | solution.py:24
  48.0 56.9 %all-gather = bf16[2304,128]{1,0:T(8,128)(2,1)S(1)} all-gather(bf16[576,128]{1,0:T(8,128)(2,1)S(1)} %pad_maximum_fusion.3), channel_id=2, replica_groups=mesh['zp'=4,'l'=2,'x'=4,'zh'=4,'y_high'=2,'y_low'=2,'c'=2] {'zh'}, dimensions={0}, use_global_device_ids=true | all-gather | bytes 737280 | tf_op jit(solution)/shard_map/all_gather | solution.py:95
  106.0 20.6 %all_to_all.39 = bf16[8,64,576]{2,1,0:T(8,128)(2,1)S(1)} all-to-all(bf16[8,64,576]{2,1,0:T(8,128)(2,1)S(1)} %pad_maximum_fusion), channel_id=1, replica_groups=mesh['zp'=4,'l'=2,'x'=4,'zh'=4,'y_high'=2,'y_low'=2,'c'=2] {'y_low','c',..., dimensions={0} | all-to-all | bytes 1179648 | tf_op jit(solution)/shard_map/all_to_all | solution.py:28
  127.8 5.1 %all-to-all-start.5 = ((bf16[8,64,576]{2,1,0:T(8,128)(2,1)}), bf16[8,64,576]{2,1,0:T(8,128)(2,1)S(1)}, u32[]{:S(2)}, u32[]{:S(2)}) async-start(bf16[8,64,576]{2,1,0:T(8,128)(2,1)} %broadcast_in_dim.54), calls=%async_computation.5 | async-start | bytes 1310720 | tf_op jit(solution)/shard_map/all_to_all | solution.py:24
  132.9 9.1 %all-to-all-done.5 = bf16[8,64,576]{2,1,0:T(8,128)(2,1)S(1)} async-done(((bf16[8,64,576]{2,1,0:T(8,128)(2,1)}), bf16[8,64,576]{2,1,0:T(8,128)(2,1)S(1)}, u32[]{:S(2)}, u32[]{:S(2)}) %all-to-all-start.5) | async-done | bytes 589856 | tf_op jit(solution)/shard_map/all_to_all | solution.py:24
  143.3 4.9 %collective-permute-start.4 = (bf16[576,128]{1,0:T(8,128)(2,1)S(1)}, bf16[576,128]{1,0:T(8,128)(2,1)S(1)}, u32[]{:S(2)}, u32[]{:S(2)}) collective-permute-start(bf16[576,128]{1,0:T(8,128)(2,1)S(1)} %get-tuple-element.67), channel_id=1, source_target_pairs={{0,8},{8,16},{16,24},{24,0},{1,9},{9,17},{17,25},{25,1},{2,10},{10... | collective-permute-start | bytes 442376 | tf_op jit(solution)/shard_map/ppermute | solution.py:89
  148.2 11.8 %collective-permute-start.5 = (bf16[576,128]{1,0:T(8,128)(2,1)S(1)}, bf16[576,128]{1,0:T(8,128)(2,1)S(1)}, u32[]{:S(2)}, u32[]{:S(2)}) collective-permute-start(bf16[576,128]{1,0:T(8,128)(2,1)S(1)} %get-tuple-element.69), channel_id=1, source_target_pairs={{0,16},{8,24},{16,0},{24,8},{1,17},{9,25},{17,1},{25,9},{2,18},{10... | collective-permute-start | bytes 442376 | tf_op jit(solution)/shard_map/ppermute | solution.py:89
  160.0 10.0 %collective-permute-start.6 = (bf16[576,128]{1,0:T(8,128)(2,1)S(1)}, bf16[576,128]{1,0:T(8,128)(2,1)S(1)}, u32[]{:S(2)}, u32[]{:S(2)}) collective-permute-start(bf16[576,128]{1,0:T(8,128)(2,1)S(1)} %get-tuple-element.68), channel_id=1, source_target_pairs={{0,24},{8,0},{16,8},{24,16},{1,25},{9,1},{17,9},{25,17},{2,26},{10... | collective-permute-start | bytes 442376 | tf_op jit(solution)/shard_map/ppermute | solution.py:89
  170.6 65.2 %while.12 = (s32[]{:T(128)}, bf16[4,64,128]{2,1,0:T(8,128)(2,1)}, s32[]{:T(128)}, bf16[4,2,64,512]{3,2,1,0:T(8,128)(2,1)S(1)}, s32[]{:T(128)}, /*index=5*/u32[]{:T(128)}, u32[]{:T(128)}, s32[]{:T(128)}, bf16[]{:T(256)}) while((s32[]{:T(128)}, bf16[4,64,128]{2,1,0:T(8,128)(2,1)}, s32[]{:T(128)}, bf16[4,2,64,512]{3,2,1,0:T(8,128)(2,1)S(1)}, ...), condition=%wide.region_6.7_spmd, body=%wide.region_4.6_spmd.sunk | while | flops 655367 | bytes 4981053 | solution.py:59
  171.5 3.6 %all-to-all-start = ((bf16[4,2,64,512]{3,2,1,0:T(8,128)(2,1)}), bf16[4,2,64,512]{3,2,1,0:T(8,128)(2,1)S(1)}, u32[]{:S(2)}, u32[]{:S(2)}) async-start(bf16[4,2,64,512]{3,2,1,0:T(8,128)(2,1)} %broadcast_add_fusion.2), calls=%async_computation | async-start | bytes 1048576 | tf_op jit(solution)/shard_map/while/body/all_to_all | solution.py:28
  175.1 8.5 %all-to-all-done = bf16[4,2,64,512]{3,2,1,0:T(8,128)(2,1)S(1)} async-done(((bf16[4,2,64,512]{3,2,1,0:T(8,128)(2,1)}), bf16[4,2,64,512]{3,2,1,0:T(8,128)(2,1)S(1)}, u32[]{:S(2)}, u32[]{:S(2)}) %all-to-all-start) | async-done | bytes 524320 | tf_op jit(solution)/shard_map/while/body/all_to_all | solution.py:28
  183.7 1.9 collective-permute-start
  185.7 8.0 %collective-permute-start.1 = (bf16[64,512]{1,0:T(8,128)(2,1)S(1)}, bf16[64,512]{1,0:T(8,128)(2,1)S(1)}, u32[]{:S(2)}, u32[]{:S(2)}) collective-permute-start(bf16[64,512]{1,0:T(8,128)(2,1)S(1)} %get-tuple-element.109), channel_id=1, source_target_pairs={{0,0},{1,32},{2,64},{3,96},{4,128},{5,160},{6,192},{7,224},{32,1},... | collective-permute-start | bytes 196616 | tf_op jit(solution)/shard_map/while/body/ppermute | solution.py:37
  193.6 4.8 %collective-permute-done = bf16[64,512]{1,0:T(8,128)(2,1)S(1)} collective-permute-done((bf16[64,512]{1,0:T(8,128)(2,1)S(1)}, bf16[64,512]{1,0:T(8,128)(2,1)S(1)}, u32[]{:S(2)}, u32[]{:S(2)}) %collective-permute-start) | collective-permute-done | bytes 65568 | tf_op jit(solution)/shard_map/while/body/ppermute | solution.py:37
  198.4 6.3 %collective-permute-done.1 = bf16[64,512]{1,0:T(8,128)(2,1)S(1)} collective-permute-done((bf16[64,512]{1,0:T(8,128)(2,1)S(1)}, bf16[64,512]{1,0:T(8,128)(2,1)S(1)}, u32[]{:S(2)}, u32[]{:S(2)}) %collective-permute-start.1) | collective-permute-done | bytes 65568 | tf_op jit(solution)/shard_map/while/body/ppermute | solution.py:37
  205.4 20.2 %all-to-all-start.1 = ((bf16[4,64,128]{2,1,0:T(8,128)(2,1)}), bf16[4,64,128]{2,1,0:T(8,128)(2,1)S(1)}, u32[]{:S(2)}, u32[]{:S(2)}) async-start(bf16[4,64,128]{2,1,0:T(8,128)(2,1)} %copy.53), calls=%async_computation.1 | async-start | bytes 131072 | tf_op jit(solution)/shard_map/while/body/all_to_all | solution.py:28
  225.5 9.7 %all-to-all-done.1 = bf16[4,64,128]{2,1,0:T(8,128)(2,1)S(1)} async-done(((bf16[4,64,128]{2,1,0:T(8,128)(2,1)}), bf16[4,64,128]{2,1,0:T(8,128)(2,1)S(1)}, u32[]{:S(2)}, u32[]{:S(2)}) %all-to-all-start.1) | async-done | bytes 65568 | tf_op jit(solution)/shard_map/while/body/all_to_all | solution.py:28
  235.8 1.2 slice.60
  237.7 1.7 fusion.3
  (59 shorter events, 12.0 us)
Async XLA Ops:
  0.6 2.1 copy-start
  27.5 12.2 %collective-permute-start.2 = (bf16[64,1024]{1,0:T(8,128)(2,1)S(1)}, bf16[64,1024]{1,0:T(8,128)(2,1)S(1)}, u32[]{:S(2)}, u32[]{:S(2)}) collective-permute-start(bf16[64,1024]{1,0:T(8,128)(2,1)S(1)} %reshape.80), channel_id=1, source_target_pairs={{0,0},{1,32},{2,64},{3,96},{4,128},{5,160},{6,192},{7,224},{32,1},... | collective-permute-start | bytes 393224 | tf_op jit(solution)/shard_map/ppermute | solution.py:37
  31.4 11.7 %collective-permute-start.3 = (bf16[64,1024]{1,0:T(8,128)(2,1)S(1)}, bf16[64,1024]{1,0:T(8,128)(2,1)S(1)}, u32[]{:S(2)}, u32[]{:S(2)}) collective-permute-start(bf16[64,1024]{1,0:T(8,128)(2,1)S(1)} %reshape.80), channel_id=1, source_target_pairs={{0,128},{1,160},{2,192},{3,224},{4,0},{5,32},{6,64},{7,96},{32,129... | collective-permute-start | bytes 393224 | tf_op jit(solution)/shard_map/ppermute | solution.py:37
  44.3 3.7 %copy-start.2 = (bf16[192,128]{1,0:T(8,128)(2,1)S(1)}, bf16[192,128]{1,0:T(8,128)(2,1)}, u32[]{:S(2)}) copy-start(bf16[192,128]{1,0:T(8,128)(2,1)} %param.15) | copy-start | bytes 147460
  44.3 3.7 %copy-start.3 = (bf16[128,192]{0,1:T(8,128)(2,1)S(1)}, bf16[128,192]{0,1:T(8,128)(2,1)}, u32[]{:S(2)}) copy-start(bf16[128,192]{0,1:T(8,128)(2,1)} %param.14) | copy-start | bytes 147460
  44.3 3.7 %copy-start.4 = (bf16[128,192]{0,1:T(8,128)(2,1)S(1)}, bf16[128,192]{0,1:T(8,128)(2,1)}, u32[]{:S(2)}) copy-start(bf16[128,192]{0,1:T(8,128)(2,1)} %param.13) | copy-start | bytes 147460
  44.3 60.7 %all-to-all-start.3 = ((bf16[4,2,64,1024]{3,2,1,0:T(8,128)(2,1)}), bf16[4,2,64,1024]{3,2,1,0:T(8,128)(2,1)S(1)}, u32[]{:S(2)}, u32[]{:S(2)}) async-start(bf16[4,2,64,1024]{3,2,1,0:T(8,128)(2,1)} %broadcast_in_dim.53), calls=%async_computation.3 | async-start | bytes 2097152 | tf_op jit(solution)/shard_map/all_to_all | solution.py:24
  127.8 14.2 %all-to-all-start.5 = ((bf16[8,64,576]{2,1,0:T(8,128)(2,1)}), bf16[8,64,576]{2,1,0:T(8,128)(2,1)S(1)}, u32[]{:S(2)}, u32[]{:S(2)}) async-start(bf16[8,64,576]{2,1,0:T(8,128)(2,1)} %broadcast_in_dim.54), calls=%async_computation.5 | async-start | bytes 1310720 | tf_op jit(solution)/shard_map/all_to_all | solution.py:24
  143.3 96.1 %collective-permute-start.4 = (bf16[576,128]{1,0:T(8,128)(2,1)S(1)}, bf16[576,128]{1,0:T(8,128)(2,1)S(1)}, u32[]{:S(2)}, u32[]{:S(2)}) collective-permute-start(bf16[576,128]{1,0:T(8,128)(2,1)S(1)} %get-tuple-element.67), channel_id=1, source_target_pairs={{0,8},{8,16},{16,24},{24,0},{1,9},{9,17},{17,25},{25,1},{2,10},{10... | collective-permute-start | bytes 442376 | tf_op jit(solution)/shard_map/ppermute | solution.py:89
  148.2 91.2 %collective-permute-start.5 = (bf16[576,128]{1,0:T(8,128)(2,1)S(1)}, bf16[576,128]{1,0:T(8,128)(2,1)S(1)}, u32[]{:S(2)}, u32[]{:S(2)}) collective-permute-start(bf16[576,128]{1,0:T(8,128)(2,1)S(1)} %get-tuple-element.69), channel_id=1, source_target_pairs={{0,16},{8,24},{16,0},{24,8},{1,17},{9,25},{17,1},{25,9},{2,18},{10... | collective-permute-start | bytes 442376 | tf_op jit(solution)/shard_map/ppermute | solution.py:89
  160.0 79.4 %collective-permute-start.6 = (bf16[576,128]{1,0:T(8,128)(2,1)S(1)}, bf16[576,128]{1,0:T(8,128)(2,1)S(1)}, u32[]{:S(2)}, u32[]{:S(2)}) collective-permute-start(bf16[576,128]{1,0:T(8,128)(2,1)S(1)} %get-tuple-element.68), channel_id=1, source_target_pairs={{0,24},{8,0},{16,8},{24,16},{1,25},{9,1},{17,9},{25,17},{2,26},{10... | collective-permute-start | bytes 442376 | tf_op jit(solution)/shard_map/ppermute | solution.py:89
  171.5 12.2 %all-to-all-start = ((bf16[4,2,64,512]{3,2,1,0:T(8,128)(2,1)}), bf16[4,2,64,512]{3,2,1,0:T(8,128)(2,1)S(1)}, u32[]{:S(2)}, u32[]{:S(2)}) async-start(bf16[4,2,64,512]{3,2,1,0:T(8,128)(2,1)} %broadcast_add_fusion.2), calls=%async_computation | async-start | bytes 1048576 | tf_op jit(solution)/shard_map/while/body/all_to_all | solution.py:28
  183.7 14.7 %collective-permute-start = (bf16[64,512]{1,0:T(8,128)(2,1)S(1)}, bf16[64,512]{1,0:T(8,128)(2,1)S(1)}, u32[]{:S(2)}, u32[]{:S(2)}) collective-permute-start(bf16[64,512]{1,0:T(8,128)(2,1)S(1)} %get-tuple-element.108), channel_id=1, source_target_pairs={{0,4},{1,36},{2,68},{3,100},{4,132},{5,164},{6,196},{7,228},{32,5}... | collective-permute-start | bytes 196616 | tf_op jit(solution)/shard_map/while/body/ppermute | solution.py:37
  185.7 19.0 %collective-permute-start.1 = (bf16[64,512]{1,0:T(8,128)(2,1)S(1)}, bf16[64,512]{1,0:T(8,128)(2,1)S(1)}, u32[]{:S(2)}, u32[]{:S(2)}) collective-permute-start(bf16[64,512]{1,0:T(8,128)(2,1)S(1)} %get-tuple-element.109), channel_id=1, source_target_pairs={{0,0},{1,32},{2,64},{3,96},{4,128},{5,160},{6,192},{7,224},{32,1},... | collective-permute-start | bytes 196616 | tf_op jit(solution)/shard_map/while/body/ppermute | solution.py:37
  205.4 29.8 %all-to-all-start.1 = ((bf16[4,64,128]{2,1,0:T(8,128)(2,1)}), bf16[4,64,128]{2,1,0:T(8,128)(2,1)S(1)}, u32[]{:S(2)}, u32[]{:S(2)}) async-start(bf16[4,64,128]{2,1,0:T(8,128)(2,1)} %copy.53), calls=%async_computation.1 | async-start | bytes 131072 | tf_op jit(solution)/shard_map/while/body/all_to_all | solution.py:28
  235.2 0.6 copy-start.1

commit v7 on v6

--- a/solution.py
+++ b/solution.py
@@ -68,19 +68,22 @@
     return jnp.where(low, same, other), jnp.where(low, other, same)
 
 
-def token_chain(both):
-    both = exchange(both, "zp")
+def token_chain(both, weights):
+    both = exchange(both, "zp") + weights[:1, :1] * 0
     feat = both.shape[2] // 2
     both = both.reshape(4, CAP, 2, feat).transpose(1, 2, 0, 3).reshape(CAP, 8 * feat)
     both = jnp.stack(ordered(swap(both), swap(both, piece_flip=4)))
     return gather(both, "x", 4).reshape(8 * CAP, 8 * feat)
 
 
+def piece_sum(row_grad):
+    row_grad = jnp.sum(exchange(row_grad, "x").astype(jnp.float32), axis=0).astype(jnp.bfloat16)
+    return jnp.stack(ordered(row_grad[0], row_grad[1]))
+
+
 def grad_chain(row_grad):
-    feat = row_grad.shape[3] // 4
-    row_grad = jnp.sum(exchange(row_grad, "x").astype(jnp.float32), axis=0).astype(jnp.bfloat16)
-    same, other = ordered(row_grad[0], row_grad[1])
-    same, other = swap(same), swap(other, group_flip=4)
+    feat = row_grad.shape[2] // 4
+    same, other = swap(row_grad[0]), swap(row_grad[1], group_flip=4)
     row_grad = (same.astype(jnp.float32) + other.astype(jnp.float32)).astype(jnp.bfloat16)
     return exchange(row_grad.reshape(CAP, 4, feat).transpose(1, 0, 2), "zp")
 
@@ -101,7 +104,7 @@
     cot_rows = jnp.dot(picker, out_grad, preferred_element_type=jnp.float32)
     carried = (row_weight[:, None] * cot_rows).astype(jnp.bfloat16)
     both = jnp.concatenate([picked, carried], axis=1).reshape(WINDOW, CAP, 2 * feat)
-    both = token_chain(both)
+    both = token_chain(both, weights)
     rows, carried = both[:, : 4 * feat], both[:, 4 * feat :]
 
     parts = jnp.concatenate(
@@ -132,13 +135,19 @@
     terms = terms.reshape(3 * hid, 4, feat).transpose(1, 0, 2)
     here = lax.axis_index("zh")
     parts = [lax.dynamic_index_in_dim(terms, (here + d) % 4, 0, False) for d in range(4)]
-    moved = [shift(parts[d], d) for d in (1, 2, 3)]
+    half = 3 * hid // 2
+    low, high = shift(parts[2][:half], 1), shift(parts[2][half:], 3)
     row_grad = contract(row_grads, gate_up, 1, 0).astype(jnp.bfloat16)
     row_grad = row_grad.reshape(4, 2, CAP, 4 * feat)
+    row_grad = once(piece_sum, row_grad, (2, CAP, 4 * feat))
+    after = row_grad[0, :1, :1] * 0
+    ahead = parts[1] + jnp.concatenate([low, jnp.zeros_like(high)], axis=0) + after
+    behind = parts[3] + jnp.concatenate([jnp.zeros_like(low), high], axis=0) + after
+    row_grad = row_grad + (ahead[:1, :1] + behind[:1, :1]) * 0
+    ahead, behind = shift(ahead, 1), shift(behind, 3)
     row_grad = once(grad_chain, row_grad, (WINDOW, CAP, feat))
     summed = parts[0].astype(jnp.float32) + row_grad[0, :1, :1].astype(jnp.float32) * 0
-    for part in moved:
-        summed = summed + part.astype(jnp.float32)
+    summed = summed + ahead.astype(jnp.float32) + behind.astype(jnp.float32)
     summed = summed.astype(jnp.bfloat16)
     gate_grad, up_grad = summed[:hid].T, summed[hid : 2 * hid].T
     down_grad = summed[2 * hid :]

time: 241 us -> 244 us (1.012)
  blocking collectives: 101 us -> 64.2 us
  waiting for transfers between devices: 45.9 us -> 64.1 us
  starting transfers between devices: 77.2 us -> 89.3 us
  local copies, waits for them, and re-layouts: 6.66 us -> 10.8 us
  between operations: 1.58 us -> 4.26 us
    all_to_all x2 -> x1, blocking collectives: 43.7 us -> 13.8 us  [exchange(): return lax.all_to_all(blocks, axis, 0, 0)]
    all_to_all x2, waiting for transfers between devices: 9.1 us -> 23.9 us  [gather(): return lax.all_to_all(copies, axis, 0, 0)]
    all_to_all x2 -> x3, starting transfers between devices: 23.8 us -> 33.7 us  [exchange(): return lax.all_to_all(blocks, axis, 0, 0)]
    all_gather x1, blocking collectives: 56.9 us -> 50.3 us  [shards(): weights = lax.all_gather(own, 'zh')]
    ppermute x4, waiting for transfers between devices: 18.7 us -> 21.6 us  [swap(): return lax.ppermute(block, ('l', 'x', 'y_high', 'y_low', 'c'), pairs)]
    slice x0 -> x5, local copies, waits for them, and re-layouts: none -> 2.74 us  [the longest x1 1.19 us: shards(): after = row_grad[0, :1, :1] * 0]
    ppermute x3 -> x4, starting transfers between devices: 26.6 us -> 29.1 us  [shift(): return lax.ppermute(block, 'zh', [(j, (j + d) % 4) for j in range(4)])]
    all_to_all x2 -> x3, waiting for transfers between devices: 18.2 us -> 18.6 us  [exchange(): return lax.all_to_all(blocks, axis, 0, 0)]
  transfers between devices with their start and end apart: 11 -> 13, of which waited for: 7 -> 8; matrix products, arithmetic and copies ran while one was open for 2% -> 4% of each run, Pallas kernels for 0% -> 0%
where the time goes in v7:
time: 244 us; the launch traced here: 243 us
  starting transfers between devices  89.3 us (37%)
  blocking collectives  64.2 us (26%)
  waiting for transfers between devices  64.1 us (26%)
  local copies, waits for them, and re-layouts  10.8 us (4%)
  other arithmetic  4.99 us (2%)
  matrix products  4.96 us (2%)
  between operations  4.26 us (2%)
    all_gather x1, blocking collectives, shards(): weights = lax.all_gather(own, 'zh')  50.3 us
    all_to_all x3, starting transfers between devices, exchange(): return lax.all_to_all(blocks, axis, 0, 0)  33.7 us
    ppermute x4, starting transfers between devices, shift(): return lax.ppermute(block, 'zh', [(j, (j + d) % 4) for j in range(4)])  29.1 us
    all_to_all x2, waiting for transfers between devices, gather(): return lax.all_to_all(copies, axis, 0, 0)  23.9 us
    ppermute x4, waiting for transfers between devices, swap(): return lax.ppermute(block, ('l', 'x', 'y_high', 'y_low', 'c'), pairs)  21.6 us
    all_to_all x3, waiting for transfers between devices, exchange(): return lax.all_to_all(blocks, axis, 0, 0)  18.6 us
    ppermute x4, starting transfers between devices, swap(): return lax.ppermute(block, ('l', 'x', 'y_high', 'y_low', 'c'), pairs)  17.9 us
    all_to_all x1, blocking collectives, exchange(): return lax.all_to_all(blocks, axis, 0, 0)  13.8 us
  transfers between devices with their start and end apart: 13, of which 8 were waited for; matrix products, arithmetic and copies ran while one was open for 4% of the time, Pallas kernels for 0%

profile of v7, /device:TPU:24, one launch (start us, length us, event | category | flops | bytes accessed | tf_op | source)
XLA Modules:
  0.0 242.6 jit_solution(13369233924426300705)
XLA Ops:
  4.7 11.2 %all-to-all-start.2 = ((bf16[4,64,256]{2,1,0:T(8,128)(2,1)}), bf16[4,64,256]{2,1,0:T(8,128)(2,1)S(1)}, u32[]{:S(2)}, u32[]{:S(2)}) async-start(bf16[4,64,256]{2,1,0:T(8,128)(2,1)} %bitcast.5), calls=%async_computation.2 | async-start | bytes 262144 | tf_op jit(solution)/shard_map/all_to_all | solution.py:28
  15.9 50.3 %all-gather = bf16[2304,128]{1,0:T(8,128)(2,1)S(1)} all-gather(bf16[576,128]{1,0:T(8,128)(2,1)S(1)} %pad_maximum_fusion.4), channel_id=2, replica_groups=mesh['zp'=4,'l'=2,'x'=4,'zh'=4,'y_high'=2,'y_low'=2,'c'=2] {'zh'}, dimensions={0}, use_global_device_ids=true | all-gather | bytes 737280 | tf_op jit(solution)/shard_map/all_gather | solution.py:98
  67.8 4.1 %collective-permute-start.2 = (bf16[64,1024]{1,0:T(8,128)(2,1)S(1)}, bf16[64,1024]{1,0:T(8,128)(2,1)S(1)}, u32[]{:S(2)}, u32[]{:S(2)}) collective-permute-start(bf16[64,1024]{1,0:T(8,128)(2,1)S(1)} %reshape.79), channel_id=1, source_target_pairs={{0,0},{1,32},{2,64},{3,96},{4,128},{5,160},{6,192},{7,224},{32,1},... | collective-permute-start | bytes 393224 | tf_op jit(solution)/shard_map/ppermute | solution.py:37
  71.9 3.9 %collective-permute-start.3 = (bf16[64,1024]{1,0:T(8,128)(2,1)S(1)}, bf16[64,1024]{1,0:T(8,128)(2,1)S(1)}, u32[]{:S(2)}, u32[]{:S(2)}) collective-permute-start(bf16[64,1024]{1,0:T(8,128)(2,1)S(1)} %reshape.79), channel_id=1, source_target_pairs={{0,128},{1,160},{2,192},{3,224},{4,0},{5,32},{6,64},{7,96},{32,129... | collective-permute-start | bytes 393224 | tf_op jit(solution)/shard_map/ppermute | solution.py:37
  75.8 7.0 %collective-permute-done.2 = bf16[64,1024]{1,0:T(8,128)(2,1)S(1)} collective-permute-done((bf16[64,1024]{1,0:T(8,128)(2,1)S(1)}, bf16[64,1024]{1,0:T(8,128)(2,1)S(1)}, u32[]{:S(2)}, u32[]{:S(2)}) %collective-permute-start.2) | collective-permute-done | bytes 131104 | tf_op jit(solution)/shard_map/ppermute | solution.py:37
  85.7 3.5 %all-to-all-start.3 = ((bf16[4,2,64,1024]{3,2,1,0:T(8,128)(2,1)}), bf16[4,2,64,1024]{3,2,1,0:T(8,128)(2,1)S(1)}, u32[]{:S(2)}, u32[]{:S(2)}) async-start(bf16[4,2,64,1024]{3,2,1,0:T(8,128)(2,1)} %broadcast_in_dim.59), calls=%async_computation.3 | async-start | bytes 2097152 | tf_op jit(solution)/shard_map/all_to_all | solution.py:24
  89.3 14.8 %all-to-all-done.3 = bf16[4,2,64,1024]{3,2,1,0:T(8,128)(2,1)S(1)} async-done(((bf16[4,2,64,1024]{3,2,1,0:T(8,128)(2,1)}), bf16[4,2,64,1024]{3,2,1,0:T(8,128)(2,1)S(1)}, u32[]{:S(2)}, u32[]{:S(2)}) %all-to-all-start.3) | async-done | bytes 1048608 | tf_op jit(solution)/shard_map/all_to_all | solution.py:24
  105.1 13.8 %all_to_all.35 = bf16[8,64,576]{2,1,0:T(8,128)(2,1)S(1)} all-to-all(bf16[8,64,576]{2,1,0:T(8,128)(2,1)S(1)} %pad_maximum_fusion.1), channel_id=1, replica_groups=mesh['zp'=4,'l'=2,'x'=4,'zh'=4,'y_high'=2,'y_low'=2,'c'=2] {'y_low','c',..., dimensions={0} | all-to-all | bytes 1179648 | tf_op jit(solution)/shard_map/all_to_all | solution.py:28
  120.1 5.1 %all-to-all-start.5 = ((bf16[8,64,576]{2,1,0:T(8,128)(2,1)}), bf16[8,64,576]{2,1,0:T(8,128)(2,1)S(1)}, u32[]{:S(2)}, u32[]{:S(2)}) async-start(bf16[8,64,576]{2,1,0:T(8,128)(2,1)} %broadcast_in_dim.60), calls=%async_computation.5 | async-start | bytes 1310720 | tf_op jit(solution)/shard_map/all_to_all | solution.py:24
  125.2 9.1 %all-to-all-done.5 = bf16[8,64,576]{2,1,0:T(8,128)(2,1)S(1)} async-done(((bf16[8,64,576]{2,1,0:T(8,128)(2,1)}), bf16[8,64,576]{2,1,0:T(8,128)(2,1)S(1)}, u32[]{:S(2)}, u32[]{:S(2)}) %all-to-all-start.5) | async-done | bytes 589856 | tf_op jit(solution)/shard_map/all_to_all | solution.py:24
  135.7 6.8 %collective-permute-start.4 = (bf16[288,128]{1,0:T(8,128)(2,1)S(1)}, bf16[288,128]{1,0:T(8,128)(2,1)S(1)}, u32[]{:S(2)}, u32[]{:S(2)}) collective-permute-start(bf16[288,128]{1,0:T(8,128)(2,1)S(1)} %get-tuple-element.115), channel_id=1, source_target_pairs={{0,8},{8,16},{16,24},{24,0},{1,9},{9,17},{17,25},{25,1},{2,10},{10... | collective-permute-start | bytes 221192 | tf_op jit(solution)/shard_map/ppermute | solution.py:92
  142.5 7.7 %collective-permute-start.5 = (bf16[288,128]{1,0:T(8,128)(2,1)S(1)}, bf16[288,128]{1,0:T(8,128)(2,1)S(1)}, u32[]{:S(2)}, u32[]{:S(2)}) collective-permute-start(bf16[288,128]{1,0:T(8,128)(2,1)S(1)} %get-tuple-element.114), channel_id=1, source_target_pairs={{0,24},{8,0},{16,8},{24,16},{1,25},{9,1},{17,9},{25,17},{2,26},{10... | collective-permute-start | bytes 221192 | tf_op jit(solution)/shard_map/ppermute | solution.py:92
  150.9 14.1 %while.22 = (s32[]{:T(128)}, bf16[2,64,512]{2,1,0:T(8,128)(2,1)}, s32[]{:T(128)}, bf16[4,2,64,512]{3,2,1,0:T(8,128)(2,1)S(1)}, s32[]{:T(128)}, /*index=5*/u32[]{:T(128)}, u32[]{:T(128)}, s32[]{:T(128)}, bf16[]{:T(256)}) while((s32[]{:T(128)}, bf16[2,64,512]{2,1,0:T(8,128)(2,1)}, s32[]{:T(128)}, bf16[4,2,64,512]{3,2,1,0:T(8,128)(2,1)S(1)}, ...), condition=%wide.region_6.7_spmd, body=%wide.region_4.6_spmd.sunk | while | flops 589831 | bytes 3801265 | solution.py:59
  151.8 3.5 %all-to-all-start = ((bf16[4,2,64,512]{3,2,1,0:T(8,128)(2,1)}), bf16[4,2,64,512]{3,2,1,0:T(8,128)(2,1)S(1)}, u32[]{:S(2)}, u32[]{:S(2)}) async-start(bf16[4,2,64,512]{3,2,1,0:T(8,128)(2,1)} %broadcast_add_fusion.6), calls=%async_computation | async-start | bytes 1048576 | tf_op jit(solution)/shard_map/while/body/all_to_all | solution.py:28
  155.2 9.0 %all-to-all-done = bf16[4,2,64,512]{3,2,1,0:T(8,128)(2,1)S(1)} async-done(((bf16[4,2,64,512]{3,2,1,0:T(8,128)(2,1)}), bf16[4,2,64,512]{3,2,1,0:T(8,128)(2,1)S(1)}, u32[]{:S(2)}, u32[]{:S(2)}) %all-to-all-start) | async-done | bytes 524320 | tf_op jit(solution)/shard_map/while/body/all_to_all | solution.py:28
  167.5 6.8 %collective-permute-start.6 = (bf16[576,128]{1,0:T(8,128)(2,1)S(1)}, bf16[576,128]{1,0:T(8,128)(2,1)S(1)}, u32[]{:S(2)}, u32[]{:S(2)}) collective-permute-start(bf16[576,128]{1,0:T(8,128)(2,1)S(1)} %get-tuple-element.101), channel_id=1, source_target_pairs={{0,8},{8,16},{16,24},{24,0},{1,9},{9,17},{17,25},{25,1},{2,10},{10... | collective-permute-start | bytes 442376 | tf_op jit(solution)/shard_map/ppermute | solution.py:92
  174.8 7.7 %collective-permute-start.7 = (bf16[576,128]{1,0:T(8,128)(2,1)S(1)}, bf16[576,128]{1,0:T(8,128)(2,1)S(1)}, u32[]{:S(2)}, u32[]{:S(2)}) collective-permute-start(bf16[576,128]{1,0:T(8,128)(2,1)S(1)} %get-tuple-element.100), channel_id=1, source_target_pairs={{0,24},{8,0},{16,8},{24,16},{1,25},{9,1},{17,9},{25,17},{2,26},{10... | collective-permute-start | bytes 442376 | tf_op jit(solution)/shard_map/ppermute | solution.py:92
  185.4 52.9 %while.23 = (s32[]{:T(128)}, bf16[4,64,128]{2,1,0:T(8,128)(2,1)}, s32[]{:T(128)}, bf16[2,64,512]{2,1,0:T(8,128)(2,1)S(1)}, s32[]{:T(128)}) while((s32[]{:T(128)}, bf16[4,64,128]{2,1,0:T(8,128)(2,1)}, s32[]{:T(128)}, bf16[2,64,512]{2,1,0:T(8,128)(2,1)S(1)}, s32[]{:T(128)}) %tuple.62), condition=%wide.region_8.9_spmd, body=%wide.region_7.8_spmd.sunk | while | flops 196611 | bytes 1966289 | solution.py:59
  185.4 3.2 %collective-permute-start = (bf16[64,512]{1,0:T(8,128)(2,1)S(1)}, bf16[64,512]{1,0:T(8,128)(2,1)S(1)}, u32[]{:S(2)}, u32[]{:S(2)}) collective-permute-start(bf16[64,512]{1,0:T(8,128)(2,1)S(1)} %get-tuple-element.170), channel_id=1, source_target_pairs={{0,4},{1,36},{2,68},{3,100},{4,132},{5,164},{6,196},{7,228},{32,5}... | collective-permute-start | bytes 196616 | tf_op jit(solution)/shard_map/while/body/ppermute | solution.py:37
  188.6 6.7 %collective-permute-start.1 = (bf16[64,512]{1,0:T(8,128)(2,1)S(1)}, bf16[64,512]{1,0:T(8,128)(2,1)S(1)}, u32[]{:S(2)}, u32[]{:S(2)}) collective-permute-start(bf16[64,512]{1,0:T(8,128)(2,1)S(1)} %get-tuple-element.171), channel_id=1, source_target_pairs={{0,0},{1,32},{2,64},{3,96},{4,128},{5,160},{6,192},{7,224},{32,1},... | collective-permute-start | bytes 196616 | tf_op jit(solution)/shard_map/while/body/ppermute | solution.py:37
  195.4 11.0 %collective-permute-done = bf16[64,512]{1,0:T(8,128)(2,1)S(1)} collective-permute-done((bf16[64,512]{1,0:T(8,128)(2,1)S(1)}, bf16[64,512]{1,0:T(8,128)(2,1)S(1)}, u32[]{:S(2)}, u32[]{:S(2)}) %collective-permute-start) | collective-permute-done | bytes 65568 | tf_op jit(solution)/shard_map/while/body/ppermute | solution.py:37
  206.4 1.9 collective-permute-done.1
  208.9 19.0 %all-to-all-start.1 = ((bf16[4,64,128]{2,1,0:T(8,128)(2,1)}), bf16[4,64,128]{2,1,0:T(8,128)(2,1)S(1)}, u32[]{:S(2)}, u32[]{:S(2)}) async-start(bf16[4,64,128]{2,1,0:T(8,128)(2,1)} %copy.53), calls=%async_computation.1 | async-start | bytes 131072 | tf_op jit(solution)/shard_map/while/body/all_to_all | solution.py:28
  228.0 9.7 %all-to-all-done.1 = bf16[4,64,128]{2,1,0:T(8,128)(2,1)S(1)} async-done(((bf16[4,64,128]{2,1,0:T(8,128)(2,1)}), bf16[4,64,128]{2,1,0:T(8,128)(2,1)S(1)}, u32[]{:S(2)}, u32[]{:S(2)}) %all-to-all-start.1) | async-done | bytes 65568 | tf_op jit(solution)/shard_map/while/body/all_to_all | solution.py:28
  (75 shorter events, 22.4 us)
Async XLA Ops:
  0.6 2.1 copy-start
  0.6 15.3 %copy-start.4 = (bf16[128,192]{0,1:T(8,128)(2,1)S(1)}, bf16[128,192]{0,1:T(8,128)(2,1)}, u32[]{:S(2)}) copy-start(bf16[128,192]{0,1:T(8,128)(2,1)} %param.15) | copy-start | bytes 147460
  0.7 15.3 %copy-start.3 = (bf16[128,192]{0,1:T(8,128)(2,1)S(1)}, bf16[128,192]{0,1:T(8,128)(2,1)}, u32[]{:S(2)}) copy-start(bf16[128,192]{0,1:T(8,128)(2,1)} %param.16) | copy-start | bytes 147460
  0.7 15.3 %copy-start.2 = (bf16[192,128]{1,0:T(8,128)(2,1)S(1)}, bf16[192,128]{1,0:T(8,128)(2,1)}, u32[]{:S(2)}) copy-start(bf16[192,128]{1,0:T(8,128)(2,1)} %param.17) | copy-start | bytes 147460
  4.7 62.7 %all-to-all-start.2 = ((bf16[4,64,256]{2,1,0:T(8,128)(2,1)}), bf16[4,64,256]{2,1,0:T(8,128)(2,1)S(1)}, u32[]{:S(2)}, u32[]{:S(2)}) async-start(bf16[4,64,256]{2,1,0:T(8,128)(2,1)} %bitcast.5), calls=%async_computation.2 | async-start | bytes 262144 | tf_op jit(solution)/shard_map/all_to_all | solution.py:28
  67.8 15.1 %collective-permute-start.2 = (bf16[64,1024]{1,0:T(8,128)(2,1)S(1)}, bf16[64,1024]{1,0:T(8,128)(2,1)S(1)}, u32[]{:S(2)}, u32[]{:S(2)}) collective-permute-start(bf16[64,1024]{1,0:T(8,128)(2,1)S(1)} %reshape.79), channel_id=1, source_target_pairs={{0,0},{1,32},{2,64},{3,96},{4,128},{5,160},{6,192},{7,224},{32,1},... | collective-permute-start | bytes 393224 | tf_op jit(solution)/shard_map/ppermute | solution.py:37
  71.9 12.6 %collective-permute-start.3 = (bf16[64,1024]{1,0:T(8,128)(2,1)S(1)}, bf16[64,1024]{1,0:T(8,128)(2,1)S(1)}, u32[]{:S(2)}, u32[]{:S(2)}) collective-permute-start(bf16[64,1024]{1,0:T(8,128)(2,1)S(1)} %reshape.79), channel_id=1, source_target_pairs={{0,128},{1,160},{2,192},{3,224},{4,0},{5,32},{6,64},{7,96},{32,129... | collective-permute-start | bytes 393224 | tf_op jit(solution)/shard_map/ppermute | solution.py:37
  85.7 18.4 %all-to-all-start.3 = ((bf16[4,2,64,1024]{3,2,1,0:T(8,128)(2,1)}), bf16[4,2,64,1024]{3,2,1,0:T(8,128)(2,1)S(1)}, u32[]{:S(2)}, u32[]{:S(2)}) async-start(bf16[4,2,64,1024]{3,2,1,0:T(8,128)(2,1)} %broadcast_in_dim.59), calls=%async_computation.3 | async-start | bytes 2097152 | tf_op jit(solution)/shard_map/all_to_all | solution.py:24
  120.1 14.2 %all-to-all-start.5 = ((bf16[8,64,576]{2,1,0:T(8,128)(2,1)}), bf16[8,64,576]{2,1,0:T(8,128)(2,1)S(1)}, u32[]{:S(2)}, u32[]{:S(2)}) async-start(bf16[8,64,576]{2,1,0:T(8,128)(2,1)} %broadcast_in_dim.60), calls=%async_computation.5 | async-start | bytes 1310720 | tf_op jit(solution)/shard_map/all_to_all | solution.py:24
  135.7 31.2 %collective-permute-start.4 = (bf16[288,128]{1,0:T(8,128)(2,1)S(1)}, bf16[288,128]{1,0:T(8,128)(2,1)S(1)}, u32[]{:S(2)}, u32[]{:S(2)}) collective-permute-start(bf16[288,128]{1,0:T(8,128)(2,1)S(1)} %get-tuple-element.115), channel_id=1, source_target_pairs={{0,8},{8,16},{16,24},{24,0},{1,9},{9,17},{17,25},{25,1},{2,10},{10... | collective-permute-start | bytes 221192 | tf_op jit(solution)/shard_map/ppermute | solution.py:92
  142.5 24.4 %collective-permute-start.5 = (bf16[288,128]{1,0:T(8,128)(2,1)S(1)}, bf16[288,128]{1,0:T(8,128)(2,1)S(1)}, u32[]{:S(2)}, u32[]{:S(2)}) collective-permute-start(bf16[288,128]{1,0:T(8,128)(2,1)S(1)} %get-tuple-element.114), channel_id=1, source_target_pairs={{0,24},{8,0},{16,8},{24,16},{1,25},{9,1},{17,9},{25,17},{2,26},{10... | collective-permute-start | bytes 221192 | tf_op jit(solution)/shard_map/ppermute | solution.py:92
  151.8 12.4 %all-to-all-start = ((bf16[4,2,64,512]{3,2,1,0:T(8,128)(2,1)}), bf16[4,2,64,512]{3,2,1,0:T(8,128)(2,1)S(1)}, u32[]{:S(2)}, u32[]{:S(2)}) async-start(bf16[4,2,64,512]{3,2,1,0:T(8,128)(2,1)} %broadcast_add_fusion.6), calls=%async_computation | async-start | bytes 1048576 | tf_op jit(solution)/shard_map/while/body/all_to_all | solution.py:28
  167.5 74.4 %collective-permute-start.6 = (bf16[576,128]{1,0:T(8,128)(2,1)S(1)}, bf16[576,128]{1,0:T(8,128)(2,1)S(1)}, u32[]{:S(2)}, u32[]{:S(2)}) collective-permute-start(bf16[576,128]{1,0:T(8,128)(2,1)S(1)} %get-tuple-element.101), channel_id=1, source_target_pairs={{0,8},{8,16},{16,24},{24,0},{1,9},{9,17},{17,25},{25,1},{2,10},{10... | collective-permute-start | bytes 442376 | tf_op jit(solution)/shard_map/ppermute | solution.py:92
  174.8 67.0 %collective-permute-start.7 = (bf16[576,128]{1,0:T(8,128)(2,1)S(1)}, bf16[576,128]{1,0:T(8,128)(2,1)S(1)}, u32[]{:S(2)}, u32[]{:S(2)}) collective-permute-start(bf16[576,128]{1,0:T(8,128)(2,1)S(1)} %get-tuple-element.100), channel_id=1, source_target_pairs={{0,24},{8,0},{16,8},{24,16},{1,25},{9,1},{17,9},{25,17},{2,26},{10... | collective-permute-start | bytes 442376 | tf_op jit(solution)/shard_map/ppermute | solution.py:92
  185.4 20.9 %collective-permute-start = (bf16[64,512]{1,0:T(8,128)(2,1)S(1)}, bf16[64,512]{1,0:T(8,128)(2,1)S(1)}, u32[]{:S(2)}, u32[]{:S(2)}) collective-permute-start(bf16[64,512]{1,0:T(8,128)(2,1)S(1)} %get-tuple-element.170), channel_id=1, source_target_pairs={{0,4},{1,36},{2,68},{3,100},{4,132},{5,164},{6,196},{7,228},{32,5}... | collective-permute-start | bytes 196616 | tf_op jit(solution)/shard_map/while/body/ppermute | solution.py:37
  188.6 19.6 %collective-permute-start.1 = (bf16[64,512]{1,0:T(8,128)(2,1)S(1)}, bf16[64,512]{1,0:T(8,128)(2,1)S(1)}, u32[]{:S(2)}, u32[]{:S(2)}) collective-permute-start(bf16[64,512]{1,0:T(8,128)(2,1)S(1)} %get-tuple-element.171), channel_id=1, source_target_pairs={{0,0},{1,32},{2,64},{3,96},{4,128},{5,160},{6,192},{7,224},{32,1},... | collective-permute-start | bytes 196616 | tf_op jit(solution)/shard_map/while/body/ppermute | solution.py:37
  208.9 28.7 %all-to-all-start.1 = ((bf16[4,64,128]{2,1,0:T(8,128)(2,1)}), bf16[4,64,128]{2,1,0:T(8,128)(2,1)S(1)}, u32[]{:S(2)}, u32[]{:S(2)}) async-start(bf16[4,64,128]{2,1,0:T(8,128)(2,1)} %copy.53), calls=%async_computation.1 | async-start | bytes 131072 | tf_op jit(solution)/shard_map/while/body/all_to_all | solution.py:28
  237.6 0.6 copy-start.1

commit v8 on v6

--- a/solution.py
+++ b/solution.py
@@ -60,7 +60,7 @@
         lambda state: state[0] < turns,
         lambda state: (state[0] + 1, state[1], step(state[1] + state[0].astype(jnp.bfloat16))),
         start,
-    )[2]
+    )[::2]
 
 
 def ordered(same, other):
@@ -85,24 +85,21 @@
     return exchange(row_grad.reshape(CAP, 4, feat).transpose(1, 0, 2), "zp")
 
 
-def shift(block, d):
-    return lax.ppermute(block, "zh", [(j, (j + d) % 4) for j in range(4)])
-
-
 def shards(tokens, out_grad, route_probs, expert_ids, gate_weight, up_weight, down_weight):
     hid, feat = down_weight.shape
     own = jnp.concatenate([gate_weight.T, up_weight.T, down_weight], axis=0)
-    weights = lax.all_gather(own, "zh")
-    weights = jnp.concatenate(list(weights), axis=1)
-    gate_up, down = weights[: 2 * hid], weights[2 * hid :]
+    weights = lax.all_gather(own, ("c", "zh")).reshape(2, 4, 3 * hid, feat)
 
     picker, row_weight = select(route_probs, expert_ids)
     picked = jnp.dot(picker, tokens, preferred_element_type=jnp.float32).astype(jnp.bfloat16)
     cot_rows = jnp.dot(picker, out_grad, preferred_element_type=jnp.float32)
     carried = (row_weight[:, None] * cot_rows).astype(jnp.bfloat16)
     both = jnp.concatenate([picked, carried], axis=1).reshape(WINDOW, CAP, 2 * feat)
-    both = token_chain(both)
+    turns, both = once(token_chain, both, (8 * CAP, 8 * feat))
     rows, carried = both[:, : 4 * feat], both[:, 4 * feat :]
+    weights = lax.dynamic_index_in_dim(weights, lax.axis_index("c") + turns - 1, 0, False)
+    weights = jnp.concatenate(list(weights), axis=1)
+    gate_up, down = weights[: 2 * hid], weights[2 * hid :]
 
     parts = jnp.concatenate(
         [contract(rows, gate_up, 1, 1), contract(carried, down, 1, 1)], axis=1
@@ -129,19 +126,13 @@
     terms = jnp.concatenate(
         [contract(row_grads, rows, 0, 0), contract(hidden, carried, 0, 0)], axis=0
     ).astype(jnp.bfloat16)
-    terms = terms.reshape(3 * hid, 4, feat).transpose(1, 0, 2)
-    here = lax.axis_index("zh")
-    parts = [lax.dynamic_index_in_dim(terms, (here + d) % 4, 0, False) for d in range(4)]
-    moved = [shift(parts[d], d) for d in (1, 2, 3)]
-    row_grad = contract(row_grads, gate_up, 1, 0).astype(jnp.bfloat16)
-    row_grad = row_grad.reshape(4, 2, CAP, 4 * feat)
-    row_grad = once(grad_chain, row_grad, (WINDOW, CAP, feat))
-    summed = parts[0].astype(jnp.float32) + row_grad[0, :1, :1].astype(jnp.float32) * 0
-    for part in moved:
-        summed = summed + part.astype(jnp.float32)
-    summed = summed.astype(jnp.bfloat16)
-    gate_grad, up_grad = summed[:hid].T, summed[hid : 2 * hid].T
-    down_grad = summed[2 * hid :]
+    summed = lax.psum_scatter(terms.reshape(3 * hid, 4, feat).transpose(1, 0, 2), "zh")
+    row_grad = contract(row_grads, gate_up, 1, 0).astype(jnp.bfloat16).reshape(4, 2, CAP, 4 * feat)
+    turns, row_grad = once(grad_chain, row_grad, (WINDOW, CAP, feat))
+    gate_grad, up_grad, down_grad = (
+        jnp.where(turns > 0, summed[i * hid : (i + 1) * hid], 0) for i in range(3)
+    )
+    gate_grad, up_grad = gate_grad.T, up_grad.T
 
     x_grad = contract(picker, row_grad.reshape(WINDOW * CAP, feat), 0, 0).astype(jnp.bfloat16)
     return (x_grad, gate_grad, up_grad, down_grad)

time: 241 us -> 235 us (0.975)
  the two profiles are of different devices: /device:TPU:24 before, /device:TPU:118 now
where the time goes in v8:
time: 235 us; the launch traced here: 234 us
  waiting for transfers between devices  128 us (54%)
  starting transfers between devices  38.9 us (17%)
  blocking collectives  32.8 us (14%)
  between operations  14.2 us (6%)
  local copies, waits for them, and re-layouts  8.22 us (3%)
  other arithmetic  7.02 us (3%)
  matrix products  4.96 us (2%)
    reduce_scatter x1, waiting for transfers between devices, shards(): lax.psum_scatter(terms.reshape(3 * hid, 4, feat).transpose(1, 0, 2), 'zh')  39.9 us
    all_gather x1, waiting for transfers between devices, shards(): weights = lax.all_gather(own, ('c', 'zh')).reshape(2, 4, 3 * hid, feat)  34 us
    all_to_all x2, blocking collectives, exchange(): return lax.all_to_all(blocks, axis, 0, 0)  32.8 us
    all_to_all x2, waiting for transfers between devices, exchange(): return lax.all_to_all(blocks, axis, 0, 0)  22.4 us
    all_to_all x2, waiting for transfers between devices, gather(): return lax.all_to_all(copies, axis, 0, 0)  21.2 us
    ppermute x4, starting transfers between devices, swap(): return lax.ppermute(block, ('l', 'x', 'y_high', 'y_low', 'c'), pairs)  17.1 us
    all_to_all x2, starting transfers between devices, exchange(): return lax.all_to_all(blocks, axis, 0, 0)  12.1 us
    ppermute x4, waiting for transfers between devices, swap(): return lax.ppermute(block, ('l', 'x', 'y_high', 'y_low', 'c'), pairs)  10.6 us
  transfers between devices with their start and end apart: 10, of which 10 were waited for; matrix products, arithmetic and copies ran while one was open for 4% of the time, Pallas kernels for 0%

profile of v8, /device:TPU:118, one launch (start us, length us, event | category | flops | bytes accessed | tf_op | source)
XLA Modules:
  0.0 234.3 jit_solution(3144549289823227289)
XLA Ops:
  7.2 1.5 pad_maximum_fusion.3
  13.3 52.3 %while.22 = (s32[]{:T(128)}, bf16[512,1024]{1,0:T(8,128)(2,1)}, s32[]{:T(128)}, bf16[4,64,256]{2,1,0:T(8,128)(2,1)S(1)}, s32[]{:T(128)}, /*index=5*/u32[]{:T(128)}, u32[]{:T(128)}, s32[]{:T(128)}) while((s32[]{:T(128)}, bf16[512,1024]{1,0:T(8,128)(2,1)}, s32[]{:T(128)}, bf16[4,64,256]{2,1,0:T(8,128)(2,1)S(1)}, s32[]{:T(128)}, ...), condition=%wide.region_4.5_spmd, body=%wide.region_3.4_spmd.sunk | while | flops 327687 | bytes 12058899 | solution.py:59
  13.3 18.8 %all_to_all.41 = bf16[4,64,256]{2,1,0:T(8,128)(2,1)S(1)} all-to-all(bf16[4,64,256]{2,1,0:T(8,128)(2,1)S(1)} %broadcast_add_fusion.4), channel_id=1, replica_groups=mesh['zp'=4,'l'=2,'x'=4,'zh'=4,'y_high'=2,'y_low'=2,'c'=2] {'zp'}, dimensions={0} | all-to-all | bytes 262144 | tf_op jit(solution)/shard_map/while/body/all_to_all | solution.py:28
  32.4 1.9 collective-permute-start
  34.3 6.1 %collective-permute-start.1 = (bf16[64,1024]{1,0:T(8,128)(2,1)S(1)}, bf16[64,1024]{1,0:T(8,128)(2,1)S(1)}, u32[]{:S(2)}, u32[]{:S(2)}) collective-permute-start(bf16[64,1024]{1,0:T(8,128)(2,1)S(1)} %reshape.97), channel_id=1, source_target_pairs={{0,128},{1,160},{2,192},{3,224},{4,0},{5,32},{6,64},{7,96},{32,129... | collective-permute-start | bytes 393224 | tf_op jit(solution)/shard_map/while/body/ppermute | solution.py:37
  40.4 3.1 %collective-permute-done = bf16[64,1024]{1,0:T(8,128)(2,1)S(1)} collective-permute-done((bf16[64,1024]{1,0:T(8,128)(2,1)S(1)}, bf16[64,1024]{1,0:T(8,128)(2,1)S(1)}, u32[]{:S(2)}, u32[]{:S(2)}) %collective-permute-start) | collective-permute-done | bytes 131104 | tf_op jit(solution)/shard_map/while/body/ppermute | solution.py:37
  43.5 3.6 %collective-permute-done.1 = bf16[64,1024]{1,0:T(8,128)(2,1)S(1)} collective-permute-done((bf16[64,1024]{1,0:T(8,128)(2,1)S(1)}, bf16[64,1024]{1,0:T(8,128)(2,1)S(1)}, u32[]{:S(2)}, u32[]{:S(2)}) %collective-permute-start.1) | collective-permute-done | bytes 131104 | tf_op jit(solution)/shard_map/while/body/ppermute | solution.py:37
  48.3 4.5 %all-to-all-start.1 = ((bf16[4,2,64,1024]{3,2,1,0:T(8,128)(2,1)}), bf16[4,2,64,1024]{3,2,1,0:T(8,128)(2,1)S(1)}, u32[]{:S(2)}, u32[]{:S(2)}) async-start(bf16[4,2,64,1024]{3,2,1,0:T(8,128)(2,1)} %broadcast_in_dim.73), calls=%async_computation.1 | async-start | bytes 2097152 | tf_op jit(solution)/shard_map/while/body/all_to_all | solution.py:24
  52.8 11.7 %all-to-all-done.1 = bf16[4,2,64,1024]{3,2,1,0:T(8,128)(2,1)S(1)} async-done(((bf16[4,2,64,1024]{3,2,1,0:T(8,128)(2,1)}), bf16[4,2,64,1024]{3,2,1,0:T(8,128)(2,1)S(1)}, u32[]{:S(2)}, u32[]{:S(2)}) %all-to-all-start.1) | async-done | bytes 1048608 | tf_op jit(solution)/shard_map/while/body/all_to_all | solution.py:24
  65.5 34.0 %all-gather.3.cloned.1.call-done = bf16[4608,128]{1,0:T(8,128)(2,1)} async-done(((bf16[576,128]{1,0:T(8,128)(2,1)}), bf16[4608,128]{1,0:T(8,128)(2,1)}) %all-gather.3.cloned.1.call-update) | async-done | bytes 1179664 | tf_op jit(solution)/shard_map/all_gather | solution.py:91
  102.0 14.0 %all_to_all.40 = bf16[8,64,576]{2,1,0:T(8,128)(2,1)S(1)} all-to-all(bf16[8,64,576]{2,1,0:T(8,128)(2,1)S(1)} %pad_maximum_fusion.1), channel_id=1, replica_groups=mesh['zp'=4,'l'=2,'x'=4,'zh'=4,'y_high'=2,'y_low'=2,'c'=2] {'y_low','c',..., dimensions={0} | all-to-all | bytes 1179648 | tf_op jit(solution)/shard_map/all_to_all | solution.py:28
  117.2 5.2 %all-to-all-start.5 = ((bf16[8,64,576]{2,1,0:T(8,128)(2,1)}), bf16[8,64,576]{2,1,0:T(8,128)(2,1)S(1)}, u32[]{:S(2)}, u32[]{:S(2)}) async-start(bf16[8,64,576]{2,1,0:T(8,128)(2,1)} %broadcast_in_dim.63), calls=%async_computation.5 | async-start | bytes 1310720 | tf_op jit(solution)/shard_map/all_to_all | solution.py:24
  122.4 9.5 %all-to-all-done.5 = bf16[8,64,576]{2,1,0:T(8,128)(2,1)S(1)} async-done(((bf16[8,64,576]{2,1,0:T(8,128)(2,1)}), bf16[8,64,576]{2,1,0:T(8,128)(2,1)S(1)}, u32[]{:S(2)}, u32[]{:S(2)}) %all-to-all-start.5) | async-done | bytes 589856 | tf_op jit(solution)/shard_map/all_to_all | solution.py:24
  134.7 49.6 %while.23 = (s32[]{:T(128)}, bf16[4,64,128]{2,1,0:T(8,128)(2,1)}, s32[]{:T(128)}, bf16[4,2,64,512]{3,2,1,0:T(8,128)(2,1)S(1)}, s32[]{:T(128)}, /*index=5*/u32[]{:T(128)}, u32[]{:T(128)}, s32[]{:T(128)}, bf16[]{:T(256)}) while((s32[]{:T(128)}, bf16[4,64,128]{2,1,0:T(8,128)(2,1)}, s32[]{:T(128)}, bf16[4,2,64,512]{3,2,1,0:T(8,128)(2,1)S(1)}, ...), condition=%wide.region_8.9_spmd, body=%wide.region_6.8_spmd.sunk | while | flops 655367 | bytes 4981053 | solution.py:59
  135.5 6.9 %all-to-all-start.2 = ((bf16[4,2,64,512]{3,2,1,0:T(8,128)(2,1)}), bf16[4,2,64,512]{3,2,1,0:T(8,128)(2,1)S(1)}, u32[]{:S(2)}, u32[]{:S(2)}) async-start(bf16[4,2,64,512]{3,2,1,0:T(8,128)(2,1)} %broadcast_add_fusion.5), calls=%async_computation.2 | async-start | bytes 1048576 | tf_op jit(solution)/shard_map/while/body/all_to_all | solution.py:28
  142.4 7.9 %all-to-all-done.2 = bf16[4,2,64,512]{3,2,1,0:T(8,128)(2,1)S(1)} async-done(((bf16[4,2,64,512]{3,2,1,0:T(8,128)(2,1)}), bf16[4,2,64,512]{3,2,1,0:T(8,128)(2,1)S(1)}, u32[]{:S(2)}, u32[]{:S(2)}) %all-to-all-start.2) | async-done | bytes 524320 | tf_op jit(solution)/shard_map/while/body/all_to_all | solution.py:28
  150.5 2.4 %collective-permute-start.2 = (bf16[64,512]{1,0:T(8,128)(2,1)S(1)}, bf16[64,512]{1,0:T(8,128)(2,1)S(1)}, u32[]{:S(2)}, u32[]{:S(2)}) collective-permute-start(bf16[64,512]{1,0:T(8,128)(2,1)S(1)} %get-tuple-element.172), channel_id=1, source_target_pairs={{0,4},{1,36},{2,68},{3,100},{4,132},{5,164},{6,196},{7,228},{32,5}... | collective-permute-start | bytes 196616 | tf_op jit(solution)/shard_map/while/body/ppermute | solution.py:37
  152.9 6.6 %collective-permute-start.3 = (bf16[64,512]{1,0:T(8,128)(2,1)S(1)}, bf16[64,512]{1,0:T(8,128)(2,1)S(1)}, u32[]{:S(2)}, u32[]{:S(2)}) collective-permute-start(bf16[64,512]{1,0:T(8,128)(2,1)S(1)} %get-tuple-element.173), channel_id=1, source_target_pairs={{0,0},{1,32},{2,64},{3,96},{4,128},{5,160},{6,192},{7,224},{32,1},... | collective-permute-start | bytes 196616 | tf_op jit(solution)/shard_map/while/body/ppermute | solution.py:37
  160.2 3.1 %collective-permute-done.3 = bf16[64,512]{1,0:T(8,128)(2,1)S(1)} collective-permute-done((bf16[64,512]{1,0:T(8,128)(2,1)S(1)}, bf16[64,512]{1,0:T(8,128)(2,1)S(1)}, u32[]{:S(2)}, u32[]{:S(2)}) %collective-permute-start.3) | collective-permute-done | bytes 65568 | tf_op jit(solution)/shard_map/while/body/ppermute | solution.py:37
  164.1 5.2 %all-to-all-start.3 = ((bf16[4,64,128]{2,1,0:T(8,128)(2,1)}), bf16[4,64,128]{2,1,0:T(8,128)(2,1)S(1)}, u32[]{:S(2)}, u32[]{:S(2)}) async-start(bf16[4,64,128]{2,1,0:T(8,128)(2,1)} %copy.58), calls=%async_computation.3 | async-start | bytes 131072 | tf_op jit(solution)/shard_map/while/body/all_to_all | solution.py:28
  169.2 14.5 %all-to-all-done.3 = bf16[4,64,128]{2,1,0:T(8,128)(2,1)S(1)} async-done(((bf16[4,64,128]{2,1,0:T(8,128)(2,1)}), bf16[4,64,128]{2,1,0:T(8,128)(2,1)S(1)}, u32[]{:S(2)}, u32[]{:S(2)}) %all-to-all-start.3) | async-done | bytes 65568 | tf_op jit(solution)/shard_map/while/body/all_to_all | solution.py:28
  184.3 1.7 fusion.3
  186.0 39.9 %reduce-scatter.2.cloned.1.call-done = bf16[1,576,128]{2,1,0:T(8,128)(2,1)} async-done(((bf16[4,576,128]{2,1,0:T(8,128)(2,1)}), bf16[1,576,128]{2,1,0:T(8,128)(2,1)}) %reduce-scatter.2.cloned.1.call-update) | async-done | bytes 147472 | tf_op jit(solution)/shard_map/reduce_scatter | solution.py:129
  225.9 1.5 fusion.25
  (57 shorter events, 16.2 us)
Async XLA Ops:
  7.2 3.7 %copy-start = (bf16[128,128]{1,0:T(8,128)(2,1)S(1)}, bf16[128,128]{1,0:T(8,128)(2,1)}, u32[]{:S(2)}) copy-start(bf16[128,128]{1,0:T(8,128)(2,1)} %param.11) | copy-start | bytes 98308
  7.2 92.3 %all-gather.3.cloned.1.call-start = ((), (), s32[]{:S(2)}) async-start(), calls=%async_computation.8 | async-start | bytes 1327104 | tf_op jit(solution)/shard_map/all_gather | solution.py:91
  32.4 11.1 %collective-permute-start = (bf16[64,1024]{1,0:T(8,128)(2,1)S(1)}, bf16[64,1024]{1,0:T(8,128)(2,1)S(1)}, u32[]{:S(2)}, u32[]{:S(2)}) collective-permute-start(bf16[64,1024]{1,0:T(8,128)(2,1)S(1)} %reshape.97), channel_id=1, source_target_pairs={{0,0},{1,32},{2,64},{3,96},{4,128},{5,160},{6,192},{7,224},{32,1},... | collective-permute-start | bytes 393224 | tf_op jit(solution)/shard_map/while/body/ppermute | solution.py:37
  34.3 12.8 %collective-permute-start.1 = (bf16[64,1024]{1,0:T(8,128)(2,1)S(1)}, bf16[64,1024]{1,0:T(8,128)(2,1)S(1)}, u32[]{:S(2)}, u32[]{:S(2)}) collective-permute-start(bf16[64,1024]{1,0:T(8,128)(2,1)S(1)} %reshape.97), channel_id=1, source_target_pairs={{0,128},{1,160},{2,192},{3,224},{4,0},{5,32},{6,64},{7,96},{32,129... | collective-permute-start | bytes 393224 | tf_op jit(solution)/shard_map/while/body/ppermute | solution.py:37
  48.3 16.2 %all-to-all-start.1 = ((bf16[4,2,64,1024]{3,2,1,0:T(8,128)(2,1)}), bf16[4,2,64,1024]{3,2,1,0:T(8,128)(2,1)S(1)}, u32[]{:S(2)}, u32[]{:S(2)}) async-start(bf16[4,2,64,1024]{3,2,1,0:T(8,128)(2,1)} %broadcast_in_dim.73), calls=%async_computation.1 | async-start | bytes 2097152 | tf_op jit(solution)/shard_map/while/body/all_to_all | solution.py:24
  64.5 1.0 copy-start.1
  99.5 1.5 copy-start.2
  117.2 14.7 %all-to-all-start.5 = ((bf16[8,64,576]{2,1,0:T(8,128)(2,1)}), bf16[8,64,576]{2,1,0:T(8,128)(2,1)S(1)}, u32[]{:S(2)}, u32[]{:S(2)}) async-start(bf16[8,64,576]{2,1,0:T(8,128)(2,1)} %broadcast_in_dim.63), calls=%async_computation.5 | async-start | bytes 1310720 | tf_op jit(solution)/shard_map/all_to_all | solution.py:24
  122.4 103.5 %reduce-scatter.2.cloned.1.call-start = ((), (), s32[]{:S(2)}) async-start(), calls=%async_computation.7 | async-start | bytes 737280 | tf_op jit(solution)/shard_map/reduce_scatter | solution.py:129
  135.5 14.9 %all-to-all-start.2 = ((bf16[4,2,64,512]{3,2,1,0:T(8,128)(2,1)}), bf16[4,2,64,512]{3,2,1,0:T(8,128)(2,1)S(1)}, u32[]{:S(2)}, u32[]{:S(2)}) async-start(bf16[4,2,64,512]{3,2,1,0:T(8,128)(2,1)} %broadcast_add_fusion.5), calls=%async_computation.2 | async-start | bytes 1048576 | tf_op jit(solution)/shard_map/while/body/all_to_all | solution.py:28
  150.5 9.8 %collective-permute-start.2 = (bf16[64,512]{1,0:T(8,128)(2,1)S(1)}, bf16[64,512]{1,0:T(8,128)(2,1)S(1)}, u32[]{:S(2)}, u32[]{:S(2)}) collective-permute-start(bf16[64,512]{1,0:T(8,128)(2,1)S(1)} %get-tuple-element.172), channel_id=1, source_target_pairs={{0,4},{1,36},{2,68},{3,100},{4,132},{5,164},{6,196},{7,228},{32,5}... | collective-permute-start | bytes 196616 | tf_op jit(solution)/shard_map/while/body/ppermute | solution.py:37
  152.9 10.5 %collective-permute-start.3 = (bf16[64,512]{1,0:T(8,128)(2,1)S(1)}, bf16[64,512]{1,0:T(8,128)(2,1)S(1)}, u32[]{:S(2)}, u32[]{:S(2)}) collective-permute-start(bf16[64,512]{1,0:T(8,128)(2,1)S(1)} %get-tuple-element.173), channel_id=1, source_target_pairs={{0,0},{1,32},{2,64},{3,96},{4,128},{5,160},{6,192},{7,224},{32,1},... | collective-permute-start | bytes 196616 | tf_op jit(solution)/shard_map/while/body/ppermute | solution.py:37
  164.1 19.6 %all-to-all-start.3 = ((bf16[4,64,128]{2,1,0:T(8,128)(2,1)}), bf16[4,64,128]{2,1,0:T(8,128)(2,1)S(1)}, u32[]{:S(2)}, u32[]{:S(2)}) async-start(bf16[4,64,128]{2,1,0:T(8,128)(2,1)} %copy.58), calls=%async_computation.3 | async-start | bytes 131072 | tf_op jit(solution)/shard_map/while/body/all_to_all | solution.py:28
  183.7 0.6 copy-start.3
Sparse Core Ops, SparseCore 0:
  10.7 88.7 all-gather.2
  134.2 91.7 reduce-scatter.1

commit v9 on v4

--- a/solution.py
+++ b/solution.py
@@ -56,7 +56,7 @@
         lambda state: state[0] < turns,
         lambda state: (state[0] + 1, state[1], step(state[1] + state[0].astype(jnp.bfloat16))),
         start,
-    )[2]
+    )[::2]
 
 
 def token_chain(both):
@@ -76,17 +76,17 @@
 def shards(tokens, out_grad, route_probs, expert_ids, gate_weight, up_weight, down_weight):
     hid, feat = down_weight.shape
     own = jnp.concatenate([gate_weight.T, up_weight.T, down_weight], axis=0)
-    weights = lax.all_gather(own, ("zh", "c")).reshape(4, 2, 3 * hid, feat)
+    weights = lax.all_gather(own, ("c", "zh")).reshape(2, 4, 3 * hid, feat)
 
     picker, row_weight = select(route_probs, expert_ids)
     picked = jnp.dot(picker, tokens, preferred_element_type=jnp.float32).astype(jnp.bfloat16)
     cot_rows = jnp.dot(picker, out_grad, preferred_element_type=jnp.float32)
     carried = (row_weight[:, None] * cot_rows).astype(jnp.bfloat16)
     both = jnp.concatenate([picked, carried], axis=1).reshape(WINDOW, CAP, 2 * feat)
-    both = once(token_chain, both, (8 * CAP, 8 * feat))
+    turns, both = once(token_chain, both, (8 * CAP, 8 * feat))
     rows, carried = both[:, : 4 * feat], both[:, 4 * feat :]
-    weights = lax.dynamic_index_in_dim(weights, lax.axis_index("c"), 1, False)
-    weights = jnp.concatenate(list(weights), axis=1) + both[:1, :1] * 0
+    weights = lax.dynamic_index_in_dim(weights, lax.axis_index("c") + turns - 1, 0, False)
+    weights = jnp.concatenate(list(weights), axis=1)
     gate_up, down = weights[: 2 * hid], weights[2 * hid :]
 
     parts = jnp.concatenate(
@@ -116,10 +116,11 @@
     ).astype(jnp.bfloat16)
     summed = lax.psum_scatter(terms.reshape(3 * hid, 4, feat).transpose(1, 0, 2), "zh")
     row_grad = contract(row_grads, gate_up, 1, 0).astype(jnp.bfloat16).reshape(8, CAP, 4 * feat)
-    row_grad = once(grad_chain, row_grad, (WINDOW, CAP, feat))
-    summed = summed + row_grad[0, :1, :1] * 0
-    gate_grad, up_grad = summed[:hid].T, summed[hid : 2 * hid].T
-    down_grad = summed[2 * hid :]
+    turns, row_grad = once(grad_chain, row_grad, (WINDOW, CAP, feat))
+    gate_grad, up_grad, down_grad = (
+        jnp.where(turns > 0, summed[i * hid : (i + 1) * hid], 0) for i in range(3)
+    )
+    gate_grad, up_grad = gate_grad.T, up_grad.T
 
     x_grad = contract(picker, row_grad.reshape(WINDOW * CAP, feat), 0, 0).astype(jnp.bfloat16)
     return (x_grad, gate_grad, up_grad, down_grad)

time: 230 us -> 229 us (level)
  the two profiles are of different devices: /device:TPU:119 before, /device:TPU:107 now
where the time goes in v9:
time: 229 us; the launch traced here: 228 us
  waiting for transfers between devices  122 us (53%)
  blocking collectives  45.7 us (20%)
  starting transfers between devices  27.2 us (12%)
  between operations  14.2 us (6%)
  local copies, waits for them, and re-layouts  8.32 us (4%)
  other arithmetic  6.14 us (3%)
  matrix products  4.95 us (2%)
    all_to_all x2, waiting for transfers between devices, gather(): return lax.all_to_all(copies, axis, 0, 0)  54.9 us
    all_to_all x3, blocking collectives, exchange(): return lax.all_to_all(blocks, axis, 0, 0)  45.7 us
    reduce_scatter x1, waiting for transfers between devices, shards(): lax.psum_scatter(terms.reshape(3 * hid, 4, feat).transpose(1, 0, 2), 'zh')  39.7 us
    all_to_all x2, starting transfers between devices, gather(): return lax.all_to_all(copies, axis, 0, 0)  13 us
    ppermute x2, waiting for transfers between devices, swap(): return lax.ppermute(block, PIECE + GROUP, pairs)  12.4 us
    all_to_all x1, waiting for transfers between devices, exchange(): return lax.all_to_all(blocks, axis, 0, 0)  11.2 us
    all_to_all x1, starting transfers between devices, exchange(): return lax.all_to_all(blocks, axis, 0, 0)  7.27 us
    ppermute x2, starting transfers between devices, swap(): return lax.ppermute(block, PIECE + GROUP, pairs)  6.94 us
  transfers between devices with their start and end apart: 7, of which 7 were waited for; matrix products, arithmetic and copies ran while one was open for 4% of the time, Pallas kernels for 0%

profile of v9, /device:TPU:107, one launch (start us, length us, event | category | flops | bytes accessed | tf_op | source)
XLA Modules:
  0.0 228.5 jit_solution(13764065241379879148)
XLA Ops:
  7.2 1.5 pad_maximum_fusion.2
  12.1 1.1 broadcast_in_dim.58
  13.3 82.7 %while.22 = (s32[]{:T(128)}, bf16[512,1024]{1,0:T(8,128)(2,1)}, s32[]{:T(128)}, bf16[4,64,256]{2,1,0:T(8,128)(2,1)S(1)}, s32[]{:T(128)}) while((s32[]{:T(128)}, bf16[512,1024]{1,0:T(8,128)(2,1)}, s32[]{:T(128)}, bf16[4,64,256]{2,1,0:T(8,128)(2,1)S(1)}, s32[]{:T(128)}) %tuple.62), condition=%wide.region_4.5_spmd, body=%wide.region_3.4_spmd.sunk | while | flops 65539 | bytes 10354857 | solution.py:55
  13.3 17.5 %all_to_all.41 = bf16[4,64,256]{2,1,0:T(8,128)(2,1)S(1)} all-to-all(bf16[4,64,256]{2,1,0:T(8,128)(2,1)S(1)} %broadcast_add_fusion.4), channel_id=1, replica_groups=mesh['zp'=4,'l'=2,'x'=4,'zh'=4,'y'=4,'c'=2] {'zp'}, dimensions={0} | all-to-all | bytes 262144 | tf_op jit(solution)/shard_map/while/body/all_to_all | solution.py:28
  31.1 4.3 %collective-permute-start = (bf16[64,1024]{1,0:T(8,128)(2,1)S(1)}, bf16[64,1024]{1,0:T(8,128)(2,1)S(1)}, u32[]{:S(2)}, u32[]{:S(2)}) collective-permute-start(bf16[64,1024]{1,0:T(8,128)(2,1)S(1)} %reshape.93), channel_id=1, source_target_pairs={{0,0},{1,32},{2,64},{3,96},{4,128},{5,160},{6,192},{7,224},{32,1},... | collective-permute-start | bytes 393224 | tf_op jit(solution)/shard_map/while/body/ppermute | solution.py:33
  35.4 5.9 %collective-permute-done = bf16[64,1024]{1,0:T(8,128)(2,1)S(1)} collective-permute-done((bf16[64,1024]{1,0:T(8,128)(2,1)S(1)}, bf16[64,1024]{1,0:T(8,128)(2,1)S(1)}, u32[]{:S(2)}, u32[]{:S(2)}) %collective-permute-start) | collective-permute-done | bytes 131104 | tf_op jit(solution)/shard_map/while/body/ppermute | solution.py:33
  41.3 1.1 broadcast_in_dim.73
  42.4 7.6 %all-to-all-start.1 = ((bf16[8,64,1024]{2,1,0:T(8,128)(2,1)}), bf16[8,64,1024]{2,1,0:T(8,128)(2,1)S(1)}, u32[]{:S(2)}, u32[]{:S(2)}) async-start(bf16[8,64,1024]{2,1,0:T(8,128)(2,1)} %broadcast_in_dim.73), calls=%async_computation.1 | async-start | bytes 2097152 | tf_op jit(solution)/shard_map/while/body/all_to_all | solution.py:24
  50.0 45.0 %all-to-all-done.1 = bf16[8,64,1024]{2,1,0:T(8,128)(2,1)S(1)} async-done(((bf16[8,64,1024]{2,1,0:T(8,128)(2,1)}), bf16[8,64,1024]{2,1,0:T(8,128)(2,1)S(1)}, u32[]{:S(2)}, u32[]{:S(2)}) %all-to-all-start.1) | async-done | bytes 1048608 | tf_op jit(solution)/shard_map/while/body/all_to_all | solution.py:24
  95.0 1.0 copy-done.1
  96.0 3.7 %all-gather.3.cloned.1.call-done = bf16[4608,128]{1,0:T(8,128)(2,1)} async-done(((bf16[576,128]{1,0:T(8,128)(2,1)}), bf16[4608,128]{1,0:T(8,128)(2,1)}) %all-gather.3.cloned.1.call-update) | async-done | bytes 1179664 | tf_op jit(solution)/shard_map/all_gather | solution.py:79
  99.7 1.3 dynamic-slice_bitcast_fusion.3
  102.2 12.9 %all_to_all.40 = bf16[8,64,576]{2,1,0:T(8,128)(2,1)S(1)} all-to-all(bf16[8,64,576]{2,1,0:T(8,128)(2,1)S(1)} %pad_maximum_fusion), channel_id=1, replica_groups=mesh['zp'=4,'l'=2,'x'=4,'zh'=4,'y'=4,'c'=2] {'y','c'}, dimensions={0} | all-to-all | bytes 1179648 | tf_op jit(solution)/shard_map/all_to_all | solution.py:28
  116.2 5.4 %all-to-all-start.5 = ((bf16[8,64,576]{2,1,0:T(8,128)(2,1)}), bf16[8,64,576]{2,1,0:T(8,128)(2,1)S(1)}, u32[]{:S(2)}, u32[]{:S(2)}) async-start(bf16[8,64,576]{2,1,0:T(8,128)(2,1)} %broadcast_in_dim.63), calls=%async_computation.5 | async-start | bytes 1310720 | tf_op jit(solution)/shard_map/all_to_all | solution.py:24
  121.7 9.8 %all-to-all-done.5 = bf16[8,64,576]{2,1,0:T(8,128)(2,1)S(1)} async-done(((bf16[8,64,576]{2,1,0:T(8,128)(2,1)}), bf16[8,64,576]{2,1,0:T(8,128)(2,1)S(1)}, u32[]{:S(2)}, u32[]{:S(2)}) %all-to-all-start.5) | async-done | bytes 589856 | tf_op jit(solution)/shard_map/all_to_all | solution.py:24
  134.3 44.5 %while.23 = (s32[]{:T(128)}, bf16[4,64,128]{2,1,0:T(8,128)(2,1)}, s32[]{:T(128)}, bf16[8,64,512]{2,1,0:T(8,128)(2,1)S(1)}, s32[]{:T(128)}, /*index=5*/bf16[]{:T(256)}) while((s32[]{:T(128)}, bf16[4,64,128]{2,1,0:T(8,128)(2,1)}, s32[]{:T(128)}, bf16[8,64,512]{2,1,0:T(8,128)(2,1)S(1)}, s32[]{:T(128)}, /*index=5*/bf16[]{:T(256)}) %tuple.61), condition=%wide.region_8.9_spmd, body=%wide.region_6.8_spmd.sunk | while | flops 491523 | bytes 3670195 | solution.py:55
  134.3 15.4 %all_to_all.42 = bf16[8,64,512]{2,1,0:T(8,128)(2,1)S(1)} all-to-all(bf16[8,64,512]{2,1,0:T(8,128)(2,1)S(1)} %broadcast_add_fusion.5), channel_id=1, replica_groups=mesh['zp'=4,'l'=2,'x'=4,'zh'=4,'y'=4,'c'=2] {'l','x'}, dimensions={0} | all-to-all | bytes 1048576 | tf_op jit(solution)/shard_map/while/body/all_to_all | solution.py:28
  149.8 2.6 %collective-permute-start.1 = (bf16[64,512]{1,0:T(8,128)(2,1)S(1)}, bf16[64,512]{1,0:T(8,128)(2,1)S(1)}, u32[]{:S(2)}, u32[]{:S(2)}) collective-permute-start(bf16[64,512]{1,0:T(8,128)(2,1)S(1)} %reduce_sum.46), channel_id=1, source_target_pairs={{0,0},{1,32},{2,64},{3,96},{4,128},{5,160},{6,192},{7,224},{32,1},... | collective-permute-start | bytes 196616 | tf_op jit(solution)/shard_map/while/body/ppermute | solution.py:33
  152.4 6.5 %collective-permute-done.1 = bf16[64,512]{1,0:T(8,128)(2,1)S(1)} collective-permute-done((bf16[64,512]{1,0:T(8,128)(2,1)S(1)}, bf16[64,512]{1,0:T(8,128)(2,1)S(1)}, u32[]{:S(2)}, u32[]{:S(2)}) %collective-permute-start.1) | collective-permute-done | bytes 65568 | tf_op jit(solution)/shard_map/while/body/ppermute | solution.py:33
  159.6 7.3 %all-to-all-start.3 = ((bf16[4,64,128]{2,1,0:T(8,128)(2,1)}), bf16[4,64,128]{2,1,0:T(8,128)(2,1)S(1)}, u32[]{:S(2)}, u32[]{:S(2)}) async-start(bf16[4,64,128]{2,1,0:T(8,128)(2,1)} %copy.58), calls=%async_computation.3 | async-start | bytes 131072 | tf_op jit(solution)/shard_map/while/body/all_to_all | solution.py:28
  166.9 11.2 %all-to-all-done.3 = bf16[4,64,128]{2,1,0:T(8,128)(2,1)S(1)} async-done(((bf16[4,64,128]{2,1,0:T(8,128)(2,1)}), bf16[4,64,128]{2,1,0:T(8,128)(2,1)S(1)}, u32[]{:S(2)}, u32[]{:S(2)}) %all-to-all-start.3) | async-done | bytes 65568 | tf_op jit(solution)/shard_map/while/body/all_to_all | solution.py:28
  178.7 1.7 fusion.3
  180.5 39.7 %reduce-scatter.2.cloned.1.call-done = bf16[1,576,128]{2,1,0:T(8,128)(2,1)} async-done(((bf16[4,576,128]{2,1,0:T(8,128)(2,1)}), bf16[1,576,128]{2,1,0:T(8,128)(2,1)}) %reduce-scatter.2.cloned.1.call-update) | async-done | bytes 147472 | tf_op jit(solution)/shard_map/reduce_scatter | solution.py:117
  220.2 1.5 fusion.25
  (48 shorter events, 10.2 us)
Async XLA Ops:
  7.2 3.7 %copy-start = (bf16[128,128]{1,0:T(8,128)(2,1)S(1)}, bf16[128,128]{1,0:T(8,128)(2,1)}, u32[]{:S(2)}) copy-start(bf16[128,128]{1,0:T(8,128)(2,1)} %param.11) | copy-start | bytes 98308
  7.2 92.5 %all-gather.3.cloned.1.call-start = ((), (), s32[]{:S(2)}) async-start(), calls=%async_computation.8 | async-start | bytes 1327104 | tf_op jit(solution)/shard_map/all_gather | solution.py:79
  31.1 10.2 %collective-permute-start = (bf16[64,1024]{1,0:T(8,128)(2,1)S(1)}, bf16[64,1024]{1,0:T(8,128)(2,1)S(1)}, u32[]{:S(2)}, u32[]{:S(2)}) collective-permute-start(bf16[64,1024]{1,0:T(8,128)(2,1)S(1)} %reshape.93), channel_id=1, source_target_pairs={{0,0},{1,32},{2,64},{3,96},{4,128},{5,160},{6,192},{7,224},{32,1},... | collective-permute-start | bytes 393224 | tf_op jit(solution)/shard_map/while/body/ppermute | solution.py:33
  42.4 52.6 %all-to-all-start.1 = ((bf16[8,64,1024]{2,1,0:T(8,128)(2,1)}), bf16[8,64,1024]{2,1,0:T(8,128)(2,1)S(1)}, u32[]{:S(2)}, u32[]{:S(2)}) async-start(bf16[8,64,1024]{2,1,0:T(8,128)(2,1)} %broadcast_in_dim.73), calls=%async_computation.1 | async-start | bytes 2097152 | tf_op jit(solution)/shard_map/while/body/all_to_all | solution.py:24
  95.0 1.0 copy-start.1
  99.7 1.5 copy-start.2
  116.2 15.2 %all-to-all-start.5 = ((bf16[8,64,576]{2,1,0:T(8,128)(2,1)}), bf16[8,64,576]{2,1,0:T(8,128)(2,1)S(1)}, u32[]{:S(2)}, u32[]{:S(2)}) async-start(bf16[8,64,576]{2,1,0:T(8,128)(2,1)} %broadcast_in_dim.63), calls=%async_computation.5 | async-start | bytes 1310720 | tf_op jit(solution)/shard_map/all_to_all | solution.py:24
  121.7 98.5 %reduce-scatter.2.cloned.1.call-start = ((), (), s32[]{:S(2)}) async-start(), calls=%async_computation.7 | async-start | bytes 737280 | tf_op jit(solution)/shard_map/reduce_scatter | solution.py:117
  149.8 9.1 %collective-permute-start.1 = (bf16[64,512]{1,0:T(8,128)(2,1)S(1)}, bf16[64,512]{1,0:T(8,128)(2,1)S(1)}, u32[]{:S(2)}, u32[]{:S(2)}) collective-permute-start(bf16[64,512]{1,0:T(8,128)(2,1)S(1)} %reduce_sum.46), channel_id=1, source_target_pairs={{0,0},{1,32},{2,64},{3,96},{4,128},{5,160},{6,192},{7,224},{32,1},... | collective-permute-start | bytes 196616 | tf_op jit(solution)/shard_map/while/body/ppermute | solution.py:33
  159.6 18.5 %all-to-all-start.3 = ((bf16[4,64,128]{2,1,0:T(8,128)(2,1)}), bf16[4,64,128]{2,1,0:T(8,128)(2,1)S(1)}, u32[]{:S(2)}, u32[]{:S(2)}) async-start(bf16[4,64,128]{2,1,0:T(8,128)(2,1)} %copy.58), calls=%async_computation.3 | async-start | bytes 131072 | tf_op jit(solution)/shard_map/while/body/all_to_all | solution.py:28
  178.1 0.6 copy-start.3
Sparse Core Ops, SparseCore 0:
  10.7 88.9 all-gather.2
  133.7 86.3 reduce-scatter.1

commit v10 on v9

--- a/solution.py
+++ b/solution.py
@@ -10,7 +10,7 @@
 EXPERT = ("zp", "l", "x")
 FSDP = ("zh", "y", "c")
 PIECE = ("l", "x")
-GROUP = ("y", "c")
+GROUP = "y"
 
 
 def contract(left, right, left_dim, right_dim):
@@ -29,8 +29,13 @@
 
 
 def swap(block):
-    pairs = [(piece * 8 + group, group * 8 + piece) for piece in range(8) for group in range(8)]
-    return lax.ppermute(block, PIECE + GROUP, pairs)
+    pairs = [
+        ((high * 2 + low) * 4 + group, (group * 2 + low) * 4 + high)
+        for high in range(4)
+        for low in range(2)
+        for group in range(4)
+    ]
+    return lax.ppermute(block, PIECE + (GROUP,), pairs)
 
 
 def select(probs, ids):
@@ -63,7 +68,7 @@
     both = exchange(both, "zp")
     feat = both.shape[2] // 2
     both = both.reshape(4, CAP, 2, feat).transpose(1, 2, 0, 3).reshape(CAP, 8 * feat)
-    return gather(swap(both), PIECE, 8).reshape(8 * CAP, 8 * feat)
+    return gather(swap(both), PIECE, 8)
 
 
 def grad_chain(row_grad):
@@ -76,24 +81,24 @@
 def shards(tokens, out_grad, route_probs, expert_ids, gate_weight, up_weight, down_weight):
     hid, feat = down_weight.shape
     own = jnp.concatenate([gate_weight.T, up_weight.T, down_weight], axis=0)
-    weights = lax.all_gather(own, ("c", "zh")).reshape(2, 4, 3 * hid, feat)
+    weights = lax.all_gather(own, ("c", "zh"))
 
     picker, row_weight = select(route_probs, expert_ids)
     picked = jnp.dot(picker, tokens, preferred_element_type=jnp.float32).astype(jnp.bfloat16)
     cot_rows = jnp.dot(picker, out_grad, preferred_element_type=jnp.float32)
     carried = (row_weight[:, None] * cot_rows).astype(jnp.bfloat16)
     both = jnp.concatenate([picked, carried], axis=1).reshape(WINDOW, CAP, 2 * feat)
-    turns, both = once(token_chain, both, (8 * CAP, 8 * feat))
-    rows, carried = both[:, : 4 * feat], both[:, 4 * feat :]
-    weights = lax.dynamic_index_in_dim(weights, lax.axis_index("c") + turns - 1, 0, False)
-    weights = jnp.concatenate(list(weights), axis=1)
+    turns, both = once(token_chain, both, (8, CAP, 8 * feat))
+    both = both.reshape(4, 2, CAP, 2, 4 * feat).transpose(3, 0, 2, 1, 4)
+    rows, carried = both.reshape(2, 4 * CAP, 8 * feat)
+    weights = jnp.where(turns > 0, weights, 0).transpose(1, 0, 2).reshape(3 * hid, 8 * feat)
     gate_up, down = weights[: 2 * hid], weights[2 * hid :]
 
     parts = jnp.concatenate(
         [contract(rows, gate_up, 1, 1), contract(carried, down, 1, 1)], axis=1
     ).astype(jnp.bfloat16)
     values = jnp.sum(
-        exchange(parts.reshape(8, CAP, 3 * hid), GROUP).astype(jnp.float32), axis=0
+        exchange(parts.reshape(4, CAP, 3 * hid), GROUP).astype(jnp.float32), axis=0
     )
     gate_value, up_value, hidden_grad = (
         values[:, :hid],
@@ -108,14 +113,18 @@
         jnp.bfloat16
     )
     acts = jnp.concatenate([gate_rows_grad, up_rows_grad, hidden], axis=1)
-    acts = gather(acts, GROUP, 8).reshape(8 * CAP, 3 * hid)
+    acts = gather(acts, GROUP, 4).reshape(4 * CAP, 3 * hid)
     row_grads, hidden = acts[:, : 2 * hid], acts[:, 2 * hid :]
 
     terms = jnp.concatenate(
         [contract(row_grads, rows, 0, 0), contract(hidden, carried, 0, 0)], axis=0
     ).astype(jnp.bfloat16)
-    summed = lax.psum_scatter(terms.reshape(3 * hid, 4, feat).transpose(1, 0, 2), "zh")
-    row_grad = contract(row_grads, gate_up, 1, 0).astype(jnp.bfloat16).reshape(8, CAP, 4 * feat)
+    terms = exchange(terms.reshape(3 * hid, 2, 4, feat).transpose(1, 2, 0, 3), "c")
+    terms = jnp.sum(terms.astype(jnp.float32), axis=0).astype(jnp.bfloat16)
+    summed = lax.psum_scatter(terms, "zh")
+    row_grad = contract(row_grads, gate_up, 1, 0).astype(jnp.bfloat16)
+    row_grad = row_grad.reshape(4, CAP, 2, 4 * feat).transpose(0, 2, 1, 3)
+    row_grad = row_grad.reshape(8, CAP, 4 * feat)
     turns, row_grad = once(grad_chain, row_grad, (WINDOW, CAP, feat))
     gate_grad, up_grad, down_grad = (
         jnp.where(turns > 0, summed[i * hid : (i + 1) * hid], 0) for i in range(3)

time: 229 us -> 233 us (1.017)
  waiting for transfers between devices: 122 us -> 115 us
  local copies, waits for them, and re-layouts: 8.32 us -> 14.8 us
  blocking collectives: 45.7 us -> 49.4 us
  starting transfers between devices: 27.2 us -> 24.7 us
    all_to_all x2, starting transfers between devices: 13 us -> 9.14 us  [gather(): return lax.all_to_all(copies, axis, 0, 0)]
    all_gather x1, waiting for transfers between devices: 3.69 us -> 0.01 us  [shards(): weights = lax.all_gather(own, ('c', 'zh'))]
    all_to_all x3 -> x4, blocking collectives: 45.7 us -> 49.4 us  [exchange(): return lax.all_to_all(blocks, axis, 0, 0)]
    reshape x0 -> x3, local copies, waits for them, and re-layouts: none -> 3.29 us  [the longest x2 2.92 us: shards(): both = both.reshape(4, 2, CAP, 2, 4 * feat).transpose(3, 0, 2, 1, 4)]
    all_to_all x2, waiting for transfers between devices: 54.9 us -> 51.9 us  [gather(): return lax.all_to_all(copies, axis, 0, 0)]
  transfers between devices with their start and end apart: 7 -> 7, of which waited for: 7 -> 6; matrix products, arithmetic and copies ran while one was open for 4% -> 6% of each run, Pallas kernels for 0% -> 0%
where the time goes in v10:
time: 233 us; the launch traced here: 232 us
  waiting for transfers between devices  115 us (49%)
  blocking collectives  49.4 us (21%)
  starting transfers between devices  24.7 us (11%)
  local copies, waits for them, and re-layouts  14.8 us (6%)
  between operations  14.3 us (6%)
  other arithmetic  7.74 us (3%)
  matrix products  6.17 us (3%)
    all_to_all x2, waiting for transfers between devices, gather(): return lax.all_to_all(copies, axis, 0, 0)  51.9 us
    all_to_all x4, blocking collectives, exchange(): return lax.all_to_all(blocks, axis, 0, 0)  49.4 us
    reduce_scatter x1, waiting for transfers between devices, shards(): summed = lax.psum_scatter(terms, 'zh')  39.2 us
    all_to_all x1, waiting for transfers between devices, exchange(): return lax.all_to_all(blocks, axis, 0, 0)  13.2 us
    ppermute x2, waiting for transfers between devices, swap(): return lax.ppermute(block, PIECE + (GROUP,), pairs)  11.1 us
    all_to_all x1, starting transfers between devices, exchange(): return lax.all_to_all(blocks, axis, 0, 0)  9.19 us
    all_to_all x2, starting transfers between devices, gather(): return lax.all_to_all(copies, axis, 0, 0)  9.14 us
    ppermute x2, starting transfers between devices, swap(): return lax.ppermute(block, PIECE + (GROUP,), pairs)  6.36 us
  transfers between devices with their start and end apart: 7, of which 6 were waited for; matrix products, arithmetic and copies ran while one was open for 6% of the time, Pallas kernels for 0%

profile of v10, /device:TPU:107, one launch (start us, length us, event | category | flops | bytes accessed | tf_op | source)
XLA Modules:
  0.0 232.4 jit_solution(8338555864155335376)
XLA Ops:
  7.2 1.5 pad_maximum_fusion.1
  13.3 81.3 %while.22 = (s32[]{:T(128)}, bf16[8,64,1024]{2,1,0:T(8,128)(2,1)}, s32[]{:T(128)}, bf16[4,64,256]{2,1,0:T(8,128)(2,1)S(1)}, s32[]{:T(128)}) while((s32[]{:T(128)}, bf16[8,64,1024]{2,1,0:T(8,128)(2,1)}, s32[]{:T(128)}, bf16[4,64,256]{2,1,0:T(8,128)(2,1)S(1)}, s32[]{:T(128)}) %tuple.60), condition=%wide.region_4.5_spmd, body=%wide.region_3.4_spmd.sunk | while | flops 65539 | bytes 10354857 | solution.py:60
  13.3 17.5 %all_to_all.47 = bf16[4,64,256]{2,1,0:T(8,128)(2,1)S(1)} all-to-all(bf16[4,64,256]{2,1,0:T(8,128)(2,1)S(1)} %broadcast_add_fusion.4), channel_id=1, replica_groups=mesh['zp'=4,'l'=2,'x'=4,'zh'=4,'y'=4,'c'=2] {'zp'}, dimensions={0} | all-to-all | bytes 262144 | tf_op jit(solution)/shard_map/while/body/all_to_all | solution.py:28
  31.1 4.3 %collective-permute-start = (bf16[64,1024]{1,0:T(8,128)(2,1)S(1)}, bf16[64,1024]{1,0:T(8,128)(2,1)S(1)}, u32[]{:S(2)}, u32[]{:S(2)}) collective-permute-start(bf16[64,1024]{1,0:T(8,128)(2,1)S(1)} %reshape.104), channel_id=1, source_target_pairs={{0,0},{2,64},{4,128},{6,192},{32,32},{34,96},{36,160},{38,224},{64... | collective-permute-start | bytes 393224 | tf_op jit(solution)/shard_map/while/body/ppermute | solution.py:38
  35.4 4.8 %collective-permute-done = bf16[64,1024]{1,0:T(8,128)(2,1)S(1)} collective-permute-done((bf16[64,1024]{1,0:T(8,128)(2,1)S(1)}, bf16[64,1024]{1,0:T(8,128)(2,1)S(1)}, u32[]{:S(2)}, u32[]{:S(2)}) %collective-permute-start) | collective-permute-done | bytes 131104 | tf_op jit(solution)/shard_map/while/body/ppermute | solution.py:38
  41.4 4.5 %all-to-all-start.1 = ((bf16[8,64,1024]{2,1,0:T(8,128)(2,1)}), bf16[8,64,1024]{2,1,0:T(8,128)(2,1)S(1)}, u32[]{:S(2)}, u32[]{:S(2)}) async-start(bf16[8,64,1024]{2,1,0:T(8,128)(2,1)} %broadcast_in_dim.78), calls=%async_computation.1 | async-start | bytes 2097152 | tf_op jit(solution)/shard_map/while/body/all_to_all | solution.py:24
  45.9 47.7 %all-to-all-done.1 = bf16[8,64,1024]{2,1,0:T(8,128)(2,1)S(1)} async-done(((bf16[8,64,1024]{2,1,0:T(8,128)(2,1)}), bf16[8,64,1024]{2,1,0:T(8,128)(2,1)S(1)}, u32[]{:S(2)}, u32[]{:S(2)}) %all-to-all-start.1) | async-done | bytes 1048608 | tf_op jit(solution)/shard_map/while/body/all_to_all | solution.py:24
  94.6 1.8 reshape.85
  98.7 1.2 dot_general.44
  99.9 1.4 broadcast_select_fusion
  103.3 1.5 convolution_convert_fusion.4
  105.3 9.6 %all_to_all.45 = bf16[4,64,576]{2,1,0:T(8,128)(2,1)S(1)} all-to-all(bf16[4,64,576]{2,1,0:T(8,128)(2,1)S(1)} %pad_maximum_fusion), channel_id=1, replica_groups=mesh['zp'=4,'l'=2,'x'=4,'zh'=4,'y'=4,'c'=2] {'y'}, dimensions={0} | all-to-all | bytes 589824 | tf_op jit(solution)/shard_map/all_to_all | solution.py:28
  115.9 4.6 %all-to-all-start.5 = ((bf16[4,64,576]{2,1,0:T(8,128)(2,1)}), bf16[4,64,576]{2,1,0:T(8,128)(2,1)S(1)}, u32[]{:S(2)}, u32[]{:S(2)}) async-start(bf16[4,64,576]{2,1,0:T(8,128)(2,1)} %broadcast_in_dim.68), calls=%async_computation.5 | async-start | bytes 655360 | tf_op jit(solution)/shard_map/all_to_all | solution.py:24
  121.1 4.1 %all-to-all-done.5 = bf16[4,64,576]{2,1,0:T(8,128)(2,1)S(1)} async-done(((bf16[4,64,576]{2,1,0:T(8,128)(2,1)}), bf16[4,64,576]{2,1,0:T(8,128)(2,1)S(1)}, u32[]{:S(2)}, u32[]{:S(2)}) %all-to-all-start.5) | async-done | bytes 294944 | tf_op jit(solution)/shard_map/all_to_all | solution.py:24
  127.0 7.8 %all_to_all.46 = bf16[2,4,576,128]{3,2,1,0:T(8,128)(2,1)S(1)} all-to-all(bf16[2,4,576,128]{3,2,1,0:T(8,128)(2,1)S(1)} %maximum_bitcast_fusion), channel_id=1, replica_groups=mesh['zp'=4,'l'=2,'x'=4,'zh'=4,'y'=4,'c'=2] {'c'}, dimensions={0} | all-to-all | bytes 2359296 | tf_op jit(solution)/shard_map/all_to_all | solution.py:28
  136.6 46.6 %while.23 = (s32[]{:T(128)}, bf16[4,64,128]{2,1,0:T(8,128)(2,1)}, s32[]{:T(128)}, bf16[8,64,512]{2,1,0:T(8,128)(2,1)S(1)}, s32[]{:T(128)}, /*index=5*/bf16[]{:T(256)}) while((s32[]{:T(128)}, bf16[4,64,128]{2,1,0:T(8,128)(2,1)}, s32[]{:T(128)}, bf16[8,64,512]{2,1,0:T(8,128)(2,1)S(1)}, s32[]{:T(128)}, /*index=5*/bf16[]{:T(256)}) %tuple.59), condition=%wide.region_8.9_spmd, body=%wide.region_6.8_spmd.sunk | while | flops 491523 | bytes 3670195 | solution.py:60
  136.7 14.5 %all_to_all.48 = bf16[8,64,512]{2,1,0:T(8,128)(2,1)S(1)} all-to-all(bf16[8,64,512]{2,1,0:T(8,128)(2,1)S(1)} %broadcast_add_fusion.5), channel_id=1, replica_groups=mesh['zp'=4,'l'=2,'x'=4,'zh'=4,'y'=4,'c'=2] {'l','x'}, dimensions={0} | all-to-all | bytes 1048576 | tf_op jit(solution)/shard_map/while/body/all_to_all | solution.py:28
  151.2 2.1 collective-permute-start.1
  153.3 6.3 %collective-permute-done.1 = bf16[64,512]{1,0:T(8,128)(2,1)S(1)} collective-permute-done((bf16[64,512]{1,0:T(8,128)(2,1)S(1)}, bf16[64,512]{1,0:T(8,128)(2,1)S(1)}, u32[]{:S(2)}, u32[]{:S(2)}) %collective-permute-start.1) | collective-permute-done | bytes 65568 | tf_op jit(solution)/shard_map/while/body/ppermute | solution.py:38
  160.2 9.2 %all-to-all-start.3 = ((bf16[4,64,128]{2,1,0:T(8,128)(2,1)}), bf16[4,64,128]{2,1,0:T(8,128)(2,1)S(1)}, u32[]{:S(2)}, u32[]{:S(2)}) async-start(bf16[4,64,128]{2,1,0:T(8,128)(2,1)} %copy.84), calls=%async_computation.3 | async-start | bytes 131072 | tf_op jit(solution)/shard_map/while/body/all_to_all | solution.py:28
  169.4 13.2 %all-to-all-done.3 = bf16[4,64,128]{2,1,0:T(8,128)(2,1)S(1)} async-done(((bf16[4,64,128]{2,1,0:T(8,128)(2,1)}), bf16[4,64,128]{2,1,0:T(8,128)(2,1)S(1)}, u32[]{:S(2)}, u32[]{:S(2)}) %all-to-all-start.3) | async-done | bytes 65568 | tf_op jit(solution)/shard_map/while/body/all_to_all | solution.py:28
  183.2 1.7 fusion.1
  184.9 39.2 %reduce-scatter.2.cloned.1.call-done = bf16[1,576,128]{2,1,0:T(8,128)(2,1)} async-done(((bf16[4,576,128]{2,1,0:T(8,128)(2,1)}), bf16[1,576,128]{2,1,0:T(8,128)(2,1)}) %reduce-scatter.2.cloned.1.call-update) | async-done | bytes 147472 | tf_op jit(solution)/shard_map/reduce_scatter | solution.py:124
  224.1 1.5 fusion.12
  (60 shorter events, 18.2 us)
Async XLA Ops:
  7.2 3.7 %copy-start = (bf16[128,128]{1,0:T(8,128)(2,1)S(1)}, bf16[128,128]{1,0:T(8,128)(2,1)}, u32[]{:S(2)}) copy-start(bf16[128,128]{1,0:T(8,128)(2,1)} %param.11) | copy-start | bytes 98308
  7.2 92.7 %all-gather.3.cloned.1.call-start = ((), (), s32[]{:S(2)}) async-start(), calls=%async_computation.9 | async-start | bytes 1327104 | tf_op jit(solution)/shard_map/all_gather | solution.py:84
  31.1 9.1 %collective-permute-start = (bf16[64,1024]{1,0:T(8,128)(2,1)S(1)}, bf16[64,1024]{1,0:T(8,128)(2,1)S(1)}, u32[]{:S(2)}, u32[]{:S(2)}) collective-permute-start(bf16[64,1024]{1,0:T(8,128)(2,1)S(1)} %reshape.104), channel_id=1, source_target_pairs={{0,0},{2,64},{4,128},{6,192},{32,32},{34,96},{36,160},{38,224},{64... | collective-permute-start | bytes 393224 | tf_op jit(solution)/shard_map/while/body/ppermute | solution.py:38
  41.4 52.3 %all-to-all-start.1 = ((bf16[8,64,1024]{2,1,0:T(8,128)(2,1)}), bf16[8,64,1024]{2,1,0:T(8,128)(2,1)S(1)}, u32[]{:S(2)}, u32[]{:S(2)}) async-start(bf16[8,64,1024]{2,1,0:T(8,128)(2,1)} %broadcast_in_dim.78), calls=%async_computation.1 | async-start | bytes 2097152 | tf_op jit(solution)/shard_map/while/body/all_to_all | solution.py:24
  93.6 1.0 copy-start.1
  115.9 9.3 %all-to-all-start.5 = ((bf16[4,64,576]{2,1,0:T(8,128)(2,1)}), bf16[4,64,576]{2,1,0:T(8,128)(2,1)S(1)}, u32[]{:S(2)}, u32[]{:S(2)}) async-start(bf16[4,64,576]{2,1,0:T(8,128)(2,1)} %broadcast_in_dim.68), calls=%async_computation.5 | async-start | bytes 655360 | tf_op jit(solution)/shard_map/all_to_all | solution.py:24
  120.5 103.6 %reduce-scatter.2.cloned.1.call-start = ((), (), s32[]{:S(2)}) async-start(), calls=%async_computation.8 | async-start | bytes 737280 | tf_op jit(solution)/shard_map/reduce_scatter | solution.py:124
  151.2 8.3 %collective-permute-start.1 = (bf16[64,512]{1,0:T(8,128)(2,1)S(1)}, bf16[64,512]{1,0:T(8,128)(2,1)S(1)}, u32[]{:S(2)}, u32[]{:S(2)}) collective-permute-start(bf16[64,512]{1,0:T(8,128)(2,1)S(1)} %reduce_sum.59), channel_id=1, source_target_pairs={{0,0},{2,64},{4,128},{6,192},{32,32},{34,96},{36,160},{38,224},{64... | collective-permute-start | bytes 196616 | tf_op jit(solution)/shard_map/while/body/ppermute | solution.py:38
  160.2 22.4 %all-to-all-start.3 = ((bf16[4,64,128]{2,1,0:T(8,128)(2,1)}), bf16[4,64,128]{2,1,0:T(8,128)(2,1)S(1)}, u32[]{:S(2)}, u32[]{:S(2)}) async-start(bf16[4,64,128]{2,1,0:T(8,128)(2,1)} %copy.84), calls=%async_computation.3 | async-start | bytes 131072 | tf_op jit(solution)/shard_map/while/body/all_to_all | solution.py:28
  182.6 0.6 copy-start.2
Sparse Core Ops, SparseCore 0:
  10.7 87.6 all-gather.2
  136.1 87.9 reduce-scatter.1
